TPU v7x, 32 devices: a whole 2x2x4 slice. The times are simulated.
32 devices in a mesh: items: 16 (over z, y, core), heads: 2 (over x).
Axes of the slice: x: 2, y: 2, z: 4, core: 2. Of those that a mesh axis runs over, the one named last changes fastest.
Arguments:
- hidden_in: bfloat16 [16384, 768], P('items'), may hold values from -6 to 6
- cluster_order: int32 [12, 16, 1024], P('heads', 'items'), may hold values from 0 to 1023, as said below
- qkv_weight: bfloat16 [3, 768, 768], P(None, None, 'heads'), may hold values from -0.21875 to 0.21875
- qv_bias: float32 [2, 768], P(None, 'heads'), may hold values from -3 to 3
- out_weight: bfloat16 [768, 768], P('heads'), may hold values from -0.875 to 0.875
- out_bias: float32 [768], replicated, may hold values from -2 to 2
- norm1_gain: float32 [768], replicated, may hold values from 0.5 to 1.5
- norm1_bias: float32 [768], replicated, may hold values from -2 to 2
- up_weight: bfloat16 [768, 3072], P(None, 'heads'), may hold values from -0.21875 to 0.21875
- up_bias: float32 [3072], P('heads'), may hold values from -2 to 2
- down_weight: bfloat16 [3072, 768], P('heads'), may hold values from -0.109375 to 0.109375
- down_bias: float32 [768], replicated, may hold values from -2 to 2
- norm2_gain: float32 [768], replicated, may hold values from 0.5 to 1.5
- norm2_bias: float32 [768], replicated, may hold values from -2 to 2
- cotangent: bfloat16 [16384, 768], P('items'), may hold values from -6 to 6
Outputs:
- mixed: bfloat16 [16384, 768], P('items')
- input_grad: bfloat16 [16384, 768], P('items')
- qkv_weight_grad: float32 [3, 768, 768], P(None, 'items', 'heads')
- qv_bias_grad: float32 [2, 768], P(None, 'heads')
- out_weight_grad: float32 [768, 768], P('heads', 'items')
- out_bias_grad: float32 [768], replicated
- norm1_gain_grad: float32 [768], replicated
- norm1_bias_grad: float32 [768], replicated
- up_weight_grad: float32 [768, 3072], P('items', 'heads')
- up_bias_grad: float32 [3072], P('heads')
- down_weight_grad: float32 [3072, 768], P('heads', 'items')
- down_bias_grad: float32 [768], replicated
- norm2_gain_grad: float32 [768], replicated
- norm2_bias_grad: float32 [768], replicated
Inputs may be any that keep to these rules, and one draw needn't show every extreme that they name: `cluster_order`: for each head and each device's block of 1024 tokens, an ordering of the block's positions 0 to 1023. A block holds one item of 1024 tokens or items of 512 tokens (the last one shorter where 512 does not divide 1024); an item's positions stand together in the ordering, in an order of their own for every head.
All inputs are finite; a program needn't handle non-finite values.
Results may differ from a plain program's by a relative error of at most 0.012.
Values sent between devices are 32-bit elements; how exact they have to be, the bound alone decides.
No kernel may reach another device: no remote copies, remote signals or barrier semaphores. Data moves between devices by JAX's collectives and lax.ppermute only.
A program may use at most 128 MiB of HBM per device.

v0:
```python
import functools

import jax
import jax.numpy as jnp
from jax import lax
from jax.experimental import pallas as pl
from jax.experimental.pallas import tpu as pltpu
from jax.sharding import PartitionSpec as P

HEAD_DIM = 64
CLUSTER = 128
SCALE = HEAD_DIM**-0.5
EPSILON = 1e-05
ROW_TILE = 512
LAG = 1
GRAD_TILE = 512
UNIT_TILE = 768
BF16 = jnp.bfloat16
F32 = jnp.float32


def dot(left, right):
    return jnp.dot(left, right, preferred_element_type=F32)


def dot_nt(left, right):
    return lax.dot_general(left, right, (((1,), (1,)), ((), ())), preferred_element_type=F32)


def dot_tn(left, right):
    return lax.dot_general(left, right, (((0,), (0,)), ((), ())), preferred_element_type=F32)


def dot_tt(left, right):
    return lax.dot_general(left, right, (((0,), (1,)), ((), ())), preferred_element_type=F32)


def params_of(mib):
    return pltpu.CompilerParams(vmem_limit_bytes=mib * 1024 * 1024)


def cost(flops, bytes_accessed):
    return pl.CostEstimate(flops=int(flops) // 1000, bytes_accessed=int(bytes_accessed) // 1000, transcendentals=0)


def shape(dims, dtype):
    return jax.ShapeDtypeStruct(dims, dtype)


def whole(*dims):
    return pl.BlockSpec(dims, lambda *_: (0,) * len(dims), pipeline_mode=pl.Buffered(1))


def swapped(values):
    return lax.ppermute(values, "heads", [(0, 1), (1, 0)])


def traded(values, step, n_items):
    return lax.ppermute(values, "items", [(i, i ^ step) for i in range(n_items)])


def all_sum(values, n_items):
    step = 1
    while step < n_items:
        values = values + traded(values, step, n_items)
        step *= 2
    return values


def scattered(values, n_items, axis):
    item = lax.axis_index("items")
    size = n_items
    for bit in range(n_items.bit_length() - 1):
        dims = values.shape
        size //= 2
        halves = values.reshape(dims[:axis] + (size, 2, dims[axis] // (2 * size)) + dims[axis + 1 :])
        mine = (item >> bit) & 1
        send = lax.dynamic_index_in_dim(halves, 1 - mine, axis + 1, keepdims=False)
        keep = lax.dynamic_index_in_dim(halves, mine, axis + 1, keepdims=False)
        values = keep + traded(send, 1 << bit, n_items)
        values = values.reshape(dims[:axis] + (-1,) + dims[axis + 1 :])
    return values


class Halving:
    def __init__(self, keep, send, order, n_items):
        self.terms, self.order, self.n_items = [keep], list(order), n_items
        self.send, self.extra, self.bit = send, None, 0

    def trade(self):
        self.got = traded(self.send, 1 << self.bit, self.n_items)
        if self.extra is not None:
            self.more = traded(self.extra, 1 << self.bit, self.n_items)
        return self

    def add(self):
        terms = self.terms + [self.got]
        if self.extra is not None:
            self.extra = self.extra + self.more
        if not self.order:
            return sum(term.reshape(term.shape[1:]) for term in terms)
        self.bit = self.order.pop(0)
        mine = (lax.axis_index("items") >> self.bit) & 1
        terms = [v.reshape((2, v.shape[0] // 2) + v.shape[1:]) for v in terms]
        part = lambda k: [lax.dynamic_index_in_dim(v, k, 0, keepdims=False) for v in terms]
        self.send, self.terms = sum(part(1 - mine)), part(mine)
        return self.send


def arrived(sums, *before):
    got = [one.got for one in sums] + [one.more for one in sums if one.extra is not None]
    got = list(lax.optimization_barrier(tuple(got) + before))
    for one in sums:
        one.got = got.pop(0)
    for one in sums:
        if one.extra is not None:
            one.more = got.pop(0)
    return [one.add() for one in sums]


def after(values, *others):
    return lax.optimization_barrier((values,) + others)[0]


def selector(row_ref, h, sel_ref, slot):
    rows = sel_ref.shape[1]
    step = 256
    for r in range(0, rows, step):
        subs = lax.broadcasted_iota(jnp.int32, (step, rows), 0) + r
        found = jnp.where(row_ref[0, h : h + 1, :] == subs, 1.0, 0.0)
        sel_ref[slot, r : r + step, :] = found.astype(BF16)


def spans_of(rows):
    return [slice(c, c + CLUSTER) for c in range(0, rows, CLUSTER)]


def attend_kernel(x_ref, w_ref, bias_ref, row_ref, ctx_ref, moved_ref, probs_ref, sel_ref):
    rows = x_ref.shape[0]
    spans = spans_of(rows)
    for h in range(2):
        selector(row_ref, h, sel_ref, h)
    weight = jnp.concatenate([w_ref[c] for c in range(3)], axis=1)
    flat = dot_tt(weight, x_ref[...])
    parts = [flat[:128] + bias_ref[:, 0:1], flat[128:256], flat[256:] + bias_ref[:, 1:2]]
    parts = [part.astype(BF16) for part in parts]
    for h in range(2):
        cut = slice(h * HEAD_DIM, (h + 1) * HEAD_DIM)
        qkv = jnp.concatenate([part[cut] for part in parts], axis=0)
        moved = dot(qkv, sel_ref[h]).astype(BF16)
        moved_ref[h] = moved
        query, key, value = moved[:HEAD_DIM], moved[HEAD_DIM : 2 * HEAD_DIM], moved[2 * HEAD_DIM :]
        scores = jnp.concatenate([dot_tn(query[:, s], key[:, s]) for s in spans], axis=0) * SCALE
        shifted = jnp.exp(scores - jnp.max(scores, axis=-1, keepdims=True))
        probs = shifted / jnp.sum(shifted, axis=-1, keepdims=True)
        probs_b = probs.astype(BF16)
        probs_ref[h] = probs_b
        mixed = jnp.concatenate([dot_nt(value[:, s], probs_b[s]) for s in spans], axis=1)
        context = dot_nt(mixed.astype(BF16), sel_ref[h])
        ctx_ref[cut, :] = context.astype(BF16)


def attend(x, weight, bias_cols, order_rows):
    rows, width = x.shape
    pairs = order_rows.shape[0]
    local = weight.shape[2]
    return pl.pallas_call(
        attend_kernel,
        grid=(pairs,),
        in_specs=[
            whole(rows, width),
            pl.BlockSpec((3, width, 128), lambda p: (0, 0, p)),
            pl.BlockSpec((128, 2), lambda p: (p, 0)),
            pl.BlockSpec((1, 2, rows), lambda p: (p, 0, 0)),
        ],
        out_specs=[
            pl.BlockSpec((128, rows), lambda p: (p, 0)),
            pl.BlockSpec((2, 3 * HEAD_DIM, rows), lambda p: (p, 0, 0)),
            pl.BlockSpec((2, rows, CLUSTER), lambda p: (p, 0, 0)),
        ],
        out_shape=[
            shape((local, rows), BF16),
            shape((2 * pairs, 3 * HEAD_DIM, rows), BF16),
            shape((2 * pairs, rows, CLUSTER), BF16),
        ],
        scratch_shapes=[pltpu.VMEM((2, rows, rows), BF16)],
        compiler_params=params_of(40),
        cost_estimate=cost(12e9, 12e6),
        name="attend",
    )(x, weight, bias_cols, order_rows)


def block_place(j, order):
    place = 0
    for bit in order:
        place = 2 * place + ((j >> bit) & 1)
    return place


def write_halves(values, keep_ref, send_ref, mine, order, at):
    blocks = 2 ** (len(order) + 1)
    rows = values.shape[0] // blocks
    for j in range(0, blocks, 2):
        even, odd = values[j * rows : (j + 1) * rows], values[(j + 1) * rows : (j + 2) * rows]
        place = (block_place(j, order),) + at
        keep_ref[place] = jnp.where(mine == 0, even, odd)
        send_ref[place] = jnp.where(mine == 0, odd, even)


def attend_back_kernel(
    orders, core_ref, x_ref, da_ref, ow_ref, ctx_ref, w_ref, row_ref, moved_ref, probs_ref, part_ref, bias_ref, *refs
):
    *grad_refs, sel_ref = refs
    rows = da_ref.shape[0]
    spans = spans_of(rows)
    for h in range(2):
        selector(row_ref, h, sel_ref, h)
    d_attn = da_ref[...]
    d_context = dot_nt(ow_ref[...], d_attn).astype(BF16)
    d_out = dot_tt(d_attn, ctx_ref[...])
    found = []
    for h in range(2):
        d_moved = dot(d_context[h * HEAD_DIM : (h + 1) * HEAD_DIM], sel_ref[h]).astype(BF16)
        moved = moved_ref[h]
        query, key, value = moved[:HEAD_DIM], moved[HEAD_DIM : 2 * HEAD_DIM], moved[2 * HEAD_DIM :]
        probs_b = probs_ref[h]
        probs = probs_b.astype(F32)
        d_value = jnp.concatenate([dot(d_moved[:, s], probs_b[s]) for s in spans], axis=1)
        d_probs = jnp.concatenate([dot_tn(d_moved[:, s], value[:, s]) for s in spans], axis=0)
        inner = jnp.sum(probs * d_probs, axis=-1, keepdims=True)
        d_scores = (probs * (d_probs - inner)).astype(BF16)
        d_query = jnp.concatenate([dot_nt(key[:, s], d_scores[s]) for s in spans], axis=1) * SCALE
        d_key = jnp.concatenate([dot(query[:, s], d_scores[s]) for s in spans], axis=1) * SCALE
        three = jnp.concatenate([d_query, d_key, d_value], axis=0).astype(BF16)
        found.append(dot_nt(three, sel_ref[h]).astype(BF16))
    d_qkv = jnp.concatenate(
        [f[c * HEAD_DIM : (c + 1) * HEAD_DIM] for c in range(3) for f in found], axis=0
    )
    sums = dot_nt(jnp.ones((8, rows), BF16), d_qkv)
    bias_ref[0:1, :] = sums[0:1, :128]
    bias_ref[1:2, :] = sums[0:1, 256:]
    grads = dot_tt(x_ref[...], d_qkv)
    for c in range(4):
        values = grads[:, c * 128 : (c + 1) * 128] if c < 3 else d_out
        if orders:
            write_halves(values, *grad_refs[c // 2 * 2 :][:2], core_ref[0], orders[c // 2], (c % 2,))
        else:
            grad_refs[0][c] = values
    part = dot_tt(d_qkv, jnp.concatenate([w_ref[c] for c in range(3)], axis=1))

    @pl.when(pl.program_id(0) == 0)
    def _():
        part_ref[...] = part

    @pl.when(pl.program_id(0) > 0)
    def _():
        part_ref[...] += part


def attend_back(orders, core, x, d_attn, out_weight, context, weight, order_rows, moved, probs):
    rows, width = x.shape
    local = weight.shape[2]
    pairs = order_rows.shape[0]
    if orders:
        blocks = 2 ** len(orders[0])
        height = width // (2 * blocks)
        grad_specs = [pl.BlockSpec((blocks, 2, height, 128), lambda p: (0, 0, 0, p))] * 4
        grad_shapes = [shape((blocks, 2, height, local), F32)] * 4
    else:
        grad_specs = [pl.BlockSpec((4, width, 128), lambda p: (0, 0, p))]
        grad_shapes = [shape((4, width, local), F32)]
    return pl.pallas_call(
        functools.partial(attend_back_kernel, orders),
        grid=(pairs,),
        in_specs=[
            pl.BlockSpec(memory_space=pltpu.SMEM),
            whole(rows, width),
            whole(rows, width),
            pl.BlockSpec((128, width), lambda p: (p, 0)),
            pl.BlockSpec((128, rows), lambda p: (p, 0)),
            pl.BlockSpec((3, width, 128), lambda p: (0, 0, p)),
            pl.BlockSpec((1, 2, rows), lambda p: (p, 0, 0)),
            pl.BlockSpec((2, 3 * HEAD_DIM, rows), lambda p: (p, 0, 0)),
            pl.BlockSpec((2, rows, CLUSTER), lambda p: (p, 0, 0)),
        ],
        out_specs=[
            pl.BlockSpec((rows, width), lambda p: (0, 0)), pl.BlockSpec((2, 128), lambda p: (0, p)), *grad_specs
        ],
        out_shape=[shape((rows, width), F32), shape((2, local), F32), *grad_shapes],
        scratch_shapes=[pltpu.VMEM((2, rows, rows), BF16)],
        compiler_params=params_of(30),
        cost_estimate=cost(20e9, 20e6),
        name="attend_back",
    )(core, x, d_attn, out_weight, context, weight, order_rows, moved, probs)


def gelu_both(hidden):
    scale = 0.7978845608028654
    square = hidden * hidden
    bent = jnp.tanh(hidden * (scale + (scale * 0.044715) * square))
    half = 0.5 + 0.5 * bent
    active = hidden * half
    slope = half + 0.5 * hidden * (1.0 - bent * bent) * (scale + (3 * scale * 0.044715) * square)
    return active.astype(BF16), slope.astype(BF16)


def normalized(values):
    centred = values - jnp.mean(values, axis=-1, keepdims=True)
    factor = lax.rsqrt(jnp.mean(centred * centred, axis=-1, keepdims=True) + EPSILON)
    return centred * factor, factor


def norm_back(grad, unit, factor):
    mean = jnp.mean(grad, axis=-1, keepdims=True)
    inner = jnp.mean(grad * unit, axis=-1, keepdims=True)
    return factor * (grad - mean - unit * inner)


def unit_cuts(units):
    return [slice(u, u + UNIT_TILE) for u in range(0, units, UNIT_TILE)]


def narrow_copies(parts, stage, sems, places, out_s):
    depth = stage.shape[0]
    rows = stage.shape[1]

    def copy(k):
        return pltpu.make_async_copy(parts[k].at[0], stage.at[k % depth], sems.at[k % depth])

    def start():
        for k in range(min(depth, len(parts))):
            copy(k).start()

    def finish():
        for k in range(len(parts)):
            copy(k).wait()
            place = pl.multiple_of(places[k] * rows, rows)
            out_s[pl.ds(place, rows), :] = stage[k % depth].astype(BF16)
            if k + depth < len(parts):
                copy(k + depth).start()

    return start, finish


def placed_kernel(count, slots_ref, *refs):
    up_parts, down_parts, refs = refs[:count], refs[count : 2 * count], refs[2 * count :]
    up_ref, down_ref, up_stage, down_stage, up_sems, down_sems = refs
    places = [slots_ref[k] for k in range(count)]
    start_up, finish_up = narrow_copies(up_parts, up_stage, up_sems, places, up_ref)
    start_down, finish_down = narrow_copies(down_parts, down_stage, down_sems, places, down_ref)
    start_up()
    start_down()
    finish_up()
    finish_down()


def placed(slots, ups, downs, group):
    count = len(ups)
    scalars = pl.BlockSpec(memory_space=pltpu.SMEM)
    anywhere = pl.BlockSpec(memory_space=pl.ANY)
    out_shape = [
        shape((group * part[0].shape[1], part[0].shape[2]), BF16) for part in (ups, downs)
    ]
    return pl.pallas_call(
        functools.partial(placed_kernel, count),
        grid=(1,),
        in_specs=[scalars] + [anywhere] * (2 * count),
        out_specs=[whole(*out.shape) for out in out_shape],
        out_shape=out_shape,
        scratch_shapes=[
            pltpu.VMEM((count,) + ups[0].shape[1:], F32), pltpu.VMEM((count,) + downs[0].shape[1:], F32),
            pltpu.SemaphoreType.DMA((count,)), pltpu.SemaphoreType.DMA((count,)),
        ],
        compiler_params=params_of(20),
        cost_estimate=cost(1e6, 1e6),
        name="placed",
    )(slots, *ups, *downs)


def feed_rows(
    here, x_ref, cot_ref, ctx_ref, far_ctx_refs, vectors, ready, out_s, far_out_s, up_s, down_s, far_up_s, far_down_s,
    mixed_ref, d_pre_ref, d_attn_ref, sums_ref, up_sums_ref, nb_s, act_s, d_feed_s, d_hidden_s, far_slope_s,
):
    units = up_s.shape[1]
    out_bias, gain1, bias1, down_bias, gain2, bias2, up_bias, far_bias = vectors
    attention = dot_tn(ctx_ref[:, here], out_s[...])
    far_ctx = jnp.concatenate([ref[:, here].astype(BF16) for ref in far_ctx_refs], axis=0)
    attention += dot_tn(far_ctx, far_out_s[...])
    yield
    unit1, factor1 = normalized(x_ref[here, :].astype(F32) + attention + out_bias)
    normed = unit1 * gain1 + bias1
    nb = normed.astype(BF16)
    nb_s[here, :] = nb
    total = normed + down_bias
    yield
    ready("near")
    for cut in unit_cuts(units):
        active, slope = gelu_both(dot(nb, up_s[:, cut]) + up_bias[:, cut])
        act_s[here, cut] = active
        d_hidden_s[here, cut] = slope
        total = total + dot(active, down_s[cut, :])
        yield
    ready("far")
    for cut in unit_cuts(units):
        far_active, far_slope = gelu_both(dot(nb, far_up_s[:, cut]) + far_bias[:, cut])
        far_slope_s[here, cut] = far_slope
        total = total + dot(far_active, far_down_s[cut, :])
        yield
    unit2, factor2 = normalized(total)
    mixed_ref[here, :] = (unit2 * gain2 + bias2).astype(BF16)
    grad = cot_ref[here, :].astype(F32)
    sums_ref[0:1, :] += jnp.sum(grad * unit2, axis=0, keepdims=True)
    sums_ref[1:2, :] += jnp.sum(grad, axis=0, keepdims=True)
    d_sum = norm_back(grad * gain2, unit2, factor2)
    d_feed = d_sum.astype(BF16)
    d_feed_s[here, :] = d_feed
    sums_ref[2:3, :] += jnp.sum(d_feed.astype(F32), axis=0, keepdims=True)
    yield
    d_normed = d_sum
    for cut in unit_cuts(units):
        d_active = dot_nt(d_feed, down_s[cut, :])
        d_hidden = (d_active * d_hidden_s[here, cut].astype(F32)).astype(BF16)
        d_hidden_s[here, cut] = d_hidden
        up_sums_ref[:, cut] += jnp.sum(d_hidden.astype(F32), axis=0, keepdims=True)
        d_normed = d_normed + dot_nt(d_hidden, up_s[:, cut])
        yield
    for cut in unit_cuts(units):
        far_d_active = dot_nt(d_feed, far_down_s[cut, :])
        far_d_hidden = (far_d_active * far_slope_s[here, cut].astype(F32)).astype(BF16)
        d_normed = d_normed + dot_nt(far_d_hidden, far_up_s[:, cut])
        yield
    sums_ref[3:4, :] += jnp.sum(d_normed * unit1, axis=0, keepdims=True)
    sums_ref[4:5, :] += jnp.sum(d_normed, axis=0, keepdims=True)
    d_pre = norm_back(d_normed * gain1, unit1, factor1)
    d_pre_ref[here, :] = d_pre
    d_attn = d_pre.astype(BF16)
    d_attn_ref[here, :] = d_attn
    sums_ref[5:6, :] += jnp.sum(d_attn.astype(F32), axis=0, keepdims=True)


def in_turn(programs, lag):
    waiting = [k * lag for k in range(len(programs))]
    while any(wait is not None for wait in waiting):
        for k, wait in enumerate(waiting):
            if wait == 0:
                if next(programs[k], "end") == "end":
                    waiting[k] = None
            elif wait is not None:
                waiting[k] = wait - 1


def feed_kernel(orders, late_count, core_ref, slots_ref, x_ref, cot_ref, ctx_ref, far0_ref, far1_ref, far2_ref, *refs):
    vector_refs, refs = refs[:8], refs[8:]
    out_hbm, near_half_hbm, far_half_hbm, up_hbm, down_hbm, far_up_hbm, far_down_hbm, *refs = refs
    up_parts, down_parts, refs = refs[:late_count], refs[late_count : 2 * late_count], refs[2 * late_count :]
    mixed_ref, d_pre_ref, d_attn_ref, sums_ref, up_sums_ref, *refs = refs
    count = 4 if orders else 2
    grad_refs, refs = refs[:count], refs[count:]
    nb_s, act_s, d_feed_s, d_hidden_s, far_slope_s, out_s, far_out_s, up_s, down_s, far_up_s, far_down_s, *refs = refs
    half_stage, up_stage, down_stage, sems, up_sems, down_sems = refs
    step = pl.program_id(0)
    rows = x_ref.shape[0]
    tiles = 1

    @pl.when(step == 0)
    def _():
        copies = [
            pltpu.make_async_copy(source, target, sems.at[k])
            for k, (source, target) in enumerate((
                (out_hbm, out_s), (near_half_hbm, half_stage.at[0]), (far_half_hbm, half_stage.at[1]),
                (up_hbm, up_s), (down_hbm, down_s), (far_up_hbm, far_up_s), (far_down_hbm, far_down_s),
            ))
        ]
        places = [slots_ref[k] for k in range(late_count)]
        start_up, finish_up = narrow_copies(up_parts, up_stage, up_sems, places, far_up_s)
        start_down, finish_down = narrow_copies(down_parts, down_stage, down_sems, places, far_down_s)
        for copy in copies:
            copy.start()
        start_up()
        start_down()
        sums_ref[...] = jnp.zeros_like(sums_ref)
        up_sums_ref[...] = jnp.zeros_like(up_sums_ref)
        for copy in copies[:3]:
            copy.wait()
        half = half_stage.shape[1]
        for k in range(2):
            place = pl.multiple_of((core_ref[0] ^ k) * half, half)
            far_out_s[pl.ds(place, half), :] = half_stage[k].astype(BF16)
        done = []

        def ready(what):
            if what in done:
                return
            done.append(what)
            for copy in copies[3:5] if what == "near" else copies[5:]:
                copy.wait()
            if what == "far":
                finish_up()
                finish_down()

        vectors = [ref[...].reshape(1, ref.shape[0]) for ref in vector_refs]
        in_turn(
            [
                feed_rows(
                    slice(r, r + ROW_TILE), x_ref, cot_ref, ctx_ref, (far0_ref, far1_ref, far2_ref), vectors, ready,
                    out_s, far_out_s, up_s, down_s, far_up_s, far_down_s, mixed_ref, d_pre_ref, d_attn_ref, sums_ref,
                    up_sums_ref, nb_s, act_s, d_feed_s, d_hidden_s, far_slope_s,
                )
                for r in range(0, rows, ROW_TILE)
            ],
            LAG,
        )

    @pl.when(step >= tiles)
    def _():
        there = pl.ds(pl.multiple_of((step - tiles) * GRAD_TILE, GRAD_TILE), GRAD_TILE)
        d_down = dot_tn(d_feed_s[...], act_s[:, there])
        d_up = dot_tn(nb_s[...], d_hidden_s[:, there])
        if orders:
            write_halves(d_down, *grad_refs[:2], core_ref[0], orders[0], ())
            write_halves(d_up, *grad_refs[2:], core_ref[0], orders[1], ())
        else:
            grad_refs[0][...] = d_down
            grad_refs[1][...] = d_up


def feed(
    orders, core, slots, x, cotangent, context, far_context, out_weight, halves, vectors, up, down, far_up, far_down,
    ups, downs,
):
    rows, width = x.shape
    local, units = out_weight.shape[0], up.shape[1]
    tiles = 1
    if orders:
        blocks = 2 ** len(orders[0])
        height = width // (2 * blocks)
        grad_specs = [
            pl.BlockSpec((blocks, height, GRAD_TILE), lambda i: (0, 0, jnp.maximum(i - tiles, 0)))
        ] * 4
        grad_shapes = [shape((blocks, height, units), F32)] * 4
    else:
        grad_specs = [pl.BlockSpec((width, GRAD_TILE), lambda i: (0, jnp.maximum(i - tiles, 0)))] * 2
        grad_shapes = [shape((width, units), F32)] * 2
    scalars = pl.BlockSpec(memory_space=pltpu.SMEM)
    anywhere = pl.BlockSpec(memory_space=pl.ANY)
    depth = len(ups)
    return pl.pallas_call(
        functools.partial(feed_kernel, orders, len(ups)),
        grid=(tiles + units // GRAD_TILE,),
        in_specs=[
            scalars, scalars, whole(rows, width), whole(rows, width), whole(local, rows),
            *[whole(*part.shape) for part in far_context], *[whole(v.shape[0]) for v in vectors],
            *[anywhere] * (7 + len(ups) + len(downs)),
        ],
        out_specs=[
            whole(rows, width), whole(rows, width), whole(rows, width), whole(8, width), whole(1, units),
            *grad_specs,
        ],
        out_shape=[
            shape((rows, width), BF16), shape((rows, width), F32), shape((rows, width), BF16),
            shape((8, width), F32), shape((1, units), F32), *grad_shapes,
        ],
        scratch_shapes=[
            pltpu.VMEM((rows, width), BF16), pltpu.VMEM((rows, units), BF16), pltpu.VMEM((rows, width), BF16),
            pltpu.VMEM((rows, units), BF16), pltpu.VMEM((rows, units), BF16),
            pltpu.VMEM((local, width), BF16), pltpu.VMEM((local, width), BF16),
            pltpu.VMEM((width, units), BF16), pltpu.VMEM((units, width), BF16),
            pltpu.VMEM((width, units), BF16), pltpu.VMEM((units, width), BF16),
            pltpu.VMEM((2,) + halves[0].shape, F32), pltpu.VMEM((depth,) + ups[0].shape[1:], F32),
            pltpu.VMEM((depth,) + downs[0].shape[1:], F32), pltpu.SemaphoreType.DMA((7,)),
            pltpu.SemaphoreType.DMA((depth,)), pltpu.SemaphoreType.DMA((depth,)),
        ],
        compiler_params=params_of(60),
        cost_estimate=cost(25e9, 30e6),
        name="feed",
    )(
        core, slots, x, cotangent, context, *far_context, *vectors, out_weight, *halves, up, down,
        far_up, far_down, *ups, *downs,
    )


def make_body(n_items):
    def body(
        hidden_in,
        cluster_order,
        qkv_weight,
        qv_bias,
        out_weight,
        out_bias,
        norm1_gain,
        norm1_bias,
        up_weight,
        up_bias,
        down_weight,
        down_bias,
        norm2_gain,
        norm2_bias,
        cotangent,
    ):
        rows, width = hidden_in.shape
        units = up_weight.shape[1]
        local = out_weight.shape[0]
        item = lax.axis_index("items")
        core = item & 1
        group = 8
        place = item % group

        def piece(values):
            count = values.shape[0] // group
            return lax.dynamic_slice_in_dim(values, place * count, count, 0).astype(F32)[None]

        up_piece = piece(up_weight)
        down_piece = piece(after(down_weight, up_piece))
        half = local // 2
        far_up = swapped(up_piece)
        far_down = swapped(down_piece)
        ordering = cluster_order[:, 0, :]
        order_rows = ordering.reshape(-1, 2, rows)
        x = after(hidden_in, up_piece, down_piece)
        context, moved, probs = attend(x, qkv_weight, qv_bias.T, order_rows)
        pairs = order_rows.shape[0]
        far_context = [
            swapped(context[p * 128 : (p + 1) * 128].astype(F32)) for p in range(pairs)
        ]
        out_piece = lax.dynamic_slice_in_dim(out_weight, core * half, half, 0)
        out_piece = out_piece.astype(F32)
        far_bias = swapped(up_bias)

        trade = lambda values, step: traded(values, step, n_items)
        at_once = lambda *values: lax.optimization_barrier(values)
        far_half = swapped(after(out_piece, down_piece))
        up0 = after(far_up, context)
        up4, up2 = trade(up0, 4), trade(up0, 2)
        down0 = after(far_down, up0)
        down4, down2 = trade(down0, 4), trade(down0, 2)
        up4, up2, down4, down2, far_half, far_context[0], far_bias = at_once(
            up4, up2, down4, down2, far_half, far_context[0], far_bias
        )
        up6, down6 = trade(up4, 2), trade(down4, 2)
        ups, downs = [up0, up4, up2], [down0, down4, down2]
        ups, downs = [[after(part, down4) for part in parts] for parts in (ups, downs)]
        up_beside = [trade(part, 1) for part in ups]
        down_beside = [trade(part, 1) for part in downs]
        other_half = trade(after(far_half, down4), 1)
        all_slots = lambda ks: jnp.stack([place ^ k ^ c for c in (0, 1) for k in ks]).astype(jnp.int32)
        slots = all_slots((6,))
        far_up, far_down = placed(all_slots((0, 4, 2)), ups + up_beside, downs + down_beside, group)
        up6, down6, far_context[1], far_context[2], far_up = at_once(
            up6, down6, far_context[1], far_context[2], far_up
        )
        ups, downs = [[part, trade(part, 1)] for part in (up6, down6)]
        which = core.astype(jnp.int32).reshape(1)

        split = width % (8 * n_items) == 0
        bits = tuple(range(1, n_items.bit_length() - 1))
        late_y = bits[1:2] + bits[:1] + bits[2:]
        mixed, d_pre, d_attn, sums, up_sums, *grads = feed(
            (bits, late_y) if split else None, which, slots, x, cotangent, context, far_context,
            out_weight, [far_half, other_half],
            [out_bias, norm1_gain, norm1_bias, down_bias, norm2_gain, norm2_bias, up_bias, far_bias],
            up_weight, down_weight, far_up, far_down, ups, downs,
        )

        def packed_of(grad_qv):
            return jnp.concatenate(
                [sums, up_sums.reshape(-1, width), grad_qv.reshape(-1, width)], axis=0
            )

        back = lambda d_attn: attend_back(
            (bits, late_y) if split else None, which, x, d_attn, out_weight, context, qkv_weight,
            order_rows, moved, probs,
        )
        if split:
            halving = lambda keep, send, order: Halving(keep, send, order, n_items).trade()
            down_sum, up_sum = halving(*grads[:2], bits), halving(*grads[2:], late_y)
            sent = arrived([down_sum, up_sum])
            down_sum.trade()
            up_sum.trade()
            part, grad_qv, *halves = back(after(d_attn, *sent))
            far_part = swapped(part)
            first, second = halving(*halves[:2], bits), halving(*halves[2:], late_y)
            sent = arrived([down_sum, up_sum], part)
            down_sum.trade()
            up_sum.trade()
            sent = arrived([first, second], *sent)
            first.extra = packed_of(grad_qv)
            first.extra = first.extra + traded(first.extra, 1, n_items)
            first.trade()
            second.trade()
            sums_all = [down_sum, up_sum, first, second]
            for _ in bits[2:]:
                arrived(sums_all)
                for one in sums_all[::-1]:
                    one.trade()
            summed_down, summed_up, *sent = arrived(sums_all)
            first.trade()
            second.trade()
            far_part = after(far_part, summed_down, summed_up, *sent)
            grad_inputs = (d_pre + part + far_part).astype(BF16)
            summed = arrived([first, second], grad_inputs)
            summed_rest = [summed[c // 2][c % 2] for c in range(4)]
            packed = first.extra
        else:
            part, grad_qv, grad_rest = back(d_attn)
            grad_inputs = (d_pre + part + swapped(part)).astype(BF16)
            summed_down = scattered(grads[0], n_items, 0)
            summed_up = scattered(grads[1], n_items, 0)
            summed_rest = scattered(grad_rest, n_items, 1)
            packed = all_sum(packed_of(grad_qv), n_items)
        small = packed[:8]
        up_small = packed[8 : 8 + units // width].reshape(units)
        qv_small = packed[8 + units // width :].reshape(2, local)
        return (
            mixed,
            grad_inputs,
            jnp.stack([summed_rest[c] for c in range(3)]),
            qv_small,
            summed_rest[3].T,
            small[5],
            small[3],
            small[4],
            summed_up,
            up_small,
            summed_down.T,
            small[2],
            small[0],
            small[1],
        )

    return body


def solution(mesh):
    return jax.shard_map(
        make_body(mesh.shape["items"]),
        mesh=mesh,
        in_specs=(
            P("items", None),
            P("heads", "items", None),
            P(None, None, "heads"),
            P(None, "heads"),
            P("heads", None),
            P(),
            P(),
            P(),
            P(None, "heads"),
            P("heads"),
            P("heads", None),
            P(),
            P(),
            P(),
            P("items", None),
        ),
        out_specs=(
            P("items", None),
            P("items", None),
            P(None, "items", "heads"),
            P(None, "heads"),
            P("heads", "items"),
            P(),
            P(),
            P(),
            P("items", "heads"),
            P("heads"),
            P("heads", "items"),
            P(),
            P(),
            P(),
        ),
        check_vma=False,
    )
```

profile of v0, /device:TPU:0, one launch (start us, length us, event | category | flops | bytes accessed | tf_op | source)
XLA Modules:
  0.0 305.4 jit_solution(2589120542610745598)
XLA Ops:
  1.8 3.0 collective-permute-start
  4.8 1.8 bitcast_convert_fusion
  8.4 13.3 %attend.1 = (bf16[384,1024]{1,0:T(8,128)(2,1)S(1)}, bf16[6,192,1024]{2,1,0:T(8,128)(2,1)S(1)}, bf16[6,1024,128]{2,1,0:T(8,128)(2,1)S(1)}) custom-call(bf16[1024,768]{1,0:T(8,128)(2,1)S(1)} %copy-done, bf16[3,768,384]{2,1,0:T(8,128)(2,1)S(1)} %copy-done.4, f32[384,2]{1,0:T(8,128)S(1)} %bitcast.102, s32[3,2,1024]{2,1,0:T(2,128)S(1)} %reshape_squeeze.3.row_ref), custom_call_target="tpu_custom_call" | custom-call | flops 12000000 | bytes 12000 | tf_op jit(solution)/shard_map/attend/pallas_call | solution.py:167
  25.1 2.0 collective-permute-start.7
  27.2 2.1 collective-permute-start.6
  29.3 2.5 collective-permute-done.3.refs_6_
  31.7 2.1 collective-permute-start.4
  33.9 1.5 collective-permute-start.5
  35.4 7.6 %collective-permute-done.8.refs_7_ = f32[1536]{0:T(1024)S(1)} collective-permute-done((f32[1536]{0:T(1024)S(1)}, f32[1536]{0:T(1024)S(1)}, u32[]{:S(2)}, u32[]{:S(2)}) %collective-permute-start.8) | collective-permute-done | bytes 6176 | tf_op jit(solution)/shard_map/ppermute | solution.py:55
  43.0 2.1 collective-permute-start.1
  45.2 1.5 collective-permute-start.2
  46.7 8.1 %collective-permute-done.6.refs_9_ = f32[192,768]{1,0:T(8,128)S(1)} collective-permute-done((f32[192,768]{1,0:T(8,128)S(1)}, f32[192,768]{1,0:T(8,128)S(1)}, u32[]{:S(2)}, u32[]{:S(2)}) %collective-permute-start.6) | collective-permute-done | bytes 589856 | tf_op jit(solution)/shard_map/ppermute | solution.py:55
  54.9 3.4 %collective-permute-done.1.refs_1_ = f32[1,96,1536]{2,1,0:T(8,128)S(1)} collective-permute-done((f32[1,96,1536]{2,1,0:T(8,128)S(1)}, f32[1,96,1536]{2,1,0:T(8,128)S(1)}, u32[]{:S(2)}, u32[]{:S(2)}) %collective-permute-start.1) | collective-permute-done | bytes 589856 | tf_op jit(solution)/shard_map/ppermute | solution.py:59
  60.5 1.8 collective-permute-done.18.refs_11_
  64.1 1.5 collective-permute-start.10
  76.1 2.9 placed.1
  79.0 1.5 copy-done.8
  82.9 10.0 %collective-permute-done.12.far2_ref = f32[128,1024]{1,0:T(8,128)} collective-permute-done((f32[128,1024]{1,0:T(8,128)}, f32[128,1024]{1,0:T(8,128)}, u32[]{:S(2)}, u32[]{:S(2)}) %collective-permute-start.12) | collective-permute-done | bytes 524320 | tf_op jit(solution)/shard_map/ppermute | solution.py:55
  96.8 68.6 %feed.1 = (bf16[1024,768]{1,0:T(8,128)(2,1)}, f32[1024,768]{1,0:T(8,128)}, bf16[1024,768]{1,0:T(8,128)(2,1)}, f32[8,768]{1,0:T(8,128)}, f32[1,1536]{1,0:T(1,128)...) custom-call(s32[1]{0:T(128)} %bitcast.core_ref, ...), custom_call_target="tpu_custom_call" | custom-call | flops 25000000 | bytes 30000 | tf_op jit(solution)/shard_map/feed/pallas_call | solution.py:547
  166.0 6.2 %collective-permute-done.22 = f32[8,48,1536]{2,1,0:T(8,128)S(1)} collective-permute-done((f32[8,48,1536]{2,1,0:T(8,128)}, f32[8,48,1536]{2,1,0:T(8,128)S(1)}, u32[]{:S(2)}, u32[]{:S(2)}) %collective-permute-start.22) | collective-permute-done | bytes 2359328 | tf_op jit(solution)/shard_map/ppermute | solution.py:59
  172.2 1.5 collective-permute-done.23
  173.8 6.9 %constant_dynamic-slice_fusion.3 = (f32[1,4,48,1536]{3,2,1,0:T(8,128)}, f32[4,48,1536]{2,1,0:T(8,128)}, f32[1,4,48,1536]{3,2,1,0:T(8,128)}, f32[1,4,48,1536]{3,2...) fusion(f32[2,4,48,1536]{3,2,1,0:T(8,128)} %bitcast.117, s32[]{:T(128)S(6)} %select_n.121, ...), kind=kLoop, calls=%fused_computation.33 | loop fusion | flops 589824 | bytes 16515088 | tf_op jit(solution)/shard_map/jit(dynamic_index_in_dim)/dynamic_slice | solution.py:105
  180.6 1.5 collective-permute-start.25
  182.7 20.5 %attend_back.1 = (f32[1024,768]{1,0:T(8,128)S(1)}, f32[2,384]{1,0:T(2,128)S(1)}, f32[8,2,48,384]{3,2,1,0:T(8,128)S(1)}, f32[8,2,48,384]{3,2,1,0:T(8,128)}, f32[8...) custom-call(s32[1]{0:T(128)} %bitcast.core_ref, bf16[1024,768]{1,0:T(8,128)(2,1)S(1)} %copy-done.1, ...), custom_call_target="tpu_custom_call" | custom-call | flops 20000000 | bytes 20000 | tf_op jit(solution)/shard_map/attend_back/pallas_call | solution.py:272
  205.9 2.3 collective-permute-done.33
  211.0 2.5 add_bitcast_fusion.4
  214.4 2.1 add_bitcast_fusion.5
  216.5 2.6 constant_dynamic-slice_fusion
  219.1 1.6 collective-permute-start.32
  220.7 2.6 constant_dynamic-slice_fusion.5
  224.9 10.8 %collective-permute-done.32 = f32[4,2,48,384]{3,2,1,0:T(8,128)} collective-permute-done((f32[4,2,48,384]{3,2,1,0:T(8,128)}, f32[4,2,48,384]{3,2,1,0:T(8,128)}, u32[]{:S(2)}, u32[]{:S(2)}) %collective-permute-start.32) | collective-permute-done | bytes 589856 | tf_op jit(solution)/shard_map/ppermute | solution.py:59
  235.7 5.5 %collective-permute-done.31 = f32[4,2,48,384]{3,2,1,0:T(8,128)} collective-permute-done((f32[4,2,48,384]{3,2,1,0:T(8,128)}, f32[4,2,48,384]{3,2,1,0:T(8,128)}, u32[]{:S(2)}, u32[]{:S(2)}) %collective-permute-start.31) | collective-permute-done | bytes 589856 | tf_op jit(solution)/shard_map/ppermute | solution.py:59
  241.2 5.4 %collective-permute-done.27 = f32[2,48,1536]{2,1,0:T(8,128)} collective-permute-done((f32[2,48,1536]{2,1,0:T(8,128)}, f32[2,48,1536]{2,1,0:T(8,128)}, u32[]{:S(2)}, u32[]{:S(2)}) %collective-permute-start.27) | collective-permute-done | bytes 589856 | tf_op jit(solution)/shard_map/ppermute | solution.py:59
  246.6 1.6 collective-permute-start.39
  248.3 1.9 add_bitcast_fusion.6
  250.7 1.7 add_bitcast_fusion.7
  253.4 2.0 bitcast_add_fusion.3
  255.4 2.6 collective-permute-start.36
  258.0 2.0 bitcast_add_fusion.4
  261.0 2.5 collective-permute-done.37
  263.5 14.7 %collective-permute-done.36 = f32[1,48,1536]{2,1,0:T(8,128)S(1)} collective-permute-done((f32[1,48,1536]{2,1,0:T(8,128)}, f32[1,48,1536]{2,1,0:T(8,128)S(1)}, u32[]{:S(2)}, u32[]{:S(2)}) %collective-permute-start.36) | collective-permute-done | bytes 294944 | tf_op jit(solution)/shard_map/ppermute | solution.py:59
  278.1 4.0 %collective-permute-done.35 = f32[1,48,1536]{2,1,0:T(8,128)} collective-permute-done((f32[1,48,1536]{2,1,0:T(8,128)}, f32[1,48,1536]{2,1,0:T(8,128)}, u32[]{:S(2)}, u32[]{:S(2)}) %collective-permute-start.35) | collective-permute-done | bytes 294944 | tf_op jit(solution)/shard_map/ppermute | solution.py:59
  284.1 3.0 collective-permute-start.41
  288.3 2.2 bitcast_add_fusion
  290.5 2.1 bitcast_add_fusion.2
  292.6 3.7 %add_convert_fusion = bf16[1024,768]{1,0:T(8,128)(2,1)} fusion(f32[1024,768]{1,0:T(8,128)} %collective-permute-done.24, f32[1024,768]{1,0:T(8,128)S(1)} %copy-done.31, f32[1024,768]{1,0:T(8,128)S(1)} %get-tuple-element.118), kind=kLoop, calls=%fused_computation | loop fusion | flops 2359296 | bytes 11010048 | tf_op jit(solution)/shard_map/convert_element_type | solution.py:699
  296.3 1.5 collective-permute-done.41
  297.9 1.6 collective-permute-done.40
  (175 shorter events, 47.4 us)
Async XLA Ops:
  1.8 27.4 %collective-permute-start = (f32[1,96,1536]{2,1,0:T(8,128)S(1)}, f32[1,96,1536]{2,1,0:T(8,128)S(1)}, u32[]{:S(2)}, u32[]{:S(2)}) collective-permute-start(f32[1,96,1536]{2,1,0:T(8,128)S(1)} %bitcast_convert_fusion.1), channel_id=1, source_target_pairs={{0,1},{1,0},{2,3},{3,2},{4,5},{5,4},{6,7},{7,6},{8,9},{9,8},{10,11... | collective-permute-start | bytes 1769480 | tf_op jit(solution)/shard_map/ppermute | solution.py:55
  6.6 25.1 %collective-permute-start.3 = (f32[1,192,768]{2,1,0:T(8,128)}, f32[1,192,768]{2,1,0:T(8,128)}, u32[]{:S(2)}, u32[]{:S(2)}) collective-permute-start(f32[1,192,768]{2,1,0:T(8,128)} %bitcast_convert_fusion), channel_id=1, source_target_pairs={{0,1},{1,0},{2,3},{3,2},{4,5},{5,4},{6,7},{7,6},{8,9},{9,8},{10,11... | collective-permute-start | bytes 1769480 | tf_op jit(solution)/shard_map/ppermute | solution.py:55
  25.1 20.1 %collective-permute-start.7 = (f32[128,1024]{1,0:T(8,128)}, f32[128,1024]{1,0:T(8,128)S(1)}, u32[]{:S(2)}, u32[]{:S(2)}) collective-permute-start(f32[128,1024]{1,0:T(8,128)} %get-tuple-element.165), channel_id=1, source_target_pairs={{0,1},{1,0},{2,3},{3,2},{4,5},{5,4},{6,7},{7,6},{8,9},{9,8},{10,11... | collective-permute-start | bytes 1572872 | tf_op jit(solution)/shard_map/ppermute | solution.py:55
  27.1 15.9 %collective-permute-start.8 = (f32[1536]{0:T(1024)S(1)}, f32[1536]{0:T(1024)S(1)}, u32[]{:S(2)}, u32[]{:S(2)}) collective-permute-start(f32[1536]{0:T(1024)S(1)} %copy-done.43), channel_id=1, source_target_pairs={{0,1},{1,0},{2,3},{3,2},{4,5},{5,4},{6,7},{7,6},{8,9},{9,8},{10,11... | collective-permute-start | bytes 18440 | tf_op jit(solution)/shard_map/ppermute | solution.py:55
  27.2 27.6 %collective-permute-start.6 = (f32[192,768]{1,0:T(8,128)S(1)}, f32[192,768]{1,0:T(8,128)S(1)}, u32[]{:S(2)}, u32[]{:S(2)}) collective-permute-start(f32[192,768]{1,0:T(8,128)S(1)} %dynamic-slice_convert_fusion), channel_id=1, source_target_pairs={{0,1},{1,0},{2,3},{3,2},{4,5},{5,4},{6,7},{7,6},{8,9},{9,8},{10,11... | collective-permute-start | bytes 1769480 | tf_op jit(solution)/shard_map/ppermute | solution.py:55
  31.7 23.1 %collective-permute-start.4 = (f32[1,192,768]{2,1,0:T(8,128)}, f32[1,192,768]{2,1,0:T(8,128)S(1)}, u32[]{:S(2)}, u32[]{:S(2)}) collective-permute-start(f32[1,192,768]{2,1,0:T(8,128)} %collective-permute-done.3.refs_6_), channel_id=1, source_target_pairs={{0,8},{2,10},{4,12},{6,14},{8,0},{10,2},{12,4},{14,6},{16,24},{18,... | collective-permute-start | bytes 1769480 | tf_op jit(solution)/shard_map/ppermute | solution.py:59
  33.9 21.0 %collective-permute-start.5 = (f32[1,192,768]{2,1,0:T(8,128)}, f32[1,192,768]{2,1,0:T(8,128)S(1)}, u32[]{:S(2)}, u32[]{:S(2)}) collective-permute-start(f32[1,192,768]{2,1,0:T(8,128)} %collective-permute-done.3.refs_6_), channel_id=1, source_target_pairs={{0,4},{2,6},{4,0},{6,2},{8,12},{10,14},{12,8},{14,10},{16,20},{18,... | collective-permute-start | bytes 1769480 | tf_op jit(solution)/shard_map/ppermute | solution.py:59
  43.0 35.9 %copy-start.44 = (f32[1536]{0:T(1024)}, f32[1536]{0:T(1024)S(1)}, u32[]{:S(2)}) copy-start(f32[1536]{0:T(1024)S(1)} %collective-permute-done.8.refs_7_) | copy-start | bytes 18436
  43.0 15.2 %collective-permute-start.1 = (f32[1,96,1536]{2,1,0:T(8,128)S(1)}, f32[1,96,1536]{2,1,0:T(8,128)S(1)}, u32[]{:S(2)}, u32[]{:S(2)}) collective-permute-start(f32[1,96,1536]{2,1,0:T(8,128)S(1)} %collective-permute-done.refs_0_), channel_id=1, source_target_pairs={{0,8},{2,10},{4,12},{6,14},{8,0},{10,2},{12,4},{14,6},{16,24},{18,... | collective-permute-start | bytes 1769480 | tf_op jit(solution)/shard_map/ppermute | solution.py:59
  45.2 33.8 %copy-start.37 = (f32[128,1024]{1,0:T(8,128)}, f32[128,1024]{1,0:T(8,128)S(1)}, u32[]{:S(2)}) copy-start(f32[128,1024]{1,0:T(8,128)S(1)} %collective-permute-done.7.far0_ref) | copy-start | bytes 1572868
  45.2 14.3 %collective-permute-start.2 = (f32[1,96,1536]{2,1,0:T(8,128)S(1)}, f32[1,96,1536]{2,1,0:T(8,128)S(1)}, u32[]{:S(2)}, u32[]{:S(2)}) collective-permute-start(f32[1,96,1536]{2,1,0:T(8,128)S(1)} %collective-permute-done.refs_0_), channel_id=1, source_target_pairs={{0,4},{2,6},{4,0},{6,2},{8,12},{10,14},{12,8},{14,10},{16,20},{18,... | collective-permute-start | bytes 1769480 | tf_op jit(solution)/shard_map/ppermute | solution.py:59
  59.5 2.8 collective-permute-start.18
  59.5 3.8 %collective-permute-start.16 = (f32[1,192,768]{2,1,0:T(8,128)}, f32[1,192,768]{2,1,0:T(8,128)S(1)}, u32[]{:S(2)}, u32[]{:S(2)}) collective-permute-start(f32[1,192,768]{2,1,0:T(8,128)} %collective-permute-done.3.refs_6_), channel_id=1, source_target_pairs={{0,2},{2,0},{4,6},{6,4},{8,10},{10,8},{12,14},{14,12},{16,18},{18,... | collective-permute-start | bytes 1769480 | tf_op jit(solution)/shard_map/ppermute | solution.py:59
  60.0 5.6 %collective-permute-start.15 = (f32[1,96,1536]{2,1,0:T(8,128)S(1)}, f32[1,96,1536]{2,1,0:T(8,128)S(1)}, u32[]{:S(2)}, u32[]{:S(2)}) collective-permute-start(f32[1,96,1536]{2,1,0:T(8,128)S(1)} %collective-permute-done.2.refs_2_), channel_id=1, source_target_pairs={{0,2},{2,0},{4,6},{6,4},{8,10},{10,8},{12,14},{14,12},{16,18},{18,... | collective-permute-start | bytes 1769480 | tf_op jit(solution)/shard_map/ppermute | solution.py:59
  60.0 6.9 %collective-permute-start.14 = (f32[1,96,1536]{2,1,0:T(8,128)S(1)}, f32[1,96,1536]{2,1,0:T(8,128)S(1)}, u32[]{:S(2)}, u32[]{:S(2)}) collective-permute-start(f32[1,96,1536]{2,1,0:T(8,128)S(1)} %collective-permute-done.1.refs_1_), channel_id=1, source_target_pairs={{0,2},{2,0},{4,6},{6,4},{8,10},{10,8},{12,14},{14,12},{16,18},{18,... | collective-permute-start | bytes 1769480 | tf_op jit(solution)/shard_map/ppermute | solution.py:59
  60.5 8.7 %collective-permute-start.13 = (f32[1,96,1536]{2,1,0:T(8,128)S(1)}, f32[1,96,1536]{2,1,0:T(8,128)S(1)}, u32[]{:S(2)}, u32[]{:S(2)}) collective-permute-start(f32[1,96,1536]{2,1,0:T(8,128)S(1)} %collective-permute-done.refs_0_), channel_id=1, source_target_pairs={{0,2},{2,0},{4,6},{6,4},{8,10},{10,8},{12,14},{14,12},{16,18},{18,... | collective-permute-start | bytes 1769480 | tf_op jit(solution)/shard_map/ppermute | solution.py:59
  63.1 7.6 %collective-permute-start.17 = (f32[1,192,768]{2,1,0:T(8,128)S(1)}, f32[1,192,768]{2,1,0:T(8,128)}, u32[]{:S(2)}, u32[]{:S(2)}) collective-permute-start(f32[1,192,768]{2,1,0:T(8,128)S(1)} %collective-permute-done.4.refs_7_), channel_id=1, source_target_pairs={{0,2},{2,0},{4,6},{6,4},{8,10},{10,8},{12,14},{14,12},{16,18},{18,... | collective-permute-start | bytes 1769480 | tf_op jit(solution)/shard_map/ppermute | solution.py:59
  64.1 28.9 %collective-permute-start.10 = (f32[1,192,768]{2,1,0:T(8,128)S(1)}, f32[1,192,768]{2,1,0:T(8,128)}, u32[]{:S(2)}, u32[]{:S(2)}) collective-permute-start(f32[1,192,768]{2,1,0:T(8,128)S(1)} %collective-permute-done.4.refs_7_), channel_id=1, source_target_pairs={{0,4},{2,6},{4,0},{6,2},{8,12},{10,14},{12,8},{14,10},{16,20},{18,... | collective-permute-start | bytes 1769480 | tf_op jit(solution)/shard_map/ppermute | solution.py:59
  66.4 26.5 %collective-permute-start.9 = (f32[1,96,1536]{2,1,0:T(8,128)S(1)}, f32[1,96,1536]{2,1,0:T(8,128)}, u32[]{:S(2)}, u32[]{:S(2)}) collective-permute-start(f32[1,96,1536]{2,1,0:T(8,128)S(1)} %collective-permute-done.1.refs_1_), channel_id=1, source_target_pairs={{0,4},{2,6},{4,0},{6,2},{8,12},{10,14},{12,8},{14,10},{16,20},{18,... | collective-permute-start | bytes 1769480 | tf_op jit(solution)/shard_map/ppermute | solution.py:59
  67.8 15.1 %collective-permute-start.11 = (f32[128,1024]{1,0:T(8,128)}, f32[128,1024]{1,0:T(8,128)}, u32[]{:S(2)}, u32[]{:S(2)}) collective-permute-start(f32[128,1024]{1,0:T(8,128)} %get-tuple-element.164), channel_id=1, source_target_pairs={{0,1},{1,0},{2,3},{3,2},{4,5},{5,4},{6,7},{7,6},{8,9},{9,8},{10,11... | collective-permute-start | bytes 1572872 | tf_op jit(solution)/shard_map/ppermute | solution.py:55
  70.1 22.9 %collective-permute-start.12 = (f32[128,1024]{1,0:T(8,128)}, f32[128,1024]{1,0:T(8,128)}, u32[]{:S(2)}, u32[]{:S(2)}) collective-permute-start(f32[128,1024]{1,0:T(8,128)} %get-tuple-element.163), channel_id=1, source_target_pairs={{0,1},{1,0},{2,3},{3,2},{4,5},{5,4},{6,7},{7,6},{8,9},{9,8},{10,11... | collective-permute-start | bytes 1572872 | tf_op jit(solution)/shard_map/ppermute | solution.py:55
  70.7 23.4 %collective-permute-start.19 = (f32[192,768]{1,0:T(8,128)}, f32[192,768]{1,0:T(8,128)}, u32[]{:S(2)}, u32[]{:S(2)}) collective-permute-start(f32[192,768]{1,0:T(8,128)} %copy-done.34), channel_id=1, source_target_pairs={{0,2},{2,0},{4,6},{6,4},{8,10},{10,8},{12,14},{14,12},{16,18},{18,... | collective-permute-start | bytes 1769480 | tf_op jit(solution)/shard_map/ppermute | solution.py:59
  93.0 2.2 collective-permute-start.20
  93.0 3.1 collective-permute-start.21
  165.4 6.8 %collective-permute-start.22 = (f32[8,48,1536]{2,1,0:T(8,128)}, f32[8,48,1536]{2,1,0:T(8,128)S(1)}, u32[]{:S(2)}, u32[]{:S(2)}) collective-permute-start(f32[8,48,1536]{2,1,0:T(8,128)} %get-tuple-element.110), channel_id=1, source_target_pairs={{0,2},{2,0},{4,6},{6,4},{8,10},{10,8},{12,14},{14,12},{16,18},{18,... | collective-permute-start | bytes 7077896 | tf_op jit(solution)/shard_map/ppermute | solution.py:59
  165.6 8.1 %collective-permute-start.23 = (f32[8,48,1536]{2,1,0:T(8,128)}, f32[8,48,1536]{2,1,0:T(8,128)}, u32[]{:S(2)}, u32[]{:S(2)}) collective-permute-start(f32[8,48,1536]{2,1,0:T(8,128)} %get-tuple-element.111), channel_id=1, source_target_pairs={{0,2},{2,0},{4,6},{6,4},{8,10},{10,8},{12,14},{14,12},{16,18},{18,... | collective-permute-start | bytes 7077896 | tf_op jit(solution)/shard_map/ppermute | solution.py:59
  180.6 29.2 %collective-permute-start.25 = (f32[4,48,1536]{2,1,0:T(8,128)}, f32[4,48,1536]{2,1,0:T(8,128)}, u32[]{:S(2)}, u32[]{:S(2)}) collective-permute-start(f32[4,48,1536]{2,1,0:T(8,128)} %get-tuple-element.169), channel_id=1, source_target_pairs={{0,4},{2,6},{4,0},{6,2},{8,12},{10,14},{12,8},{14,10},{16,20},{18,... | collective-permute-start | bytes 3538952 | tf_op jit(solution)/shard_map/ppermute | solution.py:59
  182.1 28.8 %collective-permute-start.26 = (f32[4,48,1536]{2,1,0:T(8,128)}, f32[4,48,1536]{2,1,0:T(8,128)}, u32[]{:S(2)}, u32[]{:S(2)}) collective-permute-start(f32[4,48,1536]{2,1,0:T(8,128)} %get-tuple-element.152), channel_id=1, source_target_pairs={{0,8},{2,10},{4,12},{6,14},{8,0},{10,2},{12,4},{14,6},{16,24},{18,... | collective-permute-start | bytes 3538952 | tf_op jit(solution)/shard_map/ppermute | solution.py:59
  182.7 23.2 %copy-start.40 = (f32[8,768]{1,0:T(8,128)S(1)}, f32[8,768]{1,0:T(8,128)}, u32[]{:S(2)}) copy-start(f32[8,768]{1,0:T(8,128)} %get-tuple-element.127) | copy-start | bytes 73732
  205.3 11.2 %collective-permute-start.29 = (f32[8,2,48,384]{3,2,1,0:T(8,128)}, f32[8,2,48,384]{3,2,1,0:T(8,128)}, u32[]{:S(2)}, u32[]{:S(2)}) collective-permute-start(f32[8,2,48,384]{3,2,1,0:T(8,128)} %get-tuple-element.122), channel_id=1, source_target_pairs={{0,2},{2,0},{4,6},{6,4},{8,10},{10,8},{12,14},{14,12},{16,18},{18,... | collective-permute-start | bytes 3538952 | tf_op jit(solution)/shard_map/ppermute | solution.py:59
  205.3 11.2 %collective-permute-start.30 = (f32[8,2,48,384]{3,2,1,0:T(8,128)}, f32[8,2,48,384]{3,2,1,0:T(8,128)}, u32[]{:S(2)}, u32[]{:S(2)}) collective-permute-start(f32[8,2,48,384]{3,2,1,0:T(8,128)} %get-tuple-element.123), channel_id=1, source_target_pairs={{0,2},{2,0},{4,6},{6,4},{8,10},{10,8},{12,14},{14,12},{16,18},{18,... | collective-permute-start | bytes 3538952 | tf_op jit(solution)/shard_map/ppermute | solution.py:59
  205.9 2.4 collective-permute-start.33
  208.3 84.3 %collective-permute-start.24 = (f32[1024,768]{1,0:T(8,128)S(1)}, f32[1024,768]{1,0:T(8,128)}, u32[]{:S(2)}, u32[]{:S(2)}) collective-permute-start(f32[1024,768]{1,0:T(8,128)S(1)} %get-tuple-element.118), channel_id=1, source_target_pairs={{0,1},{1,0},{2,3},{3,2},{4,5},{5,4},{6,7},{7,6},{8,9},{9,8},{10,11... | collective-permute-start | bytes 9437192 | tf_op jit(solution)/shard_map/ppermute | solution.py:55
  209.8 14.0 %collective-permute-start.34 = (f32[11,768]{1,0:T(8,128)S(1)}, f32[11,768]{1,0:T(8,128)S(1)}, u32[]{:S(2)}, u32[]{:S(2)}) collective-permute-start(f32[11,768]{1,0:T(8,128)S(1)} %fusion), channel_id=1, source_target_pairs={{0,4},{2,6},{4,0},{6,2},{8,12},{10,14},{12,8},{14,10},{16,20},{18,... | collective-permute-start | bytes 101384 | tf_op jit(solution)/shard_map/ppermute | solution.py:59
  213.4 27.8 %collective-permute-start.28 = (f32[2,48,1536]{2,1,0:T(8,128)}, f32[2,48,1536]{2,1,0:T(8,128)}, u32[]{:S(2)}, u32[]{:S(2)}) collective-permute-start(f32[2,48,1536]{2,1,0:T(8,128)} %add_bitcast_fusion.4), channel_id=1, source_target_pairs={{0,4},{2,6},{4,0},{6,2},{8,12},{10,14},{12,8},{14,10},{16,20},{18,... | collective-permute-start | bytes 1769480 | tf_op jit(solution)/shard_map/ppermute | solution.py:59
  219.1 16.6 %collective-permute-start.32 = (f32[4,2,48,384]{3,2,1,0:T(8,128)}, f32[4,2,48,384]{3,2,1,0:T(8,128)}, u32[]{:S(2)}, u32[]{:S(2)}) collective-permute-start(f32[4,2,48,384]{3,2,1,0:T(8,128)} %get-tuple-element.158), channel_id=1, source_target_pairs={{0,8},{2,10},{4,12},{6,14},{8,0},{10,2},{12,4},{14,6},{16,24},{18,... | collective-permute-start | bytes 1769480 | tf_op jit(solution)/shard_map/ppermute | solution.py:59
  223.3 17.9 %collective-permute-start.31 = (f32[4,2,48,384]{3,2,1,0:T(8,128)}, f32[4,2,48,384]{3,2,1,0:T(8,128)}, u32[]{:S(2)}, u32[]{:S(2)}) collective-permute-start(f32[4,2,48,384]{3,2,1,0:T(8,128)} %get-tuple-element.161), channel_id=1, source_target_pairs={{0,4},{2,6},{4,0},{6,2},{8,12},{10,14},{12,8},{14,10},{16,20},{18,... | collective-permute-start | bytes 1769480 | tf_op jit(solution)/shard_map/ppermute | solution.py:59
  223.8 22.8 %collective-permute-start.27 = (f32[2,48,1536]{2,1,0:T(8,128)}, f32[2,48,1536]{2,1,0:T(8,128)}, u32[]{:S(2)}, u32[]{:S(2)}) collective-permute-start(f32[2,48,1536]{2,1,0:T(8,128)} %add_bitcast_fusion.5), channel_id=1, source_target_pairs={{0,8},{2,10},{4,12},{6,14},{8,0},{10,2},{12,4},{14,6},{16,24},{18,... | collective-permute-start | bytes 1769480 | tf_op jit(solution)/shard_map/ppermute | solution.py:59
  224.8 25.8 %copy-start.32 = (f32[1,4,2,48,384]{4,3,2,1,0:T(8,128)S(1)}, f32[1,4,2,48,384]{4,3,2,1,0:T(8,128)}, u32[]{:S(2)}) copy-start(f32[1,4,2,48,384]{4,3,2,1,0:T(8,128)} %get-tuple-element.160) | copy-start | bytes 1769476
  224.8 25.8 %copy-start.33 = (f32[1,4,2,48,384]{4,3,2,1,0:T(8,128)S(1)}, f32[1,4,2,48,384]{4,3,2,1,0:T(8,128)}, u32[]{:S(2)}) copy-start(f32[1,4,2,48,384]{4,3,2,1,0:T(8,128)} %get-tuple-element.162) | copy-start | bytes 1769476
  246.6 13.4 %collective-permute-start.39 = (f32[11,768]{1,0:T(8,128)S(1)}, f32[11,768]{1,0:T(8,128)S(1)}, u32[]{:S(2)}, u32[]{:S(2)}) collective-permute-start(f32[11,768]{1,0:T(8,128)S(1)} %add.528), channel_id=1, source_target_pairs={{0,8},{2,10},{4,12},{6,14},{8,0},{10,2},{12,4},{14,6},{16,24},{18,... | collective-permute-start | bytes 101384 | tf_op jit(solution)/shard_map/ppermute | solution.py:59
  250.1 10.8 %collective-permute-start.38 = (f32[2,2,48,384]{3,2,1,0:T(8,128)}, f32[2,2,48,384]{3,2,1,0:T(8,128)}, u32[]{:S(2)}, u32[]{:S(2)}) collective-permute-start(f32[2,2,48,384]{3,2,1,0:T(8,128)} %add_bitcast_fusion.6), channel_id=1, source_target_pairs={{0,4},{2,6},{4,0},{6,2},{8,12},{10,14},{12,8},{14,10},{16,20},{18,... | collective-permute-start | bytes 884744 | tf_op jit(solution)/shard_map/ppermute | solution.py:59
  252.4 11.1 %collective-permute-start.37 = (f32[2,2,48,384]{3,2,1,0:T(8,128)}, f32[2,2,48,384]{3,2,1,0:T(8,128)}, u32[]{:S(2)}, u32[]{:S(2)}) collective-permute-start(f32[2,2,48,384]{3,2,1,0:T(8,128)} %add_bitcast_fusion.7), channel_id=1, source_target_pairs={{0,8},{2,10},{4,12},{6,14},{8,0},{10,2},{12,4},{14,6},{16,24},{18,... | collective-permute-start | bytes 884744 | tf_op jit(solution)/shard_map/ppermute | solution.py:59
  255.4 22.7 %collective-permute-start.36 = (f32[1,48,1536]{2,1,0:T(8,128)}, f32[1,48,1536]{2,1,0:T(8,128)S(1)}, u32[]{:S(2)}, u32[]{:S(2)}) collective-permute-start(f32[1,48,1536]{2,1,0:T(8,128)} %bitcast_add_fusion.3), channel_id=1, source_target_pairs={{0,16},{2,18},{4,20},{6,22},{8,24},{10,26},{12,28},{14,30},{16,0},... | collective-permute-start | bytes 884744 | tf_op jit(solution)/shard_map/ppermute | solution.py:59
  260.7 21.4 %collective-permute-start.35 = (f32[1,48,1536]{2,1,0:T(8,128)}, f32[1,48,1536]{2,1,0:T(8,128)}, u32[]{:S(2)}, u32[]{:S(2)}) collective-permute-start(f32[1,48,1536]{2,1,0:T(8,128)} %bitcast_add_fusion.4), channel_id=1, source_target_pairs={{0,16},{2,18},{4,20},{6,22},{8,24},{10,26},{12,28},{14,30},{16,0},... | collective-permute-start | bytes 884744 | tf_op jit(solution)/shard_map/ppermute | solution.py:59
  282.9 13.4 %collective-permute-start.42 = (f32[11,768]{1,0:T(8,128)S(1)}, f32[11,768]{1,0:T(8,128)S(1)}, u32[]{:S(2)}, u32[]{:S(2)}) collective-permute-start(f32[11,768]{1,0:T(8,128)S(1)} %add.548), channel_id=1, source_target_pairs={{0,16},{2,18},{4,20},{6,22},{8,24},{10,26},{12,28},{14,30},{16,0},... | collective-permute-start | bytes 101384 | tf_op jit(solution)/shard_map/ppermute | solution.py:59
  284.1 13.8 %collective-permute-start.41 = (f32[1,2,48,384]{3,2,1,0:T(8,128)S(1)}, f32[1,2,48,384]{3,2,1,0:T(8,128)S(1)}, u32[]{:S(2)}, u32[]{:S(2)}) collective-permute-start(f32[1,2,48,384]{3,2,1,0:T(8,128)S(1)} %bitcast_add_fusion.10), channel_id=1, source_target_pairs={{0,16},{2,18},{4,20},{6,22},{8,24},{10,26},{12,28},{14,30},{16,0},... | collective-permute-start | bytes 442376 | tf_op jit(solution)/shard_map/ppermute | solution.py:59
  288.2 11.3 %collective-permute-start.40 = (f32[1,2,48,384]{3,2,1,0:T(8,128)S(1)}, f32[1,2,48,384]{3,2,1,0:T(8,128)S(1)}, u32[]{:S(2)}, u32[]{:S(2)}) collective-permute-start(f32[1,2,48,384]{3,2,1,0:T(8,128)S(1)} %bitcast_add_fusion.11), channel_id=1, source_target_pairs={{0,16},{2,18},{4,20},{6,22},{8,24},{10,26},{12,28},{14,30},{16,0},... | collective-permute-start | bytes 442376 | tf_op jit(solution)/shard_map/ppermute | solution.py:59
  (42 other events, 159.8 us)
where the time goes:
time: 311 us; the launch traced here: 305 us
  Pallas kernels  105 us (34%)
  waiting for transfers between devices  93.8 us (30%)
  other arithmetic  43.5 us (14%)
  starting transfers between devices  39.2 us (13%)
  local copies, waits for them, and re-layouts  22.3 us (7%)
    pallas_call x1, Pallas kernels, feed(): pl.pallas_call(functools.partial(feed_kernel, orders, len(ups)), grid=(ti...  68.6 us
    ppermute x35, waiting for transfers between devices, traded(): lax.ppermute(values, 'items', [(i, i ^ step) for i in range(n_items)])  64.5 us
    ppermute x8, waiting for transfers between devices, swapped(): return lax.ppermute(values, 'heads', [(0, 1), (1, 0)])  29.3 us
    ppermute x35, starting transfers between devices, traded(): lax.ppermute(values, 'items', [(i, i ^ step) for i in range(n_items)])  28.6 us
    pallas_call x1, Pallas kernels, attend_back(): pl.pallas_call(functools.partial(attend_back_kernel, orders), grid=(pairs...  20.5 us
    unnamed x96, local copies, waits for them, and re-layouts  19.7 us
    add x8, other arithmetic, add(): self.send, self.terms = (sum(part(1 - mine)), part(mine))  14.5 us
    pallas_call x1, Pallas kernels, attend(): pl.pallas_call(attend_kernel, grid=(pairs,), in_specs=[whole(rows, width)...  13.3 us
  transfers between devices with their start and end apart: 43, of which 21 were waited for; matrix products, arithmetic and copies ran while one was open for 11% of the time, Pallas kernels for 12%

commit v1 on v0

--- a/solution.py
+++ b/solution.py
@@ -11,10 +11,9 @@
 CLUSTER = 128
 SCALE = HEAD_DIM**-0.5
 EPSILON = 1e-05
-ROW_TILE = 512
-LAG = 1
+ROW_TILE = 256
 GRAD_TILE = 512
-UNIT_TILE = 768
+UNIT_TILE = 1536
 BF16 = jnp.bfloat16
 F32 = jnp.float32
 
@@ -84,8 +83,20 @@
 
 class Halving:
     def __init__(self, keep, send, order, n_items):
-        self.terms, self.order, self.n_items = [keep], list(order), n_items
+        self.order, self.n_items, self.rest = list(order), n_items, keep.shape[1:]
+        self.terms = []
+        self.hold(keep)
         self.send, self.extra, self.bit = send, None, 0
+
+    def hold(self, values):
+        self.terms.append((values.reshape((2,) * len(self.order) + self.rest), []))
+
+    def part(self, term, places):
+        values, settled = term
+        starts = settled + places
+        sizes = (1,) * len(starts) + values.shape[len(starts) :]
+        starts = starts + [0] * (values.ndim - len(starts))
+        return lax.dynamic_slice(values, starts, sizes).reshape((-1,) + self.rest)
 
     def trade(self):
         self.got = traded(self.send, 1 << self.bit, self.n_items)
@@ -94,16 +105,15 @@
         return self
 
     def add(self):
-        terms = self.terms + [self.got]
+        self.hold(self.got)
         if self.extra is not None:
             self.extra = self.extra + self.more
         if not self.order:
-            return sum(term.reshape(term.shape[1:]) for term in terms)
+            return sum(self.part(term, []) for term in self.terms).reshape(self.rest)
         self.bit = self.order.pop(0)
         mine = (lax.axis_index("items") >> self.bit) & 1
-        terms = [v.reshape((2, v.shape[0] // 2) + v.shape[1:]) for v in terms]
-        part = lambda k: [lax.dynamic_index_in_dim(v, k, 0, keepdims=False) for v in terms]
-        self.send, self.terms = sum(part(1 - mine)), part(mine)
+        self.send = sum(self.part(term, [1 - mine]) for term in self.terms)
+        self.terms = [(values, settled + [mine]) for values, settled in self.terms]
         return self.send
 
 
@@ -378,137 +388,117 @@
 
 
 def feed_rows(
-    here, x_ref, cot_ref, ctx_ref, far_ctx_refs, vectors, ready, out_s, far_out_s, up_s, down_s, far_up_s, far_down_s,
-    mixed_ref, d_pre_ref, d_attn_ref, sums_ref, up_sums_ref, nb_s, act_s, d_feed_s, d_hidden_s, far_slope_s,
+    x_ref, cot_ref, ctx_ref, far_ctx_refs, vector_refs, ready, out_s, far_out_s, up_s, down_s, far_up_s, far_down_s,
+    mixed_ref, d_pre_ref, d_attn_ref, sums_ref, up_sums_ref, nb_s, act_s, d_feed_s, d_hidden_s, here,
 ):
     units = up_s.shape[1]
-    out_bias, gain1, bias1, down_bias, gain2, bias2, up_bias, far_bias = vectors
-    attention = dot_tn(ctx_ref[:, here], out_s[...])
-    far_ctx = jnp.concatenate([ref[:, here].astype(BF16) for ref in far_ctx_refs], axis=0)
+    row = lambda ref: ref[...].reshape(1, ref.shape[0])
+    out_bias, gain1, bias1, down_bias, gain2, bias2, up_bias, far_bias = map(row, vector_refs)
+    ready("out")
+    attention = dot_tn(ctx_ref[...], out_s[...])
+    far_ctx = jnp.concatenate([ref[...].astype(BF16) for ref in far_ctx_refs], axis=0)
     attention += dot_tn(far_ctx, far_out_s[...])
-    yield
-    unit1, factor1 = normalized(x_ref[here, :].astype(F32) + attention + out_bias)
+    unit1, factor1 = normalized(x_ref[...].astype(F32) + attention + out_bias)
     normed = unit1 * gain1 + bias1
     nb = normed.astype(BF16)
     nb_s[here, :] = nb
     total = normed + down_bias
-    yield
+    slopes, far_slopes = [], []
     ready("near")
     for cut in unit_cuts(units):
         active, slope = gelu_both(dot(nb, up_s[:, cut]) + up_bias[:, cut])
         act_s[here, cut] = active
-        d_hidden_s[here, cut] = slope
+        slopes.append(slope)
         total = total + dot(active, down_s[cut, :])
-        yield
     ready("far")
     for cut in unit_cuts(units):
         far_active, far_slope = gelu_both(dot(nb, far_up_s[:, cut]) + far_bias[:, cut])
-        far_slope_s[here, cut] = far_slope
+        far_slopes.append(far_slope)
         total = total + dot(far_active, far_down_s[cut, :])
-        yield
     unit2, factor2 = normalized(total)
-    mixed_ref[here, :] = (unit2 * gain2 + bias2).astype(BF16)
-    grad = cot_ref[here, :].astype(F32)
+    mixed_ref[...] = (unit2 * gain2 + bias2).astype(BF16)
+    grad = cot_ref[...].astype(F32)
     sums_ref[0:1, :] += jnp.sum(grad * unit2, axis=0, keepdims=True)
     sums_ref[1:2, :] += jnp.sum(grad, axis=0, keepdims=True)
     d_sum = norm_back(grad * gain2, unit2, factor2)
     d_feed = d_sum.astype(BF16)
     d_feed_s[here, :] = d_feed
     sums_ref[2:3, :] += jnp.sum(d_feed.astype(F32), axis=0, keepdims=True)
-    yield
     d_normed = d_sum
-    for cut in unit_cuts(units):
+    for cut, slope, far_slope in zip(unit_cuts(units), slopes, far_slopes):
         d_active = dot_nt(d_feed, down_s[cut, :])
-        d_hidden = (d_active * d_hidden_s[here, cut].astype(F32)).astype(BF16)
+        d_hidden = (d_active * slope.astype(F32)).astype(BF16)
         d_hidden_s[here, cut] = d_hidden
         up_sums_ref[:, cut] += jnp.sum(d_hidden.astype(F32), axis=0, keepdims=True)
+        far_d_active = dot_nt(d_feed, far_down_s[cut, :])
+        far_d_hidden = (far_d_active * far_slope.astype(F32)).astype(BF16)
         d_normed = d_normed + dot_nt(d_hidden, up_s[:, cut])
-        yield
-    for cut in unit_cuts(units):
-        far_d_active = dot_nt(d_feed, far_down_s[cut, :])
-        far_d_hidden = (far_d_active * far_slope_s[here, cut].astype(F32)).astype(BF16)
         d_normed = d_normed + dot_nt(far_d_hidden, far_up_s[:, cut])
-        yield
     sums_ref[3:4, :] += jnp.sum(d_normed * unit1, axis=0, keepdims=True)
     sums_ref[4:5, :] += jnp.sum(d_normed, axis=0, keepdims=True)
     d_pre = norm_back(d_normed * gain1, unit1, factor1)
-    d_pre_ref[here, :] = d_pre
+    d_pre_ref[...] = d_pre
     d_attn = d_pre.astype(BF16)
-    d_attn_ref[here, :] = d_attn
+    d_attn_ref[...] = d_attn
     sums_ref[5:6, :] += jnp.sum(d_attn.astype(F32), axis=0, keepdims=True)
 
 
-def in_turn(programs, lag):
-    waiting = [k * lag for k in range(len(programs))]
-    while any(wait is not None for wait in waiting):
-        for k, wait in enumerate(waiting):
-            if wait == 0:
-                if next(programs[k], "end") == "end":
-                    waiting[k] = None
-            elif wait is not None:
-                waiting[k] = wait - 1
-
-
-def feed_kernel(orders, late_count, core_ref, slots_ref, x_ref, cot_ref, ctx_ref, far0_ref, far1_ref, far2_ref, *refs):
+def feed_kernel(
+    orders, tiles, late_count, core_ref, slots_ref, x_ref, cot_ref, ctx_ref, far0_ref, far1_ref, far2_ref, *refs
+):
     vector_refs, refs = refs[:8], refs[8:]
     out_hbm, near_half_hbm, far_half_hbm, up_hbm, down_hbm, far_up_hbm, far_down_hbm, *refs = refs
     up_parts, down_parts, refs = refs[:late_count], refs[late_count : 2 * late_count], refs[2 * late_count :]
     mixed_ref, d_pre_ref, d_attn_ref, sums_ref, up_sums_ref, *refs = refs
     count = 4 if orders else 2
     grad_refs, refs = refs[:count], refs[count:]
-    nb_s, act_s, d_feed_s, d_hidden_s, far_slope_s, out_s, far_out_s, up_s, down_s, far_up_s, far_down_s, *refs = refs
+    nb_s, act_s, d_feed_s, d_hidden_s, out_s, far_out_s, up_s, down_s, far_up_s, far_down_s, *refs = refs
     half_stage, up_stage, down_stage, sems, up_sems, down_sems = refs
     step = pl.program_id(0)
-    rows = x_ref.shape[0]
-    tiles = 1
-
-    @pl.when(step == 0)
-    def _():
-        copies = [
-            pltpu.make_async_copy(source, target, sems.at[k])
-            for k, (source, target) in enumerate((
-                (out_hbm, out_s), (near_half_hbm, half_stage.at[0]), (far_half_hbm, half_stage.at[1]),
-                (up_hbm, up_s), (down_hbm, down_s), (far_up_hbm, far_up_s), (far_down_hbm, far_down_s),
-            ))
-        ]
-        places = [slots_ref[k] for k in range(late_count)]
-        start_up, finish_up = narrow_copies(up_parts, up_stage, up_sems, places, far_up_s)
-        start_down, finish_down = narrow_copies(down_parts, down_stage, down_sems, places, far_down_s)
-        for copy in copies:
-            copy.start()
-        start_up()
-        start_down()
-        sums_ref[...] = jnp.zeros_like(sums_ref)
-        up_sums_ref[...] = jnp.zeros_like(up_sums_ref)
-        for copy in copies[:3]:
-            copy.wait()
-        half = half_stage.shape[1]
-        for k in range(2):
-            place = pl.multiple_of((core_ref[0] ^ k) * half, half)
-            far_out_s[pl.ds(place, half), :] = half_stage[k].astype(BF16)
-        done = []
-
-        def ready(what):
-            if what in done:
-                return
-            done.append(what)
-            for copy in copies[3:5] if what == "near" else copies[5:]:
-                copy.wait()
-            if what == "far":
+    tile = x_ref.shape[0]
+    copies = [
+        pltpu.make_async_copy(source, target, sems.at[k])
+        for k, (source, target) in enumerate((
+            (out_hbm, out_s), (near_half_hbm, half_stage.at[0]), (far_half_hbm, half_stage.at[1]),
+            (up_hbm, up_s), (down_hbm, down_s), (far_up_hbm, far_up_s), (far_down_hbm, far_down_s),
+        ))
+    ]
+    places = [slots_ref[k] for k in range(late_count)]
+    start_up, finish_up = narrow_copies(up_parts, up_stage, up_sems, places, far_up_s)
+    start_down, finish_down = narrow_copies(down_parts, down_stage, down_sems, places, far_down_s)
+
+    def ready(what):
+        @pl.when(step == 0)
+        def _():
+            if what == "out":
+                for copy in copies:
+                    copy.start()
+                start_up()
+                start_down()
+                sums_ref[...] = jnp.zeros_like(sums_ref)
+                up_sums_ref[...] = jnp.zeros_like(up_sums_ref)
+                for copy in copies[:3]:
+                    copy.wait()
+                half = half_stage.shape[1]
+                for k in range(2):
+                    place = pl.multiple_of((core_ref[0] ^ k) * half, half)
+                    far_out_s[pl.ds(place, half), :] = half_stage[k].astype(BF16)
+            elif what == "near":
+                for copy in copies[3:5]:
+                    copy.wait()
+            else:
+                for copy in copies[5:]:
+                    copy.wait()
                 finish_up()
                 finish_down()
 
-        vectors = [ref[...].reshape(1, ref.shape[0]) for ref in vector_refs]
-        in_turn(
-            [
-                feed_rows(
-                    slice(r, r + ROW_TILE), x_ref, cot_ref, ctx_ref, (far0_ref, far1_ref, far2_ref), vectors, ready,
-                    out_s, far_out_s, up_s, down_s, far_up_s, far_down_s, mixed_ref, d_pre_ref, d_attn_ref, sums_ref,
-                    up_sums_ref, nb_s, act_s, d_feed_s, d_hidden_s, far_slope_s,
-                )
-                for r in range(0, rows, ROW_TILE)
-            ],
-            LAG,
+    @pl.when(step < tiles)
+    def _():
+        here = pl.ds(pl.multiple_of(step * tile, tile), tile)
+        feed_rows(
+            x_ref, cot_ref, ctx_ref, (far0_ref, far1_ref, far2_ref), vector_refs, ready, out_s, far_out_s, up_s,
+            down_s, far_up_s, far_down_s, mixed_ref, d_pre_ref, d_attn_ref, sums_ref, up_sums_ref, nb_s, act_s,
+            d_feed_s, d_hidden_s, here,
         )
 
     @pl.when(step >= tiles)
@@ -530,7 +520,10 @@
 ):
     rows, width = x.shape
     local, units = out_weight.shape[0], up.shape[1]
-    tiles = 1
+    tile = ROW_TILE
+    tiles = rows // tile
+    across = lambda cols: pl.BlockSpec((tile, cols), lambda i: (jnp.minimum(i, tiles - 1), 0))
+    along = lambda height: pl.BlockSpec((height, tile), lambda i: (0, jnp.minimum(i, tiles - 1)))
     if orders:
         blocks = 2 ** len(orders[0])
         height = width // (2 * blocks)
@@ -545,15 +538,15 @@
     anywhere = pl.BlockSpec(memory_space=pl.ANY)
     depth = len(ups)
     return pl.pallas_call(
-        functools.partial(feed_kernel, orders, len(ups)),
+        functools.partial(feed_kernel, orders, tiles, len(ups)),
         grid=(tiles + units // GRAD_TILE,),
         in_specs=[
-            scalars, scalars, whole(rows, width), whole(rows, width), whole(local, rows),
-            *[whole(*part.shape) for part in far_context], *[whole(v.shape[0]) for v in vectors],
+            scalars, scalars, across(width), across(width), along(local),
+            *[along(part.shape[0]) for part in far_context], *[whole(v.shape[0]) for v in vectors],
             *[anywhere] * (7 + len(ups) + len(downs)),
         ],
         out_specs=[
-            whole(rows, width), whole(rows, width), whole(rows, width), whole(8, width), whole(1, units),
+            across(width), across(width), across(width), whole(8, width), whole(1, units),
             *grad_specs,
         ],
         out_shape=[
@@ -562,7 +555,7 @@
         ],
         scratch_shapes=[
             pltpu.VMEM((rows, width), BF16), pltpu.VMEM((rows, units), BF16), pltpu.VMEM((rows, width), BF16),
-            pltpu.VMEM((rows, units), BF16), pltpu.VMEM((rows, units), BF16),
+            pltpu.VMEM((rows, units), BF16),
             pltpu.VMEM((local, width), BF16), pltpu.VMEM((local, width), BF16),
             pltpu.VMEM((width, units), BF16), pltpu.VMEM((units, width), BF16),
             pltpu.VMEM((width, units), BF16), pltpu.VMEM((units, width), BF16),
@@ -570,7 +563,7 @@
             pltpu.VMEM((depth,) + downs[0].shape[1:], F32), pltpu.SemaphoreType.DMA((7,)),
             pltpu.SemaphoreType.DMA((depth,)), pltpu.SemaphoreType.DMA((depth,)),
         ],
-        compiler_params=params_of(60),
+        compiler_params=params_of(56),
         cost_estimate=cost(25e9, 30e6),
         name="feed",
     )(

time: 311 us -> 284 us (0.913); the launches traced: 305 us -> 283 us
  Pallas kernels: 105 us -> 80.7 us
    pallas_call x1, Pallas kernels: 68.6 us -> 44.2 us  [feed(): pl.pallas_call(functools.partial(feed_kernel, orders, tiles, len(ups)), g...]
    dynamic_slice x3 -> x0, other arithmetic: 12.1 us -> none  [add(): lax.dynamic_index_in_dim(v, k, 0, keepdims=False)]
    add x12 -> x14, other arithmetic: 21.3 us -> 26.8 us  [the longest x12 24.3 us: add(): self.send = sum((self.part(term, [1 - mine]) for term in self.terms))]
    ppermute x35, waiting for transfers between devices: 64.5 us -> 67.8 us  [traded(): lax.ppermute(values, 'items', [(i, i ^ step) for i in range(n_items)])]
    unnamed x96 -> x90, local copies, waits for them, and re-layouts: 19.7 us -> 22.8 us
  transfers between devices with their start and end apart: 43 -> 43, of which waited for: 21 -> 21; matrix products, arithmetic and copies ran while one was open for 11% -> 12% of each run, Pallas kernels for 12% -> 13%
where the time goes in v1:
time: 284 us; the launch traced here: 283 us
  waiting for transfers between devices  96.9 us (34%)
  Pallas kernels  80.7 us (28%)
  other arithmetic  40.6 us (14%)
  starting transfers between devices  38 us (13%)
  local copies, waits for them, and re-layouts  25.4 us (9%)
    ppermute x35, waiting for transfers between devices, traded(): lax.ppermute(values, 'items', [(i, i ^ step) for i in range(n_items)])  67.8 us
    pallas_call x1, Pallas kernels, feed(): pl.pallas_call(functools.partial(feed_kernel, orders, tiles, len(ups)), g...  44.2 us
    ppermute x8, waiting for transfers between devices, swapped(): return lax.ppermute(values, 'heads', [(0, 1), (1, 0)])  29.1 us
    ppermute x35, starting transfers between devices, traded(): lax.ppermute(values, 'items', [(i, i ^ step) for i in range(n_items)])  27.4 us
    add x12, other arithmetic, add(): self.send = sum((self.part(term, [1 - mine]) for term in self.terms))  24.3 us
    unnamed x90, local copies, waits for them, and re-layouts  22.8 us
    pallas_call x1, Pallas kernels, attend_back(): pl.pallas_call(functools.partial(attend_back_kernel, orders), grid=(pairs...  20.3 us
    pallas_call x1, Pallas kernels, attend(): pl.pallas_call(attend_kernel, grid=(pairs,), in_specs=[whole(rows, width)...  13.3 us
  transfers between devices with their start and end apart: 43, of which 21 were waited for; matrix products, arithmetic and copies ran while one was open for 12% of the time, Pallas kernels for 13%

profile of v1, /device:TPU:0, one launch (start us, length us, event | category | flops | bytes accessed | tf_op | source)
XLA Modules:
  0.0 282.6 jit_solution(15800349342772497980)
XLA Ops:
  0.7 1.9 bitcast_convert_fusion.1
  2.6 2.9 %collective-permute-start = (f32[1,96,1536]{2,1,0:T(8,128)}, f32[1,96,1536]{2,1,0:T(8,128)S(1)}, u32[]{:S(2)}, u32[]{:S(2)}) collective-permute-start(f32[1,96,1536]{2,1,0:T(8,128)} %bitcast_convert_fusion.1), channel_id=1, source_target_pairs={{0,1},{1,0},{2,3},{3,2},{4,5},{5,4},{6,7},{7,6},{8,9},{9,8},{10,11... | collective-permute-start | bytes 1769480 | tf_op jit(solution)/shard_map/ppermute | solution.py:54
  5.6 1.8 bitcast_convert_fusion
  9.1 13.3 %attend.1 = (bf16[384,1024]{1,0:T(8,128)(2,1)S(1)}, bf16[6,192,1024]{2,1,0:T(8,128)(2,1)S(1)}, bf16[6,1024,128]{2,1,0:T(8,128)(2,1)S(1)}) custom-call(bf16[1024,768]{1,0:T(8,128)(2,1)S(1)} %copy-done, bf16[3,768,384]{2,1,0:T(8,128)(2,1)S(1)} %copy-done.4, f32[384,2]{1,0:T(8,128)S(1)} %bitcast.135, s32[3,2,1024]{2,1,0:T(2,128)S(1)} %reshape_squeeze.3.row_ref), custom_call_target="tpu_custom_call" | custom-call | flops 12000000 | bytes 12000 | tf_op jit(solution)/shard_map/attend/pallas_call | solution.py:177
  26.2 2.0 collective-permute-start.7
  28.4 2.1 collective-permute-start.6
  30.4 2.3 collective-permute-done.3.refs_6_
  32.7 2.1 collective-permute-start.4
  34.8 1.5 collective-permute-start.5
  36.4 7.6 %collective-permute-done.8.refs_7_ = f32[1536]{0:T(1024)S(1)} collective-permute-done((f32[1536]{0:T(1024)S(1)}, f32[1536]{0:T(1024)S(1)}, u32[]{:S(2)}, u32[]{:S(2)}) %collective-permute-start.8) | collective-permute-done | bytes 6176 | tf_op jit(solution)/shard_map/ppermute | solution.py:54
  44.0 2.1 collective-permute-start.1
  46.1 1.5 collective-permute-start.2
  47.7 8.1 %collective-permute-done.6.refs_9_ = f32[192,768]{1,0:T(8,128)S(1)} collective-permute-done((f32[192,768]{1,0:T(8,128)S(1)}, f32[192,768]{1,0:T(8,128)S(1)}, u32[]{:S(2)}, u32[]{:S(2)}) %collective-permute-start.6) | collective-permute-done | bytes 589856 | tf_op jit(solution)/shard_map/ppermute | solution.py:54
  55.8 3.4 %collective-permute-done.1.refs_1_ = f32[1,96,1536]{2,1,0:T(8,128)S(1)} collective-permute-done((f32[1,96,1536]{2,1,0:T(8,128)S(1)}, f32[1,96,1536]{2,1,0:T(8,128)S(1)}, u32[]{:S(2)}, u32[]{:S(2)}) %collective-permute-start.1) | collective-permute-done | bytes 589856 | tf_op jit(solution)/shard_map/ppermute | solution.py:58
  61.5 1.8 collective-permute-done.18.refs_11_
  65.1 1.5 collective-permute-start.10
  68.7 1.5 collective-permute-start.11
  77.0 2.9 %placed.1 = (bf16[768,1536]{1,0:T(8,128)(2,1)S(1)}, bf16[1536,768]{1,0:T(8,128)(2,1)S(1)}) custom-call(s32[6]{0:T(128)S(1)} %stack.42.slots_ref, f32[1,96,1536]{2,1,0:T(8,128)S(1)} %collective-permute-done.refs_0_, f32[1,96,1536]{2,1,0:T(8,128)S(1)} %collective-permute-done.1.refs_1_, f32[1,96,1536]{2,1,0:T(8,128)S(1)} %collective-permute-done.2.refs_2_, ...), custom_call_target="tpu_custom_call" | custom-call | flops 1000 | bytes 1000 | tf_op jit(solution)/shard_map/placed/pallas_call | solution.py:374
  83.9 10.0 %collective-permute-done.12.far2_ref = f32[128,1024]{1,0:T(8,128)} collective-permute-done((f32[128,1024]{1,0:T(8,128)}, f32[128,1024]{1,0:T(8,128)}, u32[]{:S(2)}, u32[]{:S(2)}) %collective-permute-start.12) | collective-permute-done | bytes 524320 | tf_op jit(solution)/shard_map/ppermute | solution.py:54
  97.8 44.2 %feed.1 = (bf16[1024,768]{1,0:T(8,128)(2,1)}, f32[1024,768]{1,0:T(8,128)}, bf16[1024,768]{1,0:T(8,128)(2,1)}, f32[8,768]{1,0:T(8,128)}, f32[1,1536]{1,0:T(1,128)...) custom-call(s32[1]{0:T(128)} %bitcast.core_ref, ...), custom_call_target="tpu_custom_call" | custom-call | flops 25000000 | bytes 30000 | tf_op jit(solution)/shard_map/feed/pallas_call | solution.py:540
  142.6 6.4 %collective-permute-done.22 = f32[8,48,1536]{2,1,0:T(8,128)S(1)} collective-permute-done((f32[8,48,1536]{2,1,0:T(8,128)}, f32[8,48,1536]{2,1,0:T(8,128)S(1)}, u32[]{:S(2)}, u32[]{:S(2)}) %collective-permute-start.22) | collective-permute-done | bytes 2359328 | tf_op jit(solution)/shard_map/ppermute | solution.py:58
  150.3 3.0 %dynamic-slice_add_fusion = f32[1,2,2,48,1536]{4,3,2,1,0:T(8,128)} fusion(f32[2,2,2,48,1536]{4,3,2,1,0:T(8,128)} %bitcast.18, s32[]{:T(128)S(6)} %select_n.30, f32[2,2,2,48,1536]{4,3,2,1,0:T(8,128)} %bitcast.141), kind=kLoop, calls=%fused_computation.1 | loop fusion | flops 294912 | bytes 3538948 | tf_op jit(solution)/shard_map/add | solution.py:115
  153.9 2.6 dynamic-slice_add_fusion.1
  160.8 20.3 %attend_back.1 = (f32[1024,768]{1,0:T(8,128)S(1)}, f32[2,384]{1,0:T(2,128)S(1)}, f32[8,2,48,384]{3,2,1,0:T(8,128)S(1)}, f32[8,2,48,384]{3,2,1,0:T(8,128)}, f32[8...) custom-call(s32[1]{0:T(128)} %bitcast.core_ref, bf16[1024,768]{1,0:T(8,128)(2,1)S(1)} %copy-done.1, ...), custom_call_target="tpu_custom_call" | custom-call | flops 20000000 | bytes 20000 | tf_op jit(solution)/shard_map/attend_back/pallas_call | solution.py:282
  183.8 2.3 collective-permute-done.33
  188.2 2.3 bitcast_add_fusion
  190.5 1.5 collective-permute-start.28
  192.0 2.4 bitcast_add_fusion.1
  194.5 1.9 dynamic-slice_add_fusion.2
  196.4 1.6 collective-permute-start.32
  198.0 1.9 dynamic-slice_add_fusion.3
  200.9 12.1 %collective-permute-done.32 = f32[4,2,48,384]{3,2,1,0:T(8,128)} collective-permute-done((f32[4,2,48,384]{3,2,1,0:T(8,128)}, f32[4,2,48,384]{3,2,1,0:T(8,128)}, u32[]{:S(2)}, u32[]{:S(2)}) %collective-permute-start.32) | collective-permute-done | bytes 589856 | tf_op jit(solution)/shard_map/ppermute | solution.py:58
  213.0 5.2 %collective-permute-done.31 = f32[4,2,48,384]{3,2,1,0:T(8,128)} collective-permute-done((f32[4,2,48,384]{3,2,1,0:T(8,128)}, f32[4,2,48,384]{3,2,1,0:T(8,128)}, u32[]{:S(2)}, u32[]{:S(2)}) %collective-permute-start.31) | collective-permute-done | bytes 589856 | tf_op jit(solution)/shard_map/ppermute | solution.py:58
  218.3 5.7 %collective-permute-done.27 = f32[2,48,1536]{2,1,0:T(8,128)} collective-permute-done((f32[2,48,1536]{2,1,0:T(8,128)}, f32[2,48,1536]{2,1,0:T(8,128)}, u32[]{:S(2)}, u32[]{:S(2)}) %collective-permute-start.27) | collective-permute-done | bytes 589856 | tf_op jit(solution)/shard_map/ppermute | solution.py:58
  223.9 1.6 collective-permute-start.39
  225.5 1.9 bitcast_add_fusion.3
  228.0 1.9 bitcast_add_fusion.4
  230.3 2.0 fusion.3
  232.3 2.6 collective-permute-start.36
  234.9 2.0 fusion.4
  237.9 4.3 %collective-permute-done.37 = f32[2,2,48,384]{3,2,1,0:T(8,128)} collective-permute-done((f32[2,2,48,384]{3,2,1,0:T(8,128)}, f32[2,2,48,384]{3,2,1,0:T(8,128)}, u32[]{:S(2)}, u32[]{:S(2)}) %collective-permute-start.37) | collective-permute-done | bytes 294944 | tf_op jit(solution)/shard_map/ppermute | solution.py:58
  242.2 13.3 %collective-permute-done.36 = f32[1,48,1536]{2,1,0:T(8,128)} collective-permute-done((f32[1,48,1536]{2,1,0:T(8,128)}, f32[1,48,1536]{2,1,0:T(8,128)}, u32[]{:S(2)}, u32[]{:S(2)}) %collective-permute-start.36) | collective-permute-done | bytes 294944 | tf_op jit(solution)/shard_map/ppermute | solution.py:58
  255.5 3.5 %collective-permute-done.35 = f32[1,48,1536]{2,1,0:T(8,128)} collective-permute-done((f32[1,48,1536]{2,1,0:T(8,128)}, f32[1,48,1536]{2,1,0:T(8,128)}, u32[]{:S(2)}, u32[]{:S(2)}) %collective-permute-start.35) | collective-permute-done | bytes 294944 | tf_op jit(solution)/shard_map/ppermute | solution.py:58
  260.9 3.0 %collective-permute-start.41 = (f32[1,2,48,384]{3,2,1,0:T(8,128)S(1)}, f32[1,2,48,384]{3,2,1,0:T(8,128)S(1)}, u32[]{:S(2)}, u32[]{:S(2)}) collective-permute-start(f32[1,2,48,384]{3,2,1,0:T(8,128)S(1)} %fusion.12), channel_id=1, source_target_pairs={{0,16},{2,18},{4,20},{6,22},{8,24},{10,26},{12,28},{14,30},{16,0},... | collective-permute-start | bytes 442376 | tf_op jit(solution)/shard_map/ppermute | solution.py:58
  265.2 2.9 %fusion.2 = (f32[48,1536]{1,0:T(8,128)}, f32[1536,48]{0,1:T(8,128)}) fusion(f32[1,48,1536]{2,1,0:T(8,128)} %collective-permute-done.36, f32[2,48,1536]{2,1,0:T(8,128)} %collective-permute-done.28, s32[]{:T(128)S(6)} %select_n.33, f32[2,2,48,1536]{3,2,1,0:T(8,128)} %bitcast.26, s32[]{:T(128)S(6)} %select_n.31, f32[2,2,2,48,1536]{4,3,2,1,0:T(8,128)} %bitcast.18, ...), kind=kLoop, calls=%fused_computation.10 | loop fusion | flops 589824 | bytes 3538956 | tf_op jit(solution)/shard_map/reshape | solution.py:112
  268.1 3.7 %add_convert_fusion = bf16[1024,768]{1,0:T(8,128)(2,1)} fusion(f32[1024,768]{1,0:T(8,128)} %collective-permute-done.24, f32[1024,768]{1,0:T(8,128)S(1)} %copy-done.29, f32[1024,768]{1,0:T(8,128)S(1)} %get-tuple-element.118), kind=kLoop, calls=%fused_computation | loop fusion | flops 2359296 | bytes 11010048 | tf_op jit(solution)/shard_map/convert_element_type | solution.py:692
  271.8 3.6 %collective-permute-done.41 = f32[1,2,48,384]{3,2,1,0:T(8,128)S(1)} collective-permute-done((f32[1,2,48,384]{3,2,1,0:T(8,128)S(1)}, f32[1,2,48,384]{3,2,1,0:T(8,128)S(1)}, u32[]{:S(2)}, u32[]{:S(2)}) %collective-permute-start.41) | collective-permute-done | bytes 147488 | tf_op jit(solution)/shard_map/ppermute | solution.py:58
  275.4 1.6 collective-permute-done.40
  (170 shorter events, 49.5 us)
Async XLA Ops:
  2.6 27.8 %collective-permute-start = (f32[1,96,1536]{2,1,0:T(8,128)}, f32[1,96,1536]{2,1,0:T(8,128)S(1)}, u32[]{:S(2)}, u32[]{:S(2)}) collective-permute-start(f32[1,96,1536]{2,1,0:T(8,128)} %bitcast_convert_fusion.1), channel_id=1, source_target_pairs={{0,1},{1,0},{2,3},{3,2},{4,5},{5,4},{6,7},{7,6},{8,9},{9,8},{10,11... | collective-permute-start | bytes 1769480 | tf_op jit(solution)/shard_map/ppermute | solution.py:54
  7.4 25.3 %collective-permute-start.3 = (f32[1,192,768]{2,1,0:T(8,128)}, f32[1,192,768]{2,1,0:T(8,128)}, u32[]{:S(2)}, u32[]{:S(2)}) collective-permute-start(f32[1,192,768]{2,1,0:T(8,128)} %bitcast_convert_fusion), channel_id=1, source_target_pairs={{0,1},{1,0},{2,3},{3,2},{4,5},{5,4},{6,7},{7,6},{8,9},{9,8},{10,11... | collective-permute-start | bytes 1769480 | tf_op jit(solution)/shard_map/ppermute | solution.py:54
  26.2 19.9 %collective-permute-start.7 = (f32[128,1024]{1,0:T(8,128)}, f32[128,1024]{1,0:T(8,128)S(1)}, u32[]{:S(2)}, u32[]{:S(2)}) collective-permute-start(f32[128,1024]{1,0:T(8,128)} %get-tuple-element.153), channel_id=1, source_target_pairs={{0,1},{1,0},{2,3},{3,2},{4,5},{5,4},{6,7},{7,6},{8,9},{9,8},{10,11... | collective-permute-start | bytes 1572872 | tf_op jit(solution)/shard_map/ppermute | solution.py:54
  28.3 15.7 %collective-permute-start.8 = (f32[1536]{0:T(1024)S(1)}, f32[1536]{0:T(1024)S(1)}, u32[]{:S(2)}, u32[]{:S(2)}) collective-permute-start(f32[1536]{0:T(1024)S(1)} %copy-done.40), channel_id=1, source_target_pairs={{0,1},{1,0},{2,3},{3,2},{4,5},{5,4},{6,7},{7,6},{8,9},{9,8},{10,11... | collective-permute-start | bytes 18440 | tf_op jit(solution)/shard_map/ppermute | solution.py:54
  28.4 27.4 %collective-permute-start.6 = (f32[192,768]{1,0:T(8,128)S(1)}, f32[192,768]{1,0:T(8,128)S(1)}, u32[]{:S(2)}, u32[]{:S(2)}) collective-permute-start(f32[192,768]{1,0:T(8,128)S(1)} %dynamic-slice_convert_fusion), channel_id=1, source_target_pairs={{0,1},{1,0},{2,3},{3,2},{4,5},{5,4},{6,7},{7,6},{8,9},{9,8},{10,11... | collective-permute-start | bytes 1769480 | tf_op jit(solution)/shard_map/ppermute | solution.py:54
  32.7 23.1 %collective-permute-start.4 = (f32[1,192,768]{2,1,0:T(8,128)}, f32[1,192,768]{2,1,0:T(8,128)S(1)}, u32[]{:S(2)}, u32[]{:S(2)}) collective-permute-start(f32[1,192,768]{2,1,0:T(8,128)} %collective-permute-done.3.refs_6_), channel_id=1, source_target_pairs={{0,8},{2,10},{4,12},{6,14},{8,0},{10,2},{12,4},{14,6},{16,24},{18,... | collective-permute-start | bytes 1769480 | tf_op jit(solution)/shard_map/ppermute | solution.py:58
  34.8 21.0 %collective-permute-start.5 = (f32[1,192,768]{2,1,0:T(8,128)}, f32[1,192,768]{2,1,0:T(8,128)S(1)}, u32[]{:S(2)}, u32[]{:S(2)}) collective-permute-start(f32[1,192,768]{2,1,0:T(8,128)} %collective-permute-done.3.refs_6_), channel_id=1, source_target_pairs={{0,4},{2,6},{4,0},{6,2},{8,12},{10,14},{12,8},{14,10},{16,20},{18,... | collective-permute-start | bytes 1769480 | tf_op jit(solution)/shard_map/ppermute | solution.py:58
  44.0 53.0 %copy-start.41 = (f32[1536]{0:T(1024)}, f32[1536]{0:T(1024)S(1)}, u32[]{:S(2)}) copy-start(f32[1536]{0:T(1024)S(1)} %collective-permute-done.8.refs_7_) | copy-start | bytes 18436
  44.0 15.2 %collective-permute-start.1 = (f32[1,96,1536]{2,1,0:T(8,128)S(1)}, f32[1,96,1536]{2,1,0:T(8,128)S(1)}, u32[]{:S(2)}, u32[]{:S(2)}) collective-permute-start(f32[1,96,1536]{2,1,0:T(8,128)S(1)} %collective-permute-done.refs_0_), channel_id=1, source_target_pairs={{0,8},{2,10},{4,12},{6,14},{8,0},{10,2},{12,4},{14,6},{16,24},{18,... | collective-permute-start | bytes 1769480 | tf_op jit(solution)/shard_map/ppermute | solution.py:58
  46.1 50.8 %copy-start.34 = (f32[128,1024]{1,0:T(8,128)}, f32[128,1024]{1,0:T(8,128)S(1)}, u32[]{:S(2)}) copy-start(f32[128,1024]{1,0:T(8,128)S(1)} %collective-permute-done.7.far0_ref) | copy-start | bytes 1572868
  46.1 14.3 %collective-permute-start.2 = (f32[1,96,1536]{2,1,0:T(8,128)S(1)}, f32[1,96,1536]{2,1,0:T(8,128)S(1)}, u32[]{:S(2)}, u32[]{:S(2)}) collective-permute-start(f32[1,96,1536]{2,1,0:T(8,128)S(1)} %collective-permute-done.refs_0_), channel_id=1, source_target_pairs={{0,4},{2,6},{4,0},{6,2},{8,12},{10,14},{12,8},{14,10},{16,20},{18,... | collective-permute-start | bytes 1769480 | tf_op jit(solution)/shard_map/ppermute | solution.py:58
  60.5 2.8 collective-permute-start.18
  60.5 3.8 %collective-permute-start.16 = (f32[1,192,768]{2,1,0:T(8,128)}, f32[1,192,768]{2,1,0:T(8,128)S(1)}, u32[]{:S(2)}, u32[]{:S(2)}) collective-permute-start(f32[1,192,768]{2,1,0:T(8,128)} %collective-permute-done.3.refs_6_), channel_id=1, source_target_pairs={{0,2},{2,0},{4,6},{6,4},{8,10},{10,8},{12,14},{14,12},{16,18},{18,... | collective-permute-start | bytes 1769480 | tf_op jit(solution)/shard_map/ppermute | solution.py:58
  61.0 5.6 %collective-permute-start.15 = (f32[1,96,1536]{2,1,0:T(8,128)S(1)}, f32[1,96,1536]{2,1,0:T(8,128)S(1)}, u32[]{:S(2)}, u32[]{:S(2)}) collective-permute-start(f32[1,96,1536]{2,1,0:T(8,128)S(1)} %collective-permute-done.2.refs_2_), channel_id=1, source_target_pairs={{0,2},{2,0},{4,6},{6,4},{8,10},{10,8},{12,14},{14,12},{16,18},{18,... | collective-permute-start | bytes 1769480 | tf_op jit(solution)/shard_map/ppermute | solution.py:58
  61.0 6.9 %collective-permute-start.14 = (f32[1,96,1536]{2,1,0:T(8,128)S(1)}, f32[1,96,1536]{2,1,0:T(8,128)S(1)}, u32[]{:S(2)}, u32[]{:S(2)}) collective-permute-start(f32[1,96,1536]{2,1,0:T(8,128)S(1)} %collective-permute-done.1.refs_1_), channel_id=1, source_target_pairs={{0,2},{2,0},{4,6},{6,4},{8,10},{10,8},{12,14},{14,12},{16,18},{18,... | collective-permute-start | bytes 1769480 | tf_op jit(solution)/shard_map/ppermute | solution.py:58
  61.5 8.8 %collective-permute-start.13 = (f32[1,96,1536]{2,1,0:T(8,128)S(1)}, f32[1,96,1536]{2,1,0:T(8,128)S(1)}, u32[]{:S(2)}, u32[]{:S(2)}) collective-permute-start(f32[1,96,1536]{2,1,0:T(8,128)S(1)} %collective-permute-done.refs_0_), channel_id=1, source_target_pairs={{0,2},{2,0},{4,6},{6,4},{8,10},{10,8},{12,14},{14,12},{16,18},{18,... | collective-permute-start | bytes 1769480 | tf_op jit(solution)/shard_map/ppermute | solution.py:58
  64.1 7.6 %collective-permute-start.17 = (f32[1,192,768]{2,1,0:T(8,128)S(1)}, f32[1,192,768]{2,1,0:T(8,128)}, u32[]{:S(2)}, u32[]{:S(2)}) collective-permute-start(f32[1,192,768]{2,1,0:T(8,128)S(1)} %collective-permute-done.4.refs_7_), channel_id=1, source_target_pairs={{0,2},{2,0},{4,6},{6,4},{8,10},{10,8},{12,14},{14,12},{16,18},{18,... | collective-permute-start | bytes 1769480 | tf_op jit(solution)/shard_map/ppermute | solution.py:58
  65.1 28.9 %collective-permute-start.10 = (f32[1,192,768]{2,1,0:T(8,128)S(1)}, f32[1,192,768]{2,1,0:T(8,128)}, u32[]{:S(2)}, u32[]{:S(2)}) collective-permute-start(f32[1,192,768]{2,1,0:T(8,128)S(1)} %collective-permute-done.4.refs_7_), channel_id=1, source_target_pairs={{0,4},{2,6},{4,0},{6,2},{8,12},{10,14},{12,8},{14,10},{16,20},{18,... | collective-permute-start | bytes 1769480 | tf_op jit(solution)/shard_map/ppermute | solution.py:58
  67.4 26.5 %collective-permute-start.9 = (f32[1,96,1536]{2,1,0:T(8,128)S(1)}, f32[1,96,1536]{2,1,0:T(8,128)}, u32[]{:S(2)}, u32[]{:S(2)}) collective-permute-start(f32[1,96,1536]{2,1,0:T(8,128)S(1)} %collective-permute-done.1.refs_1_), channel_id=1, source_target_pairs={{0,4},{2,6},{4,0},{6,2},{8,12},{10,14},{12,8},{14,10},{16,20},{18,... | collective-permute-start | bytes 1769480 | tf_op jit(solution)/shard_map/ppermute | solution.py:58
  68.7 15.1 %collective-permute-start.11 = (f32[128,1024]{1,0:T(8,128)}, f32[128,1024]{1,0:T(8,128)}, u32[]{:S(2)}, u32[]{:S(2)}) collective-permute-start(f32[128,1024]{1,0:T(8,128)} %get-tuple-element.152), channel_id=1, source_target_pairs={{0,1},{1,0},{2,3},{3,2},{4,5},{5,4},{6,7},{7,6},{8,9},{9,8},{10,11... | collective-permute-start | bytes 1572872 | tf_op jit(solution)/shard_map/ppermute | solution.py:54
  71.0 22.9 %collective-permute-start.12 = (f32[128,1024]{1,0:T(8,128)}, f32[128,1024]{1,0:T(8,128)}, u32[]{:S(2)}, u32[]{:S(2)}) collective-permute-start(f32[128,1024]{1,0:T(8,128)} %get-tuple-element.151), channel_id=1, source_target_pairs={{0,1},{1,0},{2,3},{3,2},{4,5},{5,4},{6,7},{7,6},{8,9},{9,8},{10,11... | collective-permute-start | bytes 1572872 | tf_op jit(solution)/shard_map/ppermute | solution.py:54
  71.7 23.4 %collective-permute-start.19 = (f32[192,768]{1,0:T(8,128)}, f32[192,768]{1,0:T(8,128)}, u32[]{:S(2)}, u32[]{:S(2)}) collective-permute-start(f32[192,768]{1,0:T(8,128)} %copy-done.31), channel_id=1, source_target_pairs={{0,2},{2,0},{4,6},{6,4},{8,10},{10,8},{12,14},{14,12},{16,18},{18,... | collective-permute-start | bytes 1769480 | tf_op jit(solution)/shard_map/ppermute | solution.py:58
  93.9 2.2 collective-permute-start.20
  93.9 3.1 %collective-permute-start.21 = (f32[1,192,768]{2,1,0:T(8,128)}, f32[1,192,768]{2,1,0:T(8,128)S(1)}, u32[]{:S(2)}, u32[]{:S(2)}) collective-permute-start(f32[1,192,768]{2,1,0:T(8,128)} %collective-permute-done.10.refs_17_), channel_id=1, source_target_pairs={{0,2},{2,0},{4,6},{6,4},{8,10},{10,8},{12,14},{14,12},{16,18},{18,... | collective-permute-start | bytes 1769480 | tf_op jit(solution)/shard_map/ppermute | solution.py:58
  142.0 7.0 %collective-permute-start.22 = (f32[8,48,1536]{2,1,0:T(8,128)}, f32[8,48,1536]{2,1,0:T(8,128)S(1)}, u32[]{:S(2)}, u32[]{:S(2)}) collective-permute-start(f32[8,48,1536]{2,1,0:T(8,128)} %get-tuple-element.110), channel_id=1, source_target_pairs={{0,2},{2,0},{4,6},{6,4},{8,10},{10,8},{12,14},{14,12},{16,18},{18,... | collective-permute-start | bytes 7077896 | tf_op jit(solution)/shard_map/ppermute | solution.py:58
  142.2 8.1 %collective-permute-start.23 = (f32[8,48,1536]{2,1,0:T(8,128)}, f32[8,48,1536]{2,1,0:T(8,128)}, u32[]{:S(2)}, u32[]{:S(2)}) collective-permute-start(f32[8,48,1536]{2,1,0:T(8,128)} %get-tuple-element.111), channel_id=1, source_target_pairs={{0,2},{2,0},{4,6},{6,4},{8,10},{10,8},{12,14},{14,12},{16,18},{18,... | collective-permute-start | bytes 7077896 | tf_op jit(solution)/shard_map/ppermute | solution.py:58
  150.3 7.6 %copy-start.11 = (bf16[6,192,1024]{2,1,0:T(8,128)(2,1)S(1)}, bf16[6,192,1024]{2,1,0:T(8,128)(2,1)}, u32[]{:S(2)}) copy-start(bf16[6,192,1024]{2,1,0:T(8,128)(2,1)} %copy-done.10) | copy-start | bytes 7077892
  153.3 34.3 %collective-permute-start.26 = (f32[4,48,1536]{2,1,0:T(8,128)}, f32[4,48,1536]{2,1,0:T(8,128)}, u32[]{:S(2)}, u32[]{:S(2)}) collective-permute-start(f32[4,48,1536]{2,1,0:T(8,128)} %bitcast.19), channel_id=1, source_target_pairs={{0,8},{2,10},{4,12},{6,14},{8,0},{10,2},{12,4},{14,6},{16,24},{18,... | collective-permute-start | bytes 3538952 | tf_op jit(solution)/shard_map/ppermute | solution.py:58
  156.5 31.7 %collective-permute-start.25 = (f32[4,48,1536]{2,1,0:T(8,128)}, f32[4,48,1536]{2,1,0:T(8,128)}, u32[]{:S(2)}, u32[]{:S(2)}) collective-permute-start(f32[4,48,1536]{2,1,0:T(8,128)} %bitcast.16), channel_id=1, source_target_pairs={{0,4},{2,6},{4,0},{6,2},{8,12},{10,14},{12,8},{14,10},{16,20},{18,... | collective-permute-start | bytes 3538952 | tf_op jit(solution)/shard_map/ppermute | solution.py:58
  160.8 22.8 %copy-start.42 = (f32[1,1536]{1,0:T(1,128)S(1)}, f32[1,1536]{1,0:T(1,128)}, u32[]{:S(2)}) copy-start(f32[1,1536]{1,0:T(1,128)} %get-tuple-element.128) | copy-start | bytes 18436
  160.8 22.9 %copy-start.37 = (f32[8,768]{1,0:T(8,128)S(1)}, f32[8,768]{1,0:T(8,128)}, u32[]{:S(2)}) copy-start(f32[8,768]{1,0:T(8,128)} %get-tuple-element.127) | copy-start | bytes 73732
  183.1 11.4 %collective-permute-start.29 = (f32[8,2,48,384]{3,2,1,0:T(8,128)}, f32[8,2,48,384]{3,2,1,0:T(8,128)}, u32[]{:S(2)}, u32[]{:S(2)}) collective-permute-start(f32[8,2,48,384]{3,2,1,0:T(8,128)} %get-tuple-element.122), channel_id=1, source_target_pairs={{0,2},{2,0},{4,6},{6,4},{8,10},{10,8},{12,14},{14,12},{16,18},{18,... | collective-permute-start | bytes 3538952 | tf_op jit(solution)/shard_map/ppermute | solution.py:58
  183.1 11.4 %collective-permute-start.30 = (f32[8,2,48,384]{3,2,1,0:T(8,128)}, f32[8,2,48,384]{3,2,1,0:T(8,128)}, u32[]{:S(2)}, u32[]{:S(2)}) collective-permute-start(f32[8,2,48,384]{3,2,1,0:T(8,128)} %get-tuple-element.123), channel_id=1, source_target_pairs={{0,2},{2,0},{4,6},{6,4},{8,10},{10,8},{12,14},{14,12},{16,18},{18,... | collective-permute-start | bytes 3538952 | tf_op jit(solution)/shard_map/ppermute | solution.py:58
  183.7 2.4 collective-permute-start.33
  186.1 82.0 %collective-permute-start.24 = (f32[1024,768]{1,0:T(8,128)S(1)}, f32[1024,768]{1,0:T(8,128)}, u32[]{:S(2)}, u32[]{:S(2)}) collective-permute-start(f32[1024,768]{1,0:T(8,128)S(1)} %get-tuple-element.118), channel_id=1, source_target_pairs={{0,1},{1,0},{2,3},{3,2},{4,5},{5,4},{6,7},{7,6},{8,9},{9,8},{10,11... | collective-permute-start | bytes 9437192 | tf_op jit(solution)/shard_map/ppermute | solution.py:54
  187.6 12.9 %collective-permute-start.34 = (f32[11,768]{1,0:T(8,128)S(1)}, f32[11,768]{1,0:T(8,128)S(1)}, u32[]{:S(2)}, u32[]{:S(2)}) collective-permute-start(f32[11,768]{1,0:T(8,128)S(1)} %fusion.14), channel_id=1, source_target_pairs={{0,4},{2,6},{4,0},{6,2},{8,12},{10,14},{12,8},{14,10},{16,20},{18,... | collective-permute-start | bytes 101384 | tf_op jit(solution)/shard_map/ppermute | solution.py:58
  190.5 27.8 %collective-permute-start.28 = (f32[2,48,1536]{2,1,0:T(8,128)}, f32[2,48,1536]{2,1,0:T(8,128)}, u32[]{:S(2)}, u32[]{:S(2)}) collective-permute-start(f32[2,48,1536]{2,1,0:T(8,128)} %bitcast_add_fusion), channel_id=1, source_target_pairs={{0,4},{2,6},{4,0},{6,2},{8,12},{10,14},{12,8},{14,10},{16,20},{18,... | collective-permute-start | bytes 1769480 | tf_op jit(solution)/shard_map/ppermute | solution.py:58
  196.4 16.6 %collective-permute-start.32 = (f32[4,2,48,384]{3,2,1,0:T(8,128)}, f32[4,2,48,384]{3,2,1,0:T(8,128)}, u32[]{:S(2)}, u32[]{:S(2)}) collective-permute-start(f32[4,2,48,384]{3,2,1,0:T(8,128)} %bitcast.33), channel_id=1, source_target_pairs={{0,8},{2,10},{4,12},{6,14},{8,0},{10,2},{12,4},{14,6},{16,24},{18,... | collective-permute-start | bytes 1769480 | tf_op jit(solution)/shard_map/ppermute | solution.py:58
  199.9 18.3 %collective-permute-start.31 = (f32[4,2,48,384]{3,2,1,0:T(8,128)}, f32[4,2,48,384]{3,2,1,0:T(8,128)}, u32[]{:S(2)}, u32[]{:S(2)}) collective-permute-start(f32[4,2,48,384]{3,2,1,0:T(8,128)} %bitcast.30), channel_id=1, source_target_pairs={{0,4},{2,6},{4,0},{6,2},{8,12},{10,14},{12,8},{14,10},{16,20},{18,... | collective-permute-start | bytes 1769480 | tf_op jit(solution)/shard_map/ppermute | solution.py:58
  200.5 23.4 %collective-permute-start.27 = (f32[2,48,1536]{2,1,0:T(8,128)}, f32[2,48,1536]{2,1,0:T(8,128)}, u32[]{:S(2)}, u32[]{:S(2)}) collective-permute-start(f32[2,48,1536]{2,1,0:T(8,128)} %bitcast_add_fusion.1), channel_id=1, source_target_pairs={{0,8},{2,10},{4,12},{6,14},{8,0},{10,2},{12,4},{14,6},{16,24},{18,... | collective-permute-start | bytes 1769480 | tf_op jit(solution)/shard_map/ppermute | solution.py:58
  223.9 13.0 %collective-permute-start.39 = (f32[11,768]{1,0:T(8,128)S(1)}, f32[11,768]{1,0:T(8,128)S(1)}, u32[]{:S(2)}, u32[]{:S(2)}) collective-permute-start(f32[11,768]{1,0:T(8,128)S(1)} %add.486), channel_id=1, source_target_pairs={{0,8},{2,10},{4,12},{6,14},{8,0},{10,2},{12,4},{14,6},{16,24},{18,... | collective-permute-start | bytes 101384 | tf_op jit(solution)/shard_map/ppermute | solution.py:58
  227.4 10.4 %collective-permute-start.38 = (f32[2,2,48,384]{3,2,1,0:T(8,128)}, f32[2,2,48,384]{3,2,1,0:T(8,128)S(1)}, u32[]{:S(2)}, u32[]{:S(2)}) collective-permute-start(f32[2,2,48,384]{3,2,1,0:T(8,128)} %bitcast_add_fusion.3), channel_id=1, source_target_pairs={{0,4},{2,6},{4,0},{6,2},{8,12},{10,14},{12,8},{14,10},{16,20},{18,... | collective-permute-start | bytes 884744 | tf_op jit(solution)/shard_map/ppermute | solution.py:58
  229.9 12.3 %collective-permute-start.37 = (f32[2,2,48,384]{3,2,1,0:T(8,128)}, f32[2,2,48,384]{3,2,1,0:T(8,128)}, u32[]{:S(2)}, u32[]{:S(2)}) collective-permute-start(f32[2,2,48,384]{3,2,1,0:T(8,128)} %bitcast_add_fusion.4), channel_id=1, source_target_pairs={{0,8},{2,10},{4,12},{6,14},{8,0},{10,2},{12,4},{14,6},{16,24},{18,... | collective-permute-start | bytes 884744 | tf_op jit(solution)/shard_map/ppermute | solution.py:58
  232.3 23.1 %collective-permute-start.36 = (f32[1,48,1536]{2,1,0:T(8,128)}, f32[1,48,1536]{2,1,0:T(8,128)}, u32[]{:S(2)}, u32[]{:S(2)}) collective-permute-start(f32[1,48,1536]{2,1,0:T(8,128)} %fusion.3), channel_id=1, source_target_pairs={{0,16},{2,18},{4,20},{6,22},{8,24},{10,26},{12,28},{14,30},{16,0},... | collective-permute-start | bytes 884744 | tf_op jit(solution)/shard_map/ppermute | solution.py:58
  237.6 21.4 %collective-permute-start.35 = (f32[1,48,1536]{2,1,0:T(8,128)}, f32[1,48,1536]{2,1,0:T(8,128)}, u32[]{:S(2)}, u32[]{:S(2)}) collective-permute-start(f32[1,48,1536]{2,1,0:T(8,128)} %fusion.4), channel_id=1, source_target_pairs={{0,16},{2,18},{4,20},{6,22},{8,24},{10,26},{12,28},{14,30},{16,0},... | collective-permute-start | bytes 884744 | tf_op jit(solution)/shard_map/ppermute | solution.py:58
  259.8 12.0 %collective-permute-start.42 = (f32[11,768]{1,0:T(8,128)S(1)}, f32[11,768]{1,0:T(8,128)S(1)}, u32[]{:S(2)}, u32[]{:S(2)}) collective-permute-start(f32[11,768]{1,0:T(8,128)S(1)} %add.506), channel_id=1, source_target_pairs={{0,16},{2,18},{4,20},{6,22},{8,24},{10,26},{12,28},{14,30},{16,0},... | collective-permute-start | bytes 101384 | tf_op jit(solution)/shard_map/ppermute | solution.py:58
  260.9 14.5 %collective-permute-start.41 = (f32[1,2,48,384]{3,2,1,0:T(8,128)S(1)}, f32[1,2,48,384]{3,2,1,0:T(8,128)S(1)}, u32[]{:S(2)}, u32[]{:S(2)}) collective-permute-start(f32[1,2,48,384]{3,2,1,0:T(8,128)S(1)} %fusion.12), channel_id=1, source_target_pairs={{0,16},{2,18},{4,20},{6,22},{8,24},{10,26},{12,28},{14,30},{16,0},... | collective-permute-start | bytes 442376 | tf_op jit(solution)/shard_map/ppermute | solution.py:58
  265.1 11.9 %collective-permute-start.40 = (f32[1,2,48,384]{3,2,1,0:T(8,128)S(1)}, f32[1,2,48,384]{3,2,1,0:T(8,128)S(1)}, u32[]{:S(2)}, u32[]{:S(2)}) collective-permute-start(f32[1,2,48,384]{3,2,1,0:T(8,128)S(1)} %fusion.13), channel_id=1, source_target_pairs={{0,16},{2,18},{4,20},{6,22},{8,24},{10,26},{12,28},{14,30},{16,0},... | collective-permute-start | bytes 442376 | tf_op jit(solution)/shard_map/ppermute | solution.py:58
  (39 other events, 99.1 us)

commit v2 on v1

--- a/solution.py
+++ b/solution.py
@@ -330,61 +330,58 @@
     return [slice(u, u + UNIT_TILE) for u in range(0, units, UNIT_TILE)]
 
 
-def narrow_copies(parts, stage, sems, places, out_s):
-    depth = stage.shape[0]
-    rows = stage.shape[1]
-
-    def copy(k):
-        return pltpu.make_async_copy(parts[k].at[0], stage.at[k % depth], sems.at[k % depth])
+def narrow_copies(parts, stage, sems, places, up_out, down_out):
+    rows, width = stage.shape[1], down_out.shape[1]
+    copies = [
+        pltpu.make_async_copy(part.at[0], stage.at[k], sems.at[k]) for k, part in enumerate(parts)
+    ]
 
     def start():
-        for k in range(min(depth, len(parts))):
-            copy(k).start()
+        for copy in copies:
+            copy.start()
 
     def finish():
-        for k in range(len(parts)):
-            copy(k).wait()
-            place = pl.multiple_of(places[k] * rows, rows)
-            out_s[pl.ds(place, rows), :] = stage[k % depth].astype(BF16)
-            if k + depth < len(parts):
-                copy(k + depth).start()
+        count = len(copies) // 2
+        for k, copy in enumerate(copies):
+            copy.wait()
+            if k < count:
+                place = pl.multiple_of(places[k] * rows, rows)
+                up_out[pl.ds(place, rows), :] = stage[k].astype(BF16)
+            else:
+                for side in range(2):
+                    place = pl.multiple_of((places[k - count] * 2 + side) * rows, rows)
+                    cut = slice(side * width, (side + 1) * width)
+                    down_out[pl.ds(place, rows), :] = stage[k, :, cut].astype(BF16)
 
     return start, finish
 
 
-def placed_kernel(count, slots_ref, *refs):
-    up_parts, down_parts, refs = refs[:count], refs[count : 2 * count], refs[2 * count :]
-    up_ref, down_ref, up_stage, down_stage, up_sems, down_sems = refs
-    places = [slots_ref[k] for k in range(count)]
-    start_up, finish_up = narrow_copies(up_parts, up_stage, up_sems, places, up_ref)
-    start_down, finish_down = narrow_copies(down_parts, down_stage, down_sems, places, down_ref)
-    start_up()
-    start_down()
-    finish_up()
-    finish_down()
-
-
-def placed(slots, ups, downs, group):
-    count = len(ups)
-    scalars = pl.BlockSpec(memory_space=pltpu.SMEM)
-    anywhere = pl.BlockSpec(memory_space=pl.ANY)
-    out_shape = [
-        shape((group * part[0].shape[1], part[0].shape[2]), BF16) for part in (ups, downs)
-    ]
+def placed_kernel(slots_ref, *refs):
+    *parts, up_ref, down_ref, stage, sems = refs
+    places = [slots_ref[k] for k in range(len(parts) // 2)]
+    start, finish = narrow_copies(parts, stage, sems, places, up_ref, down_ref)
+    start()
+    finish()
+
+
+def placed(slots, parts, group):
+    _, rows, units = parts[0].shape
+    width = units // 2
+    dims = [(group * rows, units), (2 * group * rows, width)]
     return pl.pallas_call(
-        functools.partial(placed_kernel, count),
+        placed_kernel,
         grid=(1,),
-        in_specs=[scalars] + [anywhere] * (2 * count),
-        out_specs=[whole(*out.shape) for out in out_shape],
-        out_shape=out_shape,
+        in_specs=[pl.BlockSpec(memory_space=pltpu.SMEM)]
+        + [pl.BlockSpec(memory_space=pl.ANY)] * len(parts),
+        out_specs=[whole(*out) for out in dims],
+        out_shape=[shape(out, BF16) for out in dims],
         scratch_shapes=[
-            pltpu.VMEM((count,) + ups[0].shape[1:], F32), pltpu.VMEM((count,) + downs[0].shape[1:], F32),
-            pltpu.SemaphoreType.DMA((count,)), pltpu.SemaphoreType.DMA((count,)),
-        ],
-        compiler_params=params_of(20),
+            pltpu.VMEM((len(parts),) + parts[0].shape[1:], F32), pltpu.SemaphoreType.DMA((len(parts),))
+        ],
+        compiler_params=params_of(56),
         cost_estimate=cost(1e6, 1e6),
         name="placed",
-    )(slots, *ups, *downs)
+    )(slots, *parts)
 
 
 def feed_rows(
@@ -444,16 +441,16 @@
 
 
 def feed_kernel(
-    orders, tiles, late_count, core_ref, slots_ref, x_ref, cot_ref, ctx_ref, far0_ref, far1_ref, far2_ref, *refs
+    orders, tiles, late_count, core_ref, slots_ref, x_ref, cot_ref, ctx_ref, far0_ref, far1_ref, *refs
 ):
     vector_refs, refs = refs[:8], refs[8:]
     out_hbm, near_half_hbm, far_half_hbm, up_hbm, down_hbm, far_up_hbm, far_down_hbm, *refs = refs
-    up_parts, down_parts, refs = refs[:late_count], refs[late_count : 2 * late_count], refs[2 * late_count :]
+    late_parts, refs = refs[:late_count], refs[late_count:]
     mixed_ref, d_pre_ref, d_attn_ref, sums_ref, up_sums_ref, *refs = refs
     count = 4 if orders else 2
     grad_refs, refs = refs[:count], refs[count:]
     nb_s, act_s, d_feed_s, d_hidden_s, out_s, far_out_s, up_s, down_s, far_up_s, far_down_s, *refs = refs
-    half_stage, up_stage, down_stage, sems, up_sems, down_sems = refs
+    half_stage, late_stage, sems, late_sems = refs
     step = pl.program_id(0)
     tile = x_ref.shape[0]
     copies = [
@@ -463,9 +460,10 @@
             (up_hbm, up_s), (down_hbm, down_s), (far_up_hbm, far_up_s), (far_down_hbm, far_down_s),
         ))
     ]
-    places = [slots_ref[k] for k in range(late_count)]
-    start_up, finish_up = narrow_copies(up_parts, up_stage, up_sems, places, far_up_s)
-    start_down, finish_down = narrow_copies(down_parts, down_stage, down_sems, places, far_down_s)
+    places = [slots_ref[k] for k in range(late_count // 2)]
+    start_late, finish_late = narrow_copies(
+        late_parts, late_stage, late_sems, places, far_up_s, far_down_s
+    )
 
     def ready(what):
         @pl.when(step == 0)
@@ -473,8 +471,7 @@
             if what == "out":
                 for copy in copies:
                     copy.start()
-                start_up()
-                start_down()
+                start_late()
                 sums_ref[...] = jnp.zeros_like(sums_ref)
                 up_sums_ref[...] = jnp.zeros_like(up_sums_ref)
                 for copy in copies[:3]:
@@ -489,14 +486,13 @@
             else:
                 for copy in copies[5:]:
                     copy.wait()
-                finish_up()
-                finish_down()
+                finish_late()
 
     @pl.when(step < tiles)
     def _():
         here = pl.ds(pl.multiple_of(step * tile, tile), tile)
         feed_rows(
-            x_ref, cot_ref, ctx_ref, (far0_ref, far1_ref, far2_ref), vector_refs, ready, out_s, far_out_s, up_s,
+            x_ref, cot_ref, ctx_ref, (far0_ref, far1_ref), vector_refs, ready, out_s, far_out_s, up_s,
             down_s, far_up_s, far_down_s, mixed_ref, d_pre_ref, d_attn_ref, sums_ref, up_sums_ref, nb_s, act_s,
             d_feed_s, d_hidden_s, here,
         )
@@ -516,7 +512,7 @@
 
 def feed(
     orders, core, slots, x, cotangent, context, far_context, out_weight, halves, vectors, up, down, far_up, far_down,
-    ups, downs,
+    late,
 ):
     rows, width = x.shape
     local, units = out_weight.shape[0], up.shape[1]
@@ -536,14 +532,13 @@
         grad_shapes = [shape((width, units), F32)] * 2
     scalars = pl.BlockSpec(memory_space=pltpu.SMEM)
     anywhere = pl.BlockSpec(memory_space=pl.ANY)
-    depth = len(ups)
     return pl.pallas_call(
-        functools.partial(feed_kernel, orders, tiles, len(ups)),
+        functools.partial(feed_kernel, orders, tiles, len(late)),
         grid=(tiles + units // GRAD_TILE,),
         in_specs=[
             scalars, scalars, across(width), across(width), along(local),
             *[along(part.shape[0]) for part in far_context], *[whole(v.shape[0]) for v in vectors],
-            *[anywhere] * (7 + len(ups) + len(downs)),
+            *[anywhere] * (7 + len(late)),
         ],
         out_specs=[
             across(width), across(width), across(width), whole(8, width), whole(1, units),
@@ -559,16 +554,15 @@
             pltpu.VMEM((local, width), BF16), pltpu.VMEM((local, width), BF16),
             pltpu.VMEM((width, units), BF16), pltpu.VMEM((units, width), BF16),
             pltpu.VMEM((width, units), BF16), pltpu.VMEM((units, width), BF16),
-            pltpu.VMEM((2,) + halves[0].shape, F32), pltpu.VMEM((depth,) + ups[0].shape[1:], F32),
-            pltpu.VMEM((depth,) + downs[0].shape[1:], F32), pltpu.SemaphoreType.DMA((7,)),
-            pltpu.SemaphoreType.DMA((depth,)), pltpu.SemaphoreType.DMA((depth,)),
+            pltpu.VMEM((2,) + halves[0].shape, F32), pltpu.VMEM((len(late),) + late[0].shape[1:], F32),
+            pltpu.SemaphoreType.DMA((7,)), pltpu.SemaphoreType.DMA((len(late),)),
         ],
         compiler_params=params_of(56),
         cost_estimate=cost(25e9, 30e6),
         name="feed",
     )(
         core, slots, x, cotangent, context, *far_context, *vectors, out_weight, *halves, up, down,
-        far_up, far_down, *ups, *downs,
+        far_up, far_down, *late,
     )
 
 
@@ -603,45 +597,43 @@
             return lax.dynamic_slice_in_dim(values, place * count, count, 0).astype(F32)[None]
 
         up_piece = piece(up_weight)
-        down_piece = piece(after(down_weight, up_piece))
+        two_rows = piece(after(down_weight, up_piece))
+        middle = two_rows.shape[1] // 2
+        down_piece = jnp.concatenate([two_rows[:, :middle], two_rows[:, middle:]], axis=2)
+        far_a = swapped(up_piece)
+        far_b = swapped(down_piece)
+        far_bias = swapped(up_bias)
         half = local // 2
-        far_up = swapped(up_piece)
-        far_down = swapped(down_piece)
+
         ordering = cluster_order[:, 0, :]
         order_rows = ordering.reshape(-1, 2, rows)
         x = after(hidden_in, up_piece, down_piece)
         context, moved, probs = attend(x, qkv_weight, qv_bias.T, order_rows)
         pairs = order_rows.shape[0]
         far_context = [
-            swapped(context[p * 128 : (p + 1) * 128].astype(F32)) for p in range(pairs)
+            swapped(context[:128].astype(F32)), swapped(context[128:].astype(F32))
         ]
-        out_piece = lax.dynamic_slice_in_dim(out_weight, core * half, half, 0)
-        out_piece = out_piece.astype(F32)
-        far_bias = swapped(up_bias)
+        out_piece = lax.dynamic_slice_in_dim(out_weight, core * half, half, 0).astype(F32)
 
         trade = lambda values, step: traded(values, step, n_items)
         at_once = lambda *values: lax.optimization_barrier(values)
-        far_half = swapped(after(out_piece, down_piece))
-        up0 = after(far_up, context)
-        up4, up2 = trade(up0, 4), trade(up0, 2)
-        down0 = after(far_down, up0)
-        down4, down2 = trade(down0, 4), trade(down0, 2)
-        up4, up2, down4, down2, far_half, far_context[0], far_bias = at_once(
-            up4, up2, down4, down2, far_half, far_context[0], far_bias
+        a0 = after(far_a, context)
+        a4, a2 = trade(a0, 4), trade(a0, 2)
+        b0 = after(far_b, a0)
+        far_half = swapped(after(out_piece, b0))
+        b4, b2 = trade(b0, 4), trade(b0, 2)
+        a4, a2, far_context[0], _ = at_once(a4, a2, far_context[0], b0)
+        a6 = trade(a4, 2)
+        b4, b2, far_half, _ = at_once(b4, b2, far_half, a4)
+        b6 = trade(b4, 2)
+        all_slots = lambda ks: jnp.stack([place ^ k for k in ks]).astype(jnp.int32)
+        come = [part for one in ((a0, a4, a2), (b0, b4, b2)) for part in (*one, *(trade(p, 1) for p in one))]
+        far_up, far_down = placed(all_slots((0, 4, 2, 1, 5, 3)), come, group)
+        a6, b6, far_context[1], far_bias, far_up = at_once(
+            a6, b6, far_context[1], far_bias, far_up
         )
-        up6, down6 = trade(up4, 2), trade(down4, 2)
-        ups, downs = [up0, up4, up2], [down0, down4, down2]
-        ups, downs = [[after(part, down4) for part in parts] for parts in (ups, downs)]
-        up_beside = [trade(part, 1) for part in ups]
-        down_beside = [trade(part, 1) for part in downs]
-        other_half = trade(after(far_half, down4), 1)
-        all_slots = lambda ks: jnp.stack([place ^ k ^ c for c in (0, 1) for k in ks]).astype(jnp.int32)
-        slots = all_slots((6,))
-        far_up, far_down = placed(all_slots((0, 4, 2)), ups + up_beside, downs + down_beside, group)
-        up6, down6, far_context[1], far_context[2], far_up = at_once(
-            up6, down6, far_context[1], far_context[2], far_up
-        )
-        ups, downs = [[part, trade(part, 1)] for part in (up6, down6)]
+        other_half = trade(far_half, 1)
+        late, slots = [a6, trade(a6, 1), b6, trade(b6, 1)], all_slots((6, 7))
         which = core.astype(jnp.int32).reshape(1)
 
         split = width % (8 * n_items) == 0
@@ -651,7 +643,7 @@
             (bits, late_y) if split else None, which, slots, x, cotangent, context, far_context,
             out_weight, [far_half, other_half],
             [out_bias, norm1_gain, norm1_bias, down_bias, norm2_gain, norm2_bias, up_bias, far_bias],
-            up_weight, down_weight, far_up, far_down, ups, downs,
+            up_weight, down_weight, far_up, far_down, late,
         )
 
         def packed_of(grad_qv):

time: 284 us -> 278 us (0.979)
  local copies, waits for them, and re-layouts: 25.4 us -> 14.8 us
  Pallas kernels: 80.7 us -> 83.8 us
    unnamed x90 -> x80, local copies, waits for them, and re-layouts: 22.8 us -> 11.6 us
    pallas_call x2, Pallas kernels: 47.1 us -> 50.2 us  [the longest x1 44.3 us: feed(): pl.pallas_call(functools.partial(feed_kernel, orders, tiles, len(late)),...]
    ppermute x8 -> x7, waiting for transfers between devices: 29.1 us -> 30.5 us  [swapped(): return lax.ppermute(values, 'heads', [(0, 1), (1, 0)])]
    ppermute x8 -> x7, starting transfers between devices: 10.6 us -> 10.1 us  [swapped(): return lax.ppermute(values, 'heads', [(0, 1), (1, 0)])]
  transfers between devices with their start and end apart: 43 -> 42, of which waited for: 21 -> 18; matrix products, arithmetic and copies ran while one was open for 12% -> 12% of each run, Pallas kernels for 13% -> 14%
where the time goes in v2:
time: 278 us; the launch traced here: 277 us
  waiting for transfers between devices  97.9 us (35%)
  Pallas kernels  83.8 us (30%)
  other arithmetic  40.5 us (15%)
  starting transfers between devices  39.2 us (14%)
  local copies, waits for them, and re-layouts  14.8 us (5%)
    ppermute x35, waiting for transfers between devices, traded(): lax.ppermute(values, 'items', [(i, i ^ step) for i in range(n_items)])  67.5 us
    pallas_call x1, Pallas kernels, feed(): pl.pallas_call(functools.partial(feed_kernel, orders, tiles, len(late)),...  44.3 us
    ppermute x7, waiting for transfers between devices, swapped(): return lax.ppermute(values, 'heads', [(0, 1), (1, 0)])  30.5 us
    ppermute x35, starting transfers between devices, traded(): lax.ppermute(values, 'items', [(i, i ^ step) for i in range(n_items)])  29.1 us
    add x12, other arithmetic, add(): self.send = sum((self.part(term, [1 - mine]) for term in self.terms))  24.4 us
    pallas_call x1, Pallas kernels, attend_back(): pl.pallas_call(functools.partial(attend_back_kernel, orders), grid=(pairs...  20.3 us
    pallas_call x1, Pallas kernels, attend(): pl.pallas_call(attend_kernel, grid=(pairs,), in_specs=[whole(rows, width)...  13.3 us
    unnamed x80, local copies, waits for them, and re-layouts  11.6 us
  transfers between devices with their start and end apart: 42, of which 18 were waited for; matrix products, arithmetic and copies ran while one was open for 12% of the time, Pallas kernels for 14%

profile of v2, /device:TPU:0, one launch (start us, length us, event | category | flops | bytes accessed | tf_op | source)
XLA Modules:
  0.0 277.3 jit_solution(9430828301546202581)
XLA Ops:
  0.7 1.8 bitcast_convert_fusion.1
  2.5 2.9 %collective-permute-start = (f32[1,96,1536]{2,1,0:T(8,128)}, f32[1,96,1536]{2,1,0:T(8,128)}, u32[]{:S(2)}, u32[]{:S(2)}) collective-permute-start(f32[1,96,1536]{2,1,0:T(8,128)} %bitcast_convert_fusion.1), channel_id=1, source_target_pairs={{0,1},{1,0},{2,3},{3,2},{4,5},{5,4},{6,7},{7,6},{8,9},{9,8},{10,11... | collective-permute-start | bytes 1769480 | tf_op jit(solution)/shard_map/ppermute | solution.py:54
  9.2 13.3 %attend.1 = (bf16[384,1024]{1,0:T(8,128)(2,1)S(1)}, bf16[6,192,1024]{2,1,0:T(8,128)(2,1)S(1)}, bf16[6,1024,128]{2,1,0:T(8,128)(2,1)S(1)}) custom-call(bf16[1024,768]{1,0:T(8,128)(2,1)S(1)} %copy-done, bf16[3,768,384]{2,1,0:T(8,128)(2,1)S(1)} %copy-done.4, f32[384,2]{1,0:T(8,128)S(1)} %bitcast.135, s32[3,2,1024]{2,1,0:T(2,128)S(1)} %reshape_squeeze.3.row_ref), custom_call_target="tpu_custom_call" | custom-call | flops 12000000 | bytes 12000 | tf_op jit(solution)/shard_map/attend/pallas_call | solution.py:177
  26.0 2.0 collective-permute-start.3
  28.1 1.6 collective-permute-start.1
  29.7 1.5 collective-permute-start.2
  32.5 2.1 collective-permute-start.6
  34.7 1.5 collective-permute-start.8
  36.2 7.5 %collective-permute-done.3.far0_ref = f32[128,1024]{1,0:T(8,128)S(1)} collective-permute-done((f32[128,1024]{1,0:T(8,128)}, f32[128,1024]{1,0:T(8,128)S(1)}, u32[]{:S(2)}, u32[]{:S(2)}) %collective-permute-start.3) | collective-permute-done | bytes 524320 | tf_op jit(solution)/shard_map/ppermute | solution.py:54
  43.7 2.1 collective-permute-start.7
  46.3 9.2 %collective-permute-done.8.refs_9_ = f32[192,768]{1,0:T(8,128)S(1)} collective-permute-done((f32[192,768]{1,0:T(8,128)S(1)}, f32[192,768]{1,0:T(8,128)S(1)}, u32[]{:S(2)}, u32[]{:S(2)}) %collective-permute-start.8) | collective-permute-done | bytes 589856 | tf_op jit(solution)/shard_map/ppermute | solution.py:54
  55.5 2.2 collective-permute-done.7.refs_8_
  60.3 1.6 collective-permute-start.9
  65.3 5.9 %placed.1 = (bf16[768,1536]{1,0:T(8,128)(2,1)}, bf16[1536,768]{1,0:T(8,128)(2,1)}) custom-call(s32[6]{0:T(128)} %stack.42.slots_ref, f32[1,96,1536]{2,1,0:T(8,128)} %collective-permute-done.refs_0_, f32[1,96,1536]{2,1,0:T(8,128)} %collective-permute-done.1.refs_1_, f32[1,96,1536]{2,1,0:T(8,128)} %collective-permute-done.2.refs_2_, ...), custom_call_target="tpu_custom_call" | custom-call | flops 1000 | bytes 1000 | tf_op jit(solution)/shard_map/placed/pallas_call | solution.py:371
  71.2 12.5 %collective-permute-done.11.refs_7_ = f32[1536]{0:T(1024)S(1)} collective-permute-done((f32[1536]{0:T(1024)S(1)}, f32[1536]{0:T(1024)S(1)}, u32[]{:S(2)}, u32[]{:S(2)}) %collective-permute-start.11) | collective-permute-done | bytes 6176 | tf_op jit(solution)/shard_map/ppermute | solution.py:54
  83.7 5.0 %collective-permute-done.5.refs_15_ = f32[1,96,1536]{2,1,0:T(8,128)} collective-permute-done((f32[1,96,1536]{2,1,0:T(8,128)}, f32[1,96,1536]{2,1,0:T(8,128)}, u32[]{:S(2)}, u32[]{:S(2)}) %collective-permute-start.5) | collective-permute-done | bytes 589856 | tf_op jit(solution)/shard_map/ppermute | solution.py:58
  89.8 1.9 collective-permute-done.19.refs_16_
  92.5 44.3 %feed.1 = (bf16[1024,768]{1,0:T(8,128)(2,1)}, f32[1024,768]{1,0:T(8,128)}, bf16[1024,768]{1,0:T(8,128)(2,1)}, f32[8,768]{1,0:T(8,128)}, f32[1,1536]{1,0:T(1,128)...) custom-call(s32[1]{0:T(128)} %bitcast.core_ref, ...), custom_call_target="tpu_custom_call" | custom-call | flops 25000000 | bytes 30000 | tf_op jit(solution)/shard_map/feed/pallas_call | solution.py:535
  137.4 6.2 %collective-permute-done.21 = f32[8,48,1536]{2,1,0:T(8,128)S(1)} collective-permute-done((f32[8,48,1536]{2,1,0:T(8,128)}, f32[8,48,1536]{2,1,0:T(8,128)S(1)}, u32[]{:S(2)}, u32[]{:S(2)}) %collective-permute-start.21) | collective-permute-done | bytes 2359328 | tf_op jit(solution)/shard_map/ppermute | solution.py:58
  143.6 1.6 collective-permute-done.22
  145.2 3.0 %dynamic-slice_add_fusion = f32[1,2,2,48,1536]{4,3,2,1,0:T(8,128)} fusion(f32[2,2,2,48,1536]{4,3,2,1,0:T(8,128)} %bitcast.18, s32[]{:T(128)S(6)} %select_n.30, f32[2,2,2,48,1536]{4,3,2,1,0:T(8,128)} %bitcast.141), kind=kLoop, calls=%fused_computation.1 | loop fusion | flops 294912 | bytes 3538948 | tf_op jit(solution)/shard_map/add | solution.py:115
  148.2 1.6 collective-permute-start.25
  149.8 2.6 dynamic-slice_add_fusion.1
  152.4 1.5 collective-permute-start.24
  156.8 20.3 %attend_back.1 = (f32[1024,768]{1,0:T(8,128)S(1)}, f32[2,384]{1,0:T(2,128)S(1)}, f32[8,2,48,384]{3,2,1,0:T(8,128)S(1)}, f32[8,2,48,384]{3,2,1,0:T(8,128)}, f32[8...) custom-call(s32[1]{0:T(128)} %bitcast.core_ref, bf16[1024,768]{1,0:T(8,128)(2,1)S(1)} %copy-done.1, ...), custom_call_target="tpu_custom_call" | custom-call | flops 20000000 | bytes 20000 | tf_op jit(solution)/shard_map/attend_back/pallas_call | solution.py:282
  179.7 2.3 collective-permute-done.32
  183.7 2.3 bitcast_add_fusion
  186.1 1.5 collective-permute-start.27
  187.6 2.5 bitcast_add_fusion.1
  190.1 1.9 dynamic-slice_add_fusion.2
  192.5 2.0 dynamic-slice_add_fusion.3
  195.0 1.6 collective-permute-start.26
  196.5 12.1 %collective-permute-done.31 = f32[4,2,48,384]{3,2,1,0:T(8,128)} collective-permute-done((f32[4,2,48,384]{3,2,1,0:T(8,128)}, f32[4,2,48,384]{3,2,1,0:T(8,128)}, u32[]{:S(2)}, u32[]{:S(2)}) %collective-permute-start.31) | collective-permute-done | bytes 589856 | tf_op jit(solution)/shard_map/ppermute | solution.py:58
  208.6 5.2 %collective-permute-done.30 = f32[4,2,48,384]{3,2,1,0:T(8,128)} collective-permute-done((f32[4,2,48,384]{3,2,1,0:T(8,128)}, f32[4,2,48,384]{3,2,1,0:T(8,128)}, u32[]{:S(2)}, u32[]{:S(2)}) %collective-permute-start.30) | collective-permute-done | bytes 589856 | tf_op jit(solution)/shard_map/ppermute | solution.py:58
  213.8 5.7 %collective-permute-done.26 = f32[2,48,1536]{2,1,0:T(8,128)} collective-permute-done((f32[2,48,1536]{2,1,0:T(8,128)}, f32[2,48,1536]{2,1,0:T(8,128)}, u32[]{:S(2)}, u32[]{:S(2)}) %collective-permute-start.26) | collective-permute-done | bytes 589856 | tf_op jit(solution)/shard_map/ppermute | solution.py:58
  220.0 1.9 bitcast_add_fusion.3
  222.5 1.9 bitcast_add_fusion.4
  224.4 1.6 collective-permute-start.36
  225.9 2.0 fusion.3
  227.9 2.6 collective-permute-start.35
  230.5 2.0 fusion.4
  234.5 16.0 %collective-permute-done.35 = f32[1,48,1536]{2,1,0:T(8,128)} collective-permute-done((f32[1,48,1536]{2,1,0:T(8,128)}, f32[1,48,1536]{2,1,0:T(8,128)}, u32[]{:S(2)}, u32[]{:S(2)}) %collective-permute-start.35) | collective-permute-done | bytes 294944 | tf_op jit(solution)/shard_map/ppermute | solution.py:58
  250.5 4.1 %collective-permute-done.34 = f32[1,48,1536]{2,1,0:T(8,128)} collective-permute-done((f32[1,48,1536]{2,1,0:T(8,128)}, f32[1,48,1536]{2,1,0:T(8,128)}, u32[]{:S(2)}, u32[]{:S(2)}) %collective-permute-start.34) | collective-permute-done | bytes 294944 | tf_op jit(solution)/shard_map/ppermute | solution.py:58
  256.5 3.0 %collective-permute-start.40 = (f32[1,2,48,384]{3,2,1,0:T(8,128)S(1)}, f32[1,2,48,384]{3,2,1,0:T(8,128)S(1)}, u32[]{:S(2)}, u32[]{:S(2)}) collective-permute-start(f32[1,2,48,384]{3,2,1,0:T(8,128)S(1)} %fusion.12), channel_id=1, source_target_pairs={{0,16},{2,18},{4,20},{6,22},{8,24},{10,26},{12,28},{14,30},{16,0},... | collective-permute-start | bytes 442376 | tf_op jit(solution)/shard_map/ppermute | solution.py:58
  260.7 2.9 %fusion.2 = (f32[48,1536]{1,0:T(8,128)}, f32[1536,48]{0,1:T(8,128)}) fusion(f32[1,48,1536]{2,1,0:T(8,128)} %collective-permute-done.35, f32[2,48,1536]{2,1,0:T(8,128)} %collective-permute-done.27, s32[]{:T(128)S(6)} %select_n.33, f32[2,2,48,1536]{3,2,1,0:T(8,128)} %bitcast.26, s32[]{:T(128)S(6)} %select_n.31, f32[2,2,2,48,1536]{4,3,2,1,0:T(8,128)} %bitcast.18, ...), kind=kLoop, calls=%fused_computation.12 | loop fusion | flops 589824 | bytes 3538956 | tf_op jit(solution)/shard_map/reshape | solution.py:112
  263.6 3.7 %add_convert_fusion = bf16[1024,768]{1,0:T(8,128)(2,1)} fusion(f32[1024,768]{1,0:T(8,128)} %collective-permute-done.23, f32[1024,768]{1,0:T(8,128)S(1)} %copy-done.17, f32[1024,768]{1,0:T(8,128)S(1)} %get-tuple-element.102), kind=kLoop, calls=%fused_computation | loop fusion | flops 2359296 | bytes 11010048 | tf_op jit(solution)/shard_map/convert_element_type | solution.py:684
  267.4 2.7 collective-permute-done.40
  270.1 1.6 collective-permute-done.39
  (161 shorter events, 37.4 us)
Async XLA Ops:
  2.5 25.6 %collective-permute-start = (f32[1,96,1536]{2,1,0:T(8,128)}, f32[1,96,1536]{2,1,0:T(8,128)}, u32[]{:S(2)}, u32[]{:S(2)}) collective-permute-start(f32[1,96,1536]{2,1,0:T(8,128)} %bitcast_convert_fusion.1), channel_id=1, source_target_pairs={{0,1},{1,0},{2,3},{3,2},{4,5},{5,4},{6,7},{7,6},{8,9},{9,8},{10,11... | collective-permute-start | bytes 1769480 | tf_op jit(solution)/shard_map/ppermute | solution.py:54
  7.5 25.1 %collective-permute-start.4 = (f32[1,96,1536]{2,1,0:T(8,128)}, f32[1,96,1536]{2,1,0:T(8,128)}, u32[]{:S(2)}, u32[]{:S(2)}) collective-permute-start(f32[1,96,1536]{2,1,0:T(8,128)} %pad_maximum_fusion), channel_id=1, source_target_pairs={{0,1},{1,0},{2,3},{3,2},{4,5},{5,4},{6,7},{7,6},{8,9},{9,8},{10,11... | collective-permute-start | bytes 1769480 | tf_op jit(solution)/shard_map/ppermute | solution.py:54
  9.2 18.8 %copy-start.6 = (bf16[384,768]{1,0:T(8,128)(2,1)S(1)}, bf16[384,768]{1,0:T(8,128)(2,1)}, u32[]{:S(2)}) copy-start(bf16[384,768]{1,0:T(8,128)(2,1)} %ow_ref.1) | copy-start | bytes 1769476
  25.1 33.2 %copy-start.2 = (bf16[384,1024]{1,0:T(8,128)(2,1)}, bf16[384,1024]{1,0:T(8,128)(2,1)S(1)}, u32[]{:S(2)}) copy-start(bf16[384,1024]{1,0:T(8,128)(2,1)S(1)} %get-tuple-element.73.ctx_ref) | copy-start | bytes 2359300
  25.1 38.5 %copy-start.35 = (f32[1536]{0:T(1024)S(1)}, f32[1536]{0:T(1024)}, u32[]{:S(2)}) copy-start(f32[1536]{0:T(1024)} %refs_6_.1) | copy-start | bytes 18436
  26.0 17.6 %collective-permute-start.3 = (f32[128,1024]{1,0:T(8,128)}, f32[128,1024]{1,0:T(8,128)S(1)}, u32[]{:S(2)}, u32[]{:S(2)}) collective-permute-start(f32[128,1024]{1,0:T(8,128)} %slice_convert_fusion.1), channel_id=1, source_target_pairs={{0,1},{1,0},{2,3},{3,2},{4,5},{5,4},{6,7},{7,6},{8,9},{9,8},{10,11... | collective-permute-start | bytes 1572872 | tf_op jit(solution)/shard_map/ppermute | solution.py:54
  28.1 17.6 %collective-permute-start.1 = (f32[1,96,1536]{2,1,0:T(8,128)}, f32[1,96,1536]{2,1,0:T(8,128)}, u32[]{:S(2)}, u32[]{:S(2)}) collective-permute-start(f32[1,96,1536]{2,1,0:T(8,128)} %collective-permute-done.refs_0_), channel_id=1, source_target_pairs={{0,8},{2,10},{4,12},{6,14},{8,0},{10,2},{12,4},{14,6},{16,24},{18,... | collective-permute-start | bytes 1769480 | tf_op jit(solution)/shard_map/ppermute | solution.py:58
  29.7 16.0 %collective-permute-start.2 = (f32[1,96,1536]{2,1,0:T(8,128)}, f32[1,96,1536]{2,1,0:T(8,128)}, u32[]{:S(2)}, u32[]{:S(2)}) collective-permute-start(f32[1,96,1536]{2,1,0:T(8,128)} %collective-permute-done.refs_0_), channel_id=1, source_target_pairs={{0,4},{2,6},{4,0},{6,2},{8,12},{10,14},{12,8},{14,10},{16,20},{18,... | collective-permute-start | bytes 1769480 | tf_op jit(solution)/shard_map/ppermute | solution.py:58
  32.5 22.9 %collective-permute-start.6 = (f32[1,96,1536]{2,1,0:T(8,128)}, f32[1,96,1536]{2,1,0:T(8,128)}, u32[]{:S(2)}, u32[]{:S(2)}) collective-permute-start(f32[1,96,1536]{2,1,0:T(8,128)} %collective-permute-done.4.refs_6_), channel_id=1, source_target_pairs={{0,8},{2,10},{4,12},{6,14},{8,0},{10,2},{12,4},{14,6},{16,24},{18,... | collective-permute-start | bytes 1769480 | tf_op jit(solution)/shard_map/ppermute | solution.py:58
  34.7 20.8 %collective-permute-start.8 = (f32[192,768]{1,0:T(8,128)S(1)}, f32[192,768]{1,0:T(8,128)S(1)}, u32[]{:S(2)}, u32[]{:S(2)}) collective-permute-start(f32[192,768]{1,0:T(8,128)S(1)} %dynamic-slice_convert_fusion), channel_id=1, source_target_pairs={{0,1},{1,0},{2,3},{3,2},{4,5},{5,4},{6,7},{7,6},{8,9},{9,8},{10,11... | collective-permute-start | bytes 1769480 | tf_op jit(solution)/shard_map/ppermute | solution.py:54
  43.7 14.0 %collective-permute-start.7 = (f32[1,96,1536]{2,1,0:T(8,128)}, f32[1,96,1536]{2,1,0:T(8,128)S(1)}, u32[]{:S(2)}, u32[]{:S(2)}) collective-permute-start(f32[1,96,1536]{2,1,0:T(8,128)} %collective-permute-done.4.refs_6_), channel_id=1, source_target_pairs={{0,4},{2,6},{4,0},{6,2},{8,12},{10,14},{12,8},{14,10},{16,20},{18,... | collective-permute-start | bytes 1769480 | tf_op jit(solution)/shard_map/ppermute | solution.py:58
  45.8 14.0 %collective-permute-start.15 = (f32[1,96,1536]{2,1,0:T(8,128)}, f32[1,96,1536]{2,1,0:T(8,128)S(1)}, u32[]{:S(2)}, u32[]{:S(2)}) collective-permute-start(f32[1,96,1536]{2,1,0:T(8,128)} %collective-permute-done.4.refs_6_), channel_id=1, source_target_pairs={{0,2},{2,0},{4,6},{6,4},{8,10},{10,8},{12,14},{14,12},{16,18},{18,... | collective-permute-start | bytes 1769480 | tf_op jit(solution)/shard_map/ppermute | solution.py:58
  45.8 14.0 %collective-permute-start.12 = (f32[1,96,1536]{2,1,0:T(8,128)}, f32[1,96,1536]{2,1,0:T(8,128)S(1)}, u32[]{:S(2)}, u32[]{:S(2)}) collective-permute-start(f32[1,96,1536]{2,1,0:T(8,128)} %collective-permute-done.refs_0_), channel_id=1, source_target_pairs={{0,2},{2,0},{4,6},{6,4},{8,10},{10,8},{12,14},{14,12},{16,18},{18,... | collective-permute-start | bytes 1769480 | tf_op jit(solution)/shard_map/ppermute | solution.py:58
  55.5 15.7 %copy-start.20 = (f32[192,768]{1,0:T(8,128)}, f32[192,768]{1,0:T(8,128)S(1)}, u32[]{:S(2)}) copy-start(f32[192,768]{1,0:T(8,128)S(1)} %collective-permute-done.8.refs_9_) | copy-start | bytes 1769476
  57.7 2.7 collective-permute-start.16
  57.7 4.3 %collective-permute-start.17 = (f32[1,96,1536]{2,1,0:T(8,128)S(1)}, f32[1,96,1536]{2,1,0:T(8,128)S(1)}, u32[]{:S(2)}, u32[]{:S(2)}) collective-permute-start(f32[1,96,1536]{2,1,0:T(8,128)S(1)} %collective-permute-done.7.refs_8_), channel_id=1, source_target_pairs={{0,2},{2,0},{4,6},{6,4},{8,10},{10,8},{12,14},{14,12},{16,18},{18,... | collective-permute-start | bytes 1769480 | tf_op jit(solution)/shard_map/ppermute | solution.py:58
  58.3 25.4 %collective-permute-start.10 = (f32[256,1024]{1,0:T(8,128)S(1)}, f32[256,1024]{1,0:T(8,128)S(1)}, u32[]{:S(2)}, u32[]{:S(2)}) collective-permute-start(f32[256,1024]{1,0:T(8,128)S(1)} %slice_convert_fusion), channel_id=1, source_target_pairs={{0,1},{1,0},{2,3},{3,2},{4,5},{5,4},{6,7},{7,6},{8,9},{9,8},{10,11... | collective-permute-start | bytes 3145736 | tf_op jit(solution)/shard_map/ppermute | solution.py:54
  59.8 2.7 collective-permute-start.13
  59.8 5.4 %collective-permute-start.14 = (f32[1,96,1536]{2,1,0:T(8,128)}, f32[1,96,1536]{2,1,0:T(8,128)}, u32[]{:S(2)}, u32[]{:S(2)}) collective-permute-start(f32[1,96,1536]{2,1,0:T(8,128)} %collective-permute-done.2.refs_2_), channel_id=1, source_target_pairs={{0,2},{2,0},{4,6},{6,4},{8,10},{10,8},{12,14},{14,12},{16,18},{18,... | collective-permute-start | bytes 1769480 | tf_op jit(solution)/shard_map/ppermute | solution.py:58
  60.3 23.4 %collective-permute-start.9 = (f32[1,96,1536]{2,1,0:T(8,128)}, f32[1,96,1536]{2,1,0:T(8,128)S(1)}, u32[]{:S(2)}, u32[]{:S(2)}) collective-permute-start(f32[1,96,1536]{2,1,0:T(8,128)} %collective-permute-done.6.refs_7_), channel_id=1, source_target_pairs={{0,4},{2,6},{4,0},{6,2},{8,12},{10,14},{12,8},{14,10},{16,20},{18,... | collective-permute-start | bytes 1769480 | tf_op jit(solution)/shard_map/ppermute | solution.py:58
  61.9 26.7 %collective-permute-start.5 = (f32[1,96,1536]{2,1,0:T(8,128)}, f32[1,96,1536]{2,1,0:T(8,128)}, u32[]{:S(2)}, u32[]{:S(2)}) collective-permute-start(f32[1,96,1536]{2,1,0:T(8,128)} %collective-permute-done.1.refs_1_), channel_id=1, source_target_pairs={{0,4},{2,6},{4,0},{6,2},{8,12},{10,14},{12,8},{14,10},{16,20},{18,... | collective-permute-start | bytes 1769480 | tf_op jit(solution)/shard_map/ppermute | solution.py:58
  63.6 20.1 %collective-permute-start.11 = (f32[1536]{0:T(1024)S(1)}, f32[1536]{0:T(1024)S(1)}, u32[]{:S(2)}, u32[]{:S(2)}) collective-permute-start(f32[1536]{0:T(1024)S(1)} %copy-done.35), channel_id=1, source_target_pairs={{0,1},{1,0},{2,3},{3,2},{4,5},{5,4},{6,7},{7,6},{8,9},{9,8},{10,11... | collective-permute-start | bytes 18440 | tf_op jit(solution)/shard_map/ppermute | solution.py:54
  65.3 24.5 %collective-permute-start.18 = (f32[192,768]{1,0:T(8,128)S(1)}, f32[192,768]{1,0:T(8,128)}, u32[]{:S(2)}, u32[]{:S(2)}) collective-permute-start(f32[192,768]{1,0:T(8,128)S(1)} %collective-permute-done.8.refs_9_), channel_id=1, source_target_pairs={{0,2},{2,0},{4,6},{6,4},{8,10},{10,8},{12,14},{14,12},{16,18},{18,... | collective-permute-start | bytes 1769480 | tf_op jit(solution)/shard_map/ppermute | solution.py:58
  88.7 3.0 %collective-permute-start.19 = (f32[1,96,1536]{2,1,0:T(8,128)}, f32[1,96,1536]{2,1,0:T(8,128)S(1)}, u32[]{:S(2)}, u32[]{:S(2)}) collective-permute-start(f32[1,96,1536]{2,1,0:T(8,128)} %collective-permute-done.5.refs_15_), channel_id=1, source_target_pairs={{0,2},{2,0},{4,6},{6,4},{8,10},{10,8},{12,14},{14,12},{16,18},{18,... | collective-permute-start | bytes 1769480 | tf_op jit(solution)/shard_map/ppermute | solution.py:58
  88.7 3.0 %collective-permute-start.20 = (f32[1,96,1536]{2,1,0:T(8,128)S(1)}, f32[1,96,1536]{2,1,0:T(8,128)}, u32[]{:S(2)}, u32[]{:S(2)}) collective-permute-start(f32[1,96,1536]{2,1,0:T(8,128)S(1)} %collective-permute-done.9.refs_17_), channel_id=1, source_target_pairs={{0,2},{2,0},{4,6},{6,4},{8,10},{10,8},{12,14},{14,12},{16,18},{18,... | collective-permute-start | bytes 1769480 | tf_op jit(solution)/shard_map/ppermute | solution.py:58
  136.8 6.7 %collective-permute-start.21 = (f32[8,48,1536]{2,1,0:T(8,128)}, f32[8,48,1536]{2,1,0:T(8,128)S(1)}, u32[]{:S(2)}, u32[]{:S(2)}) collective-permute-start(f32[8,48,1536]{2,1,0:T(8,128)} %get-tuple-element.94), channel_id=1, source_target_pairs={{0,2},{2,0},{4,6},{6,4},{8,10},{10,8},{12,14},{14,12},{16,18},{18,... | collective-permute-start | bytes 7077896 | tf_op jit(solution)/shard_map/ppermute | solution.py:58
  137.1 8.1 %collective-permute-start.22 = (f32[8,48,1536]{2,1,0:T(8,128)}, f32[8,48,1536]{2,1,0:T(8,128)}, u32[]{:S(2)}, u32[]{:S(2)}) collective-permute-start(f32[8,48,1536]{2,1,0:T(8,128)} %get-tuple-element.95), channel_id=1, source_target_pairs={{0,2},{2,0},{4,6},{6,4},{8,10},{10,8},{12,14},{14,12},{16,18},{18,... | collective-permute-start | bytes 7077896 | tf_op jit(solution)/shard_map/ppermute | solution.py:58
  148.2 35.0 %collective-permute-start.25 = (f32[4,48,1536]{2,1,0:T(8,128)}, f32[4,48,1536]{2,1,0:T(8,128)}, u32[]{:S(2)}, u32[]{:S(2)}) collective-permute-start(f32[4,48,1536]{2,1,0:T(8,128)} %bitcast.19), channel_id=1, source_target_pairs={{0,8},{2,10},{4,12},{6,14},{8,0},{10,2},{12,4},{14,6},{16,24},{18,... | collective-permute-start | bytes 3538952 | tf_op jit(solution)/shard_map/ppermute | solution.py:58
  152.4 31.3 %collective-permute-start.24 = (f32[4,48,1536]{2,1,0:T(8,128)}, f32[4,48,1536]{2,1,0:T(8,128)}, u32[]{:S(2)}, u32[]{:S(2)}) collective-permute-start(f32[4,48,1536]{2,1,0:T(8,128)} %bitcast.16), channel_id=1, source_target_pairs={{0,4},{2,6},{4,0},{6,2},{8,12},{10,14},{12,8},{14,10},{16,20},{18,... | collective-permute-start | bytes 3538952 | tf_op jit(solution)/shard_map/ppermute | solution.py:58
  156.8 22.8 %copy-start.37 = (f32[1,1536]{1,0:T(1,128)S(1)}, f32[1,1536]{1,0:T(1,128)}, u32[]{:S(2)}) copy-start(f32[1,1536]{1,0:T(1,128)} %get-tuple-element.112) | copy-start | bytes 18436
  156.8 22.9 %copy-start.32 = (f32[8,768]{1,0:T(8,128)S(1)}, f32[8,768]{1,0:T(8,128)}, u32[]{:S(2)}) copy-start(f32[8,768]{1,0:T(8,128)} %get-tuple-element.111) | copy-start | bytes 73732
  179.1 11.0 %collective-permute-start.28 = (f32[8,2,48,384]{3,2,1,0:T(8,128)}, f32[8,2,48,384]{3,2,1,0:T(8,128)}, u32[]{:S(2)}, u32[]{:S(2)}) collective-permute-start(f32[8,2,48,384]{3,2,1,0:T(8,128)} %get-tuple-element.106), channel_id=1, source_target_pairs={{0,2},{2,0},{4,6},{6,4},{8,10},{10,8},{12,14},{14,12},{16,18},{18,... | collective-permute-start | bytes 3538952 | tf_op jit(solution)/shard_map/ppermute | solution.py:58
  179.1 11.0 %collective-permute-start.29 = (f32[8,2,48,384]{3,2,1,0:T(8,128)}, f32[8,2,48,384]{3,2,1,0:T(8,128)}, u32[]{:S(2)}, u32[]{:S(2)}) collective-permute-start(f32[8,2,48,384]{3,2,1,0:T(8,128)} %get-tuple-element.107), channel_id=1, source_target_pairs={{0,2},{2,0},{4,6},{6,4},{8,10},{10,8},{12,14},{14,12},{16,18},{18,... | collective-permute-start | bytes 3538952 | tf_op jit(solution)/shard_map/ppermute | solution.py:58
  179.7 2.4 collective-permute-start.32
  182.1 81.6 %collective-permute-start.23 = (f32[1024,768]{1,0:T(8,128)S(1)}, f32[1024,768]{1,0:T(8,128)}, u32[]{:S(2)}, u32[]{:S(2)}) collective-permute-start(f32[1024,768]{1,0:T(8,128)S(1)} %get-tuple-element.102), channel_id=1, source_target_pairs={{0,1},{1,0},{2,3},{3,2},{4,5},{5,4},{6,7},{7,6},{8,9},{9,8},{10,11... | collective-permute-start | bytes 9437192 | tf_op jit(solution)/shard_map/ppermute | solution.py:54
  183.2 11.8 %collective-permute-start.33 = (f32[11,768]{1,0:T(8,128)S(1)}, f32[11,768]{1,0:T(8,128)S(1)}, u32[]{:S(2)}, u32[]{:S(2)}) collective-permute-start(f32[11,768]{1,0:T(8,128)S(1)} %fusion.14), channel_id=1, source_target_pairs={{0,4},{2,6},{4,0},{6,2},{8,12},{10,14},{12,8},{14,10},{16,20},{18,... | collective-permute-start | bytes 101384 | tf_op jit(solution)/shard_map/ppermute | solution.py:58
  186.1 27.8 %collective-permute-start.27 = (f32[2,48,1536]{2,1,0:T(8,128)}, f32[2,48,1536]{2,1,0:T(8,128)}, u32[]{:S(2)}, u32[]{:S(2)}) collective-permute-start(f32[2,48,1536]{2,1,0:T(8,128)} %bitcast_add_fusion), channel_id=1, source_target_pairs={{0,4},{2,6},{4,0},{6,2},{8,12},{10,14},{12,8},{14,10},{16,20},{18,... | collective-permute-start | bytes 1769480 | tf_op jit(solution)/shard_map/ppermute | solution.py:58
  192.0 16.6 %collective-permute-start.31 = (f32[4,2,48,384]{3,2,1,0:T(8,128)}, f32[4,2,48,384]{3,2,1,0:T(8,128)}, u32[]{:S(2)}, u32[]{:S(2)}) collective-permute-start(f32[4,2,48,384]{3,2,1,0:T(8,128)} %bitcast.33), channel_id=1, source_target_pairs={{0,8},{2,10},{4,12},{6,14},{8,0},{10,2},{12,4},{14,6},{16,24},{18,... | collective-permute-start | bytes 1769480 | tf_op jit(solution)/shard_map/ppermute | solution.py:58
  194.4 19.4 %collective-permute-start.30 = (f32[4,2,48,384]{3,2,1,0:T(8,128)}, f32[4,2,48,384]{3,2,1,0:T(8,128)}, u32[]{:S(2)}, u32[]{:S(2)}) collective-permute-start(f32[4,2,48,384]{3,2,1,0:T(8,128)} %bitcast.30), channel_id=1, source_target_pairs={{0,4},{2,6},{4,0},{6,2},{8,12},{10,14},{12,8},{14,10},{16,20},{18,... | collective-permute-start | bytes 1769480 | tf_op jit(solution)/shard_map/ppermute | solution.py:58
  195.0 24.5 %collective-permute-start.26 = (f32[2,48,1536]{2,1,0:T(8,128)}, f32[2,48,1536]{2,1,0:T(8,128)}, u32[]{:S(2)}, u32[]{:S(2)}) collective-permute-start(f32[2,48,1536]{2,1,0:T(8,128)} %bitcast_add_fusion.1), channel_id=1, source_target_pairs={{0,8},{2,10},{4,12},{6,14},{8,0},{10,2},{12,4},{14,6},{16,24},{18,... | collective-permute-start | bytes 1769480 | tf_op jit(solution)/shard_map/ppermute | solution.py:58
  219.5 13.0 %collective-permute-start.38 = (f32[11,768]{1,0:T(8,128)S(1)}, f32[11,768]{1,0:T(8,128)S(1)}, u32[]{:S(2)}, u32[]{:S(2)}) collective-permute-start(f32[11,768]{1,0:T(8,128)S(1)} %add.486), channel_id=1, source_target_pairs={{0,8},{2,10},{4,12},{6,14},{8,0},{10,2},{12,4},{14,6},{16,24},{18,... | collective-permute-start | bytes 101384 | tf_op jit(solution)/shard_map/ppermute | solution.py:58
  221.9 11.6 %collective-permute-start.37 = (f32[2,2,48,384]{3,2,1,0:T(8,128)}, f32[2,2,48,384]{3,2,1,0:T(8,128)S(1)}, u32[]{:S(2)}, u32[]{:S(2)}) collective-permute-start(f32[2,2,48,384]{3,2,1,0:T(8,128)} %bitcast_add_fusion.3), channel_id=1, source_target_pairs={{0,4},{2,6},{4,0},{6,2},{8,12},{10,14},{12,8},{14,10},{16,20},{18,... | collective-permute-start | bytes 884744 | tf_op jit(solution)/shard_map/ppermute | solution.py:58
  224.4 10.1 %collective-permute-start.36 = (f32[2,2,48,384]{3,2,1,0:T(8,128)}, f32[2,2,48,384]{3,2,1,0:T(8,128)}, u32[]{:S(2)}, u32[]{:S(2)}) collective-permute-start(f32[2,2,48,384]{3,2,1,0:T(8,128)} %bitcast_add_fusion.4), channel_id=1, source_target_pairs={{0,8},{2,10},{4,12},{6,14},{8,0},{10,2},{12,4},{14,6},{16,24},{18,... | collective-permute-start | bytes 884744 | tf_op jit(solution)/shard_map/ppermute | solution.py:58
  227.9 22.6 %collective-permute-start.35 = (f32[1,48,1536]{2,1,0:T(8,128)}, f32[1,48,1536]{2,1,0:T(8,128)}, u32[]{:S(2)}, u32[]{:S(2)}) collective-permute-start(f32[1,48,1536]{2,1,0:T(8,128)} %fusion.3), channel_id=1, source_target_pairs={{0,16},{2,18},{4,20},{6,22},{8,24},{10,26},{12,28},{14,30},{16,0},... | collective-permute-start | bytes 884744 | tf_op jit(solution)/shard_map/ppermute | solution.py:58
  233.1 21.4 %collective-permute-start.34 = (f32[1,48,1536]{2,1,0:T(8,128)}, f32[1,48,1536]{2,1,0:T(8,128)}, u32[]{:S(2)}, u32[]{:S(2)}) collective-permute-start(f32[1,48,1536]{2,1,0:T(8,128)} %fusion.4), channel_id=1, source_target_pairs={{0,16},{2,18},{4,20},{6,22},{8,24},{10,26},{12,28},{14,30},{16,0},... | collective-permute-start | bytes 884744 | tf_op jit(solution)/shard_map/ppermute | solution.py:58
  255.4 12.0 %collective-permute-start.41 = (f32[11,768]{1,0:T(8,128)S(1)}, f32[11,768]{1,0:T(8,128)S(1)}, u32[]{:S(2)}, u32[]{:S(2)}) collective-permute-start(f32[11,768]{1,0:T(8,128)S(1)} %add.506), channel_id=1, source_target_pairs={{0,16},{2,18},{4,20},{6,22},{8,24},{10,26},{12,28},{14,30},{16,0},... | collective-permute-start | bytes 101384 | tf_op jit(solution)/shard_map/ppermute | solution.py:58
  256.5 13.6 %collective-permute-start.40 = (f32[1,2,48,384]{3,2,1,0:T(8,128)S(1)}, f32[1,2,48,384]{3,2,1,0:T(8,128)S(1)}, u32[]{:S(2)}, u32[]{:S(2)}) collective-permute-start(f32[1,2,48,384]{3,2,1,0:T(8,128)S(1)} %fusion.12), channel_id=1, source_target_pairs={{0,16},{2,18},{4,20},{6,22},{8,24},{10,26},{12,28},{14,30},{16,0},... | collective-permute-start | bytes 442376 | tf_op jit(solution)/shard_map/ppermute | solution.py:58
  260.6 11.0 %collective-permute-start.39 = (f32[1,2,48,384]{3,2,1,0:T(8,128)S(1)}, f32[1,2,48,384]{3,2,1,0:T(8,128)S(1)}, u32[]{:S(2)}, u32[]{:S(2)}) collective-permute-start(f32[1,2,48,384]{3,2,1,0:T(8,128)S(1)} %fusion.13), channel_id=1, source_target_pairs={{0,16},{2,18},{4,20},{6,22},{8,24},{10,26},{12,28},{14,30},{16,0},... | collective-permute-start | bytes 442376 | tf_op jit(solution)/shard_map/ppermute | solution.py:58
  (33 other events, 116.6 us)

commit v3 on v2

--- a/solution.py
+++ b/solution.py
@@ -194,7 +194,7 @@
             shape((2 * pairs, rows, CLUSTER), BF16),
         ],
         scratch_shapes=[pltpu.VMEM((2, rows, rows), BF16)],
-        compiler_params=params_of(40),
+        compiler_params=params_of(58),
         cost_estimate=cost(12e9, 12e6),
         name="attend",
     )(x, weight, bias_cols, order_rows)
@@ -668,21 +668,35 @@
             down_sum.trade()
             up_sum.trade()
             sent = arrived([first, second], *sent)
-            first.extra = packed_of(grad_qv)
-            first.extra = first.extra + traded(first.extra, 1, n_items)
             first.trade()
             second.trade()
+            first.extra = packed_of(after(grad_qv, *sent))
+            first.extra = first.extra + traded(first.extra, 1, n_items)
+            first.more = traded(first.extra, 1 << first.bit, n_items)
             sums_all = [down_sum, up_sum, first, second]
-            for _ in bits[2:]:
+            for _ in bits[3:]:
                 arrived(sums_all)
                 for one in sums_all[::-1]:
                     one.trade()
-            summed_down, summed_up, *sent = arrived(sums_all)
+            arrived(sums_all)
             first.trade()
             second.trade()
+            together = traded(
+                jnp.concatenate([down_sum.send, up_sum.send]), 1 << down_sum.bit, n_items
+            )
+            together, first.got, second.got, first.more = at_once(
+                together, first.got, second.got, first.more
+            )
+            sent = [first.add(), second.add()]
+            rest = traded(jnp.concatenate(sent), 1 << first.bit, n_items)
+            first.more = traded(first.extra, 1 << first.bit, n_items)
+            down_sum.got, up_sum.got = together[:1], together[1:]
+            summed_down, summed_up = down_sum.add(), up_sum.add()
             far_part = after(far_part, summed_down, summed_up, *sent)
             grad_inputs = (d_pre + part + far_part).astype(BF16)
-            summed = arrived([first, second], grad_inputs)
+            rest, first.more, _ = at_once(rest, first.more, grad_inputs)
+            first.got, second.got = rest[:1], rest[1:]
+            summed = [first.add(), second.add()]
             summed_rest = [summed[c // 2][c % 2] for c in range(4)]
             packed = first.extra
         else:

time: 278 us -> 274 us (0.986)
  other arithmetic: 40.5 us -> 36.4 us
  local copies, waits for them, and re-layouts: 14.8 us -> 11.4 us
    unnamed x80 -> x72, local copies, waits for them, and re-layouts: 11.6 us -> 7.63 us
    reshape x1 -> x0, other arithmetic: 2.91 us -> none  [add(): return sum((self.part(term, []) for term in self.terms)).reshape(self.rest)]
    add x12 -> x11, other arithmetic: 24.4 us -> 22.1 us  [add(): self.send = sum((self.part(term, [1 - mine]) for term in self.terms))]
    ppermute x35 -> x33, waiting for transfers between devices: 67.5 us -> 69.6 us  [traded(): lax.ppermute(values, 'items', [(i, i ^ step) for i in range(n_items)])]
    ppermute x35 -> x33, starting transfers between devices: 29.1 us -> 28.3 us  [traded(): lax.ppermute(values, 'items', [(i, i ^ step) for i in range(n_items)])]
  transfers between devices with their start and end apart: 42 -> 40, of which waited for: 18 -> 19; matrix products, arithmetic and copies ran while one was open for 12% -> 12% of each run, Pallas kernels for 14% -> 15%
where the time goes in v3:
time: 274 us
  waiting for transfers between devices  99.7 us (36%)
  Pallas kernels  85.7 us (31%)
  starting transfers between devices  39.5 us (14%)
  other arithmetic  36.4 us (13%)
  local copies, waits for them, and re-layouts  11.4 us (4%)
    ppermute x33, waiting for transfers between devices, traded(): lax.ppermute(values, 'items', [(i, i ^ step) for i in range(n_items)])  69.6 us
    pallas_call x1, Pallas kernels, feed(): pl.pallas_call(functools.partial(feed_kernel, orders, tiles, len(late)),...  44.3 us
    ppermute x7, waiting for transfers between devices, swapped(): return lax.ppermute(values, 'heads', [(0, 1), (1, 0)])  30.1 us
    ppermute x33, starting transfers between devices, traded(): lax.ppermute(values, 'items', [(i, i ^ step) for i in range(n_items)])  28.3 us
    add x11, other arithmetic, add(): self.send = sum((self.part(term, [1 - mine]) for term in self.terms))  22.1 us
    pallas_call x1, Pallas kernels, attend_back(): pl.pallas_call(functools.partial(attend_back_kernel, orders), grid=(pairs...  20.1 us
    pallas_call x1, Pallas kernels, attend(): pl.pallas_call(attend_kernel, grid=(pairs,), in_specs=[whole(rows, width)...  15.4 us
    ppermute x7, starting transfers between devices, swapped(): return lax.ppermute(values, 'heads', [(0, 1), (1, 0)])  11.1 us
  transfers between devices with their start and end apart: 40, of which 19 were waited for; matrix products, arithmetic and copies ran while one was open for 12% of the time, Pallas kernels for 15%

profile of v3, /device:TPU:0, one launch (start us, length us, event | category | flops | bytes accessed | tf_op | source)
XLA Modules:
  0.0 273.7 jit_solution(10453313757785958307)
XLA Ops:
  1.7 3.0 %collective-permute-start = (f32[1,96,1536]{2,1,0:T(8,128)S(1)}, f32[1,96,1536]{2,1,0:T(8,128)S(1)}, u32[]{:S(2)}, u32[]{:S(2)}) collective-permute-start(f32[1,96,1536]{2,1,0:T(8,128)S(1)} %bitcast_convert_fusion.1), channel_id=1, source_target_pairs={{0,1},{1,0},{2,3},{3,2},{4,5},{5,4},{6,7},{7,6},{8,9},{9,8},{10,11... | collective-permute-start | bytes 1769480 | tf_op jit(solution)/shard_map/ppermute | solution.py:54
  7.4 15.4 %attend.1 = (bf16[384,1024]{1,0:T(8,128)(2,1)}, bf16[6,192,1024]{2,1,0:T(8,128)(2,1)}, bf16[6,1024,128]{2,1,0:T(8,128)(2,1)}) custom-call(bf16[1024,768]{1,0:T(8,128)(2,1)} %x_ref.2, bf16[3,768,384]{2,1,0:T(8,128)(2,1)} %w_ref.3, f32[384,2]{1,0:T(8,128)} %bitcast.148, s32[3,2,1024]{2,1,0:T(2,128)} %reshape_squeeze.3.row_ref), custom_call_target="tpu_custom_call" | custom-call | flops 12000000 | bytes 12000 | tf_op jit(solution)/shard_map/attend/pallas_call | solution.py:177
  22.9 1.9 slice_convert_fusion.1
  24.7 2.0 collective-permute-start.3
  26.8 1.6 collective-permute-start.1
  28.4 1.5 collective-permute-start.2
  30.0 1.6 collective-permute-done.4.refs_6_
  31.6 2.1 collective-permute-start.6
  33.7 1.5 collective-permute-start.8
  35.2 7.6 %collective-permute-done.3.far0_ref = f32[128,1024]{1,0:T(8,128)} collective-permute-done((f32[128,1024]{1,0:T(8,128)}, f32[128,1024]{1,0:T(8,128)}, u32[]{:S(2)}, u32[]{:S(2)}) %collective-permute-start.3) | collective-permute-done | bytes 524320 | tf_op jit(solution)/shard_map/ppermute | solution.py:54
  42.8 2.1 collective-permute-start.7
  45.4 9.1 %collective-permute-done.8.refs_9_ = f32[192,768]{1,0:T(8,128)S(1)} collective-permute-done((f32[192,768]{1,0:T(8,128)S(1)}, f32[192,768]{1,0:T(8,128)S(1)}, u32[]{:S(2)}, u32[]{:S(2)}) %collective-permute-start.8) | collective-permute-done | bytes 589856 | tf_op jit(solution)/shard_map/ppermute | solution.py:54
  54.5 2.2 collective-permute-done.7.refs_8_
  57.3 1.5 collective-permute-start.10
  59.7 1.4 collective-permute-start.9
  62.9 1.5 collective-permute-start.11
  65.0 5.9 %placed.1 = (bf16[768,1536]{1,0:T(8,128)(2,1)}, bf16[1536,768]{1,0:T(8,128)(2,1)}) custom-call(s32[6]{0:T(128)} %stack.42.slots_ref, f32[1,96,1536]{2,1,0:T(8,128)} %copy-done.17, f32[1,96,1536]{2,1,0:T(8,128)} %collective-permute-done.1.refs_1_, f32[1,96,1536]{2,1,0:T(8,128)} %collective-permute-done.2.refs_2_, f32[1,96,1536]{2,1,0:T(8,128)} %copy-done.21, ...), custom_call_target="tpu_custom_call" | custom-call | flops 1000 | bytes 1000 | tf_op jit(solution)/shard_map/placed/pallas_call | solution.py:371
  70.9 11.8 %collective-permute-done.11.refs_7_ = f32[1536]{0:T(1024)S(1)} collective-permute-done((f32[1536]{0:T(1024)S(1)}, f32[1536]{0:T(1024)S(1)}, u32[]{:S(2)}, u32[]{:S(2)}) %collective-permute-start.11) | collective-permute-done | bytes 6176 | tf_op jit(solution)/shard_map/ppermute | solution.py:54
  82.7 5.4 %collective-permute-done.5.refs_15_ = f32[1,96,1536]{2,1,0:T(8,128)} collective-permute-done((f32[1,96,1536]{2,1,0:T(8,128)}, f32[1,96,1536]{2,1,0:T(8,128)}, u32[]{:S(2)}, u32[]{:S(2)}) %collective-permute-start.5) | collective-permute-done | bytes 589856 | tf_op jit(solution)/shard_map/ppermute | solution.py:58
  92.0 44.3 %feed.1 = (bf16[1024,768]{1,0:T(8,128)(2,1)}, f32[1024,768]{1,0:T(8,128)}, bf16[1024,768]{1,0:T(8,128)(2,1)}, f32[8,768]{1,0:T(8,128)}, f32[1,1536]{1,0:T(1,128)...) custom-call(s32[1]{0:T(128)} %bitcast.core_ref, ...), custom_call_target="tpu_custom_call" | custom-call | flops 25000000 | bytes 30000 | tf_op jit(solution)/shard_map/feed/pallas_call | solution.py:535
  136.8 6.4 %collective-permute-done.21 = f32[8,48,1536]{2,1,0:T(8,128)S(1)} collective-permute-done((f32[8,48,1536]{2,1,0:T(8,128)}, f32[8,48,1536]{2,1,0:T(8,128)S(1)}, u32[]{:S(2)}, u32[]{:S(2)}) %collective-permute-start.21) | collective-permute-done | bytes 2359328 | tf_op jit(solution)/shard_map/ppermute | solution.py:58
  143.2 1.3 collective-permute-done.22
  144.5 3.0 %dynamic-slice_add_fusion = f32[1,2,2,48,1536]{4,3,2,1,0:T(8,128)} fusion(f32[2,2,2,48,1536]{4,3,2,1,0:T(8,128)} %bitcast.18, s32[]{:T(128)S(6)} %select_n.30, f32[2,2,2,48,1536]{4,3,2,1,0:T(8,128)} %bitcast.140), kind=kLoop, calls=%fused_computation.1 | loop fusion | flops 294912 | bytes 3538948 | tf_op jit(solution)/shard_map/add | solution.py:115
  147.6 1.5 collective-permute-start.25
  149.1 2.6 dynamic-slice_add_fusion.1
  151.7 1.5 collective-permute-start.24
  153.3 1.4 copy-done.7
  154.7 1.4 copy-done.8
  156.1 20.1 %attend_back.1 = (f32[1024,768]{1,0:T(8,128)S(1)}, f32[2,384]{1,0:T(2,128)S(1)}, f32[8,2,48,384]{3,2,1,0:T(8,128)S(1)}, f32[8,2,48,384]{3,2,1,0:T(8,128)}, f32[8...) custom-call(s32[1]{0:T(128)} %bitcast.core_ref, bf16[1024,768]{1,0:T(8,128)(2,1)S(1)} %copy-done, ...), custom_call_target="tpu_custom_call" | custom-call | flops 20000000 | bytes 20000 | tf_op jit(solution)/shard_map/attend_back/pallas_call | solution.py:282
  178.8 1.6 collective-permute-start.23
  180.3 2.3 bitcast_add_fusion
  182.7 2.5 bitcast_add_fusion.1
  185.2 1.9 dynamic-slice_add_fusion.2
  187.2 2.0 dynamic-slice_add_fusion.3
  195.5 12.5 %collective-permute-done.31 = f32[4,2,48,384]{3,2,1,0:T(8,128)} collective-permute-done((f32[4,2,48,384]{3,2,1,0:T(8,128)}, f32[4,2,48,384]{3,2,1,0:T(8,128)}, u32[]{:S(2)}, u32[]{:S(2)}) %collective-permute-start.31) | collective-permute-done | bytes 589856 | tf_op jit(solution)/shard_map/ppermute | solution.py:58
  208.4 11.6 %collective-permute-done.27 = f32[2,48,1536]{2,1,0:T(8,128)} collective-permute-done((f32[2,48,1536]{2,1,0:T(8,128)}, f32[2,48,1536]{2,1,0:T(8,128)}, u32[]{:S(2)}, u32[]{:S(2)}) %collective-permute-start.27) | collective-permute-done | bytes 589856 | tf_op jit(solution)/shard_map/ppermute | solution.py:58
  220.0 1.7 fusion.3
  222.6 2.6 collective-permute-start.34
  225.2 1.9 bitcast_add_fusion.3
  228.0 1.9 bitcast_add_fusion.4
  229.8 1.5 collective-permute-start.35
  232.0 12.6 %collective-permute-done.37 = f32[11,768]{1,0:T(8,128)S(1)} collective-permute-done((f32[11,768]{1,0:T(8,128)S(1)}, f32[11,768]{1,0:T(8,128)S(1)}, u32[]{:S(2)}, u32[]{:S(2)}) %collective-permute-start.37) | collective-permute-done | bytes 33824 | tf_op jit(solution)/shard_map/ppermute | solution.py:58
  244.6 6.1 %collective-permute-done.34 = f32[2,48,1536]{2,1,0:T(8,128)} collective-permute-done((f32[2,48,1536]{2,1,0:T(8,128)}, f32[2,48,1536]{2,1,0:T(8,128)}, u32[]{:S(2)}, u32[]{:S(2)}) %collective-permute-start.34) | collective-permute-done | bytes 589856 | tf_op jit(solution)/shard_map/ppermute | solution.py:58
  253.1 3.0 %collective-permute-start.38 = (f32[2,2,48,384]{3,2,1,0:T(8,128)S(1)}, f32[2,2,48,384]{3,2,1,0:T(8,128)}, u32[]{:S(2)}, u32[]{:S(2)}) collective-permute-start(f32[2,2,48,384]{3,2,1,0:T(8,128)S(1)} %pad_maximum_fusion.2), channel_id=1, source_target_pairs={{0,16},{2,18},{4,20},{6,22},{8,24},{10,26},{12,28},{14,30},{16,0},... | collective-permute-start | bytes 884744 | tf_op jit(solution)/shard_map/ppermute | solution.py:58
  256.0 2.8 %fusion.7 = (f32[1536,48]{0,1:T(8,128)}, f32[48,1536]{1,0:T(8,128)}) fusion(f32[2,48,1536]{2,1,0:T(8,128)} %collective-permute-done.34, f32[2,48,1536]{2,1,0:T(8,128)} %collective-permute-done.26, s32[]{:T(128)S(6)} %select_n.33, f32[2,2,48,1536]{3,2,1,0:T(8,128)} %bitcast.21, s32[]{:T(128)S(6)} %select_n.32, f32[2,2,2,48,1536]{4,3,2,1,0:T(8,128)} %bitcast.147, ...), kind=kLoop, calls=%fused_computation.24 | loop fusion | flops 589824 | bytes 3538956 | tf_op jit(solution)/shard_map/transpose | solution.py:723
  258.8 3.7 %add_convert_fusion = bf16[1024,768]{1,0:T(8,128)(2,1)} fusion(f32[1024,768]{1,0:T(8,128)} %collective-permute-done.23, f32[1024,768]{1,0:T(8,128)S(1)} %copy-done.14, f32[1024,768]{1,0:T(8,128)S(1)} %get-tuple-element.101), kind=kLoop, calls=%fused_computation | loop fusion | flops 2359296 | bytes 11010048 | tf_op jit(solution)/shard_map/convert_element_type | solution.py:696
  262.5 6.5 %collective-permute-done.38 = f32[2,2,48,384]{3,2,1,0:T(8,128)} collective-permute-done((f32[2,2,48,384]{3,2,1,0:T(8,128)S(1)}, f32[2,2,48,384]{3,2,1,0:T(8,128)}, u32[]{:S(2)}, u32[]{:S(2)}) %collective-permute-start.38) | collective-permute-done | bytes 294944 | tf_op jit(solution)/shard_map/ppermute | solution.py:58
  270.9 1.4 fusion.11
  (149 shorter events, 30.0 us)
Async XLA Ops:
  1.7 25.1 %collective-permute-start = (f32[1,96,1536]{2,1,0:T(8,128)S(1)}, f32[1,96,1536]{2,1,0:T(8,128)S(1)}, u32[]{:S(2)}, u32[]{:S(2)}) collective-permute-start(f32[1,96,1536]{2,1,0:T(8,128)S(1)} %bitcast_convert_fusion.1), channel_id=1, source_target_pairs={{0,1},{1,0},{2,3},{3,2},{4,5},{5,4},{6,7},{7,6},{8,9},{9,8},{10,11... | collective-permute-start | bytes 1769480 | tf_op jit(solution)/shard_map/ppermute | solution.py:54
  5.8 25.8 %collective-permute-start.4 = (f32[1,96,1536]{2,1,0:T(8,128)S(1)}, f32[1,96,1536]{2,1,0:T(8,128)}, u32[]{:S(2)}, u32[]{:S(2)}) collective-permute-start(f32[1,96,1536]{2,1,0:T(8,128)S(1)} %pad_maximum_fusion), channel_id=1, source_target_pairs={{0,1},{1,0},{2,3},{3,2},{4,5},{5,4},{6,7},{7,6},{8,9},{9,8},{10,11... | collective-permute-start | bytes 1769480 | tf_op jit(solution)/shard_map/ppermute | solution.py:54
  7.4 19.3 %copy-start.4 = (bf16[384,768]{1,0:T(8,128)(2,1)S(1)}, bf16[384,768]{1,0:T(8,128)(2,1)}, u32[]{:S(2)}) copy-start(bf16[384,768]{1,0:T(8,128)(2,1)} %ow_ref.1) | copy-start | bytes 1769476
  22.8 34.4 %copy-start.1 = (bf16[384,1024]{1,0:T(8,128)(2,1)S(1)}, bf16[384,1024]{1,0:T(8,128)(2,1)}, u32[]{:S(2)}) copy-start(bf16[384,1024]{1,0:T(8,128)(2,1)} %get-tuple-element.72.ctx_ref) | copy-start | bytes 2359300
  22.8 40.0 %copy-start.31 = (f32[1536]{0:T(1024)S(1)}, f32[1536]{0:T(1024)}, u32[]{:S(2)}) copy-start(f32[1536]{0:T(1024)} %refs_6_.1) | copy-start | bytes 18436
  24.7 18.1 %collective-permute-start.3 = (f32[128,1024]{1,0:T(8,128)}, f32[128,1024]{1,0:T(8,128)}, u32[]{:S(2)}, u32[]{:S(2)}) collective-permute-start(f32[128,1024]{1,0:T(8,128)} %slice_convert_fusion.1), channel_id=1, source_target_pairs={{0,1},{1,0},{2,3},{3,2},{4,5},{5,4},{6,7},{7,6},{8,9},{9,8},{10,11... | collective-permute-start | bytes 1572872 | tf_op jit(solution)/shard_map/ppermute | solution.py:54
  26.8 38.2 %copy-start.17 = (f32[1,96,1536]{2,1,0:T(8,128)}, f32[1,96,1536]{2,1,0:T(8,128)S(1)}, u32[]{:S(2)}) copy-start(f32[1,96,1536]{2,1,0:T(8,128)S(1)} %collective-permute-done.refs_0_) | copy-start | bytes 1769476
  26.8 18.1 %collective-permute-start.1 = (f32[1,96,1536]{2,1,0:T(8,128)S(1)}, f32[1,96,1536]{2,1,0:T(8,128)}, u32[]{:S(2)}, u32[]{:S(2)}) collective-permute-start(f32[1,96,1536]{2,1,0:T(8,128)S(1)} %collective-permute-done.refs_0_), channel_id=1, source_target_pairs={{0,8},{2,10},{4,12},{6,14},{8,0},{10,2},{12,4},{14,6},{16,24},{18,... | collective-permute-start | bytes 1769480 | tf_op jit(solution)/shard_map/ppermute | solution.py:58
  28.4 16.5 %collective-permute-start.2 = (f32[1,96,1536]{2,1,0:T(8,128)S(1)}, f32[1,96,1536]{2,1,0:T(8,128)}, u32[]{:S(2)}, u32[]{:S(2)}) collective-permute-start(f32[1,96,1536]{2,1,0:T(8,128)S(1)} %collective-permute-done.refs_0_), channel_id=1, source_target_pairs={{0,4},{2,6},{4,0},{6,2},{8,12},{10,14},{12,8},{14,10},{16,20},{18,... | collective-permute-start | bytes 1769480 | tf_op jit(solution)/shard_map/ppermute | solution.py:58
  31.6 22.9 %collective-permute-start.6 = (f32[1,96,1536]{2,1,0:T(8,128)}, f32[1,96,1536]{2,1,0:T(8,128)}, u32[]{:S(2)}, u32[]{:S(2)}) collective-permute-start(f32[1,96,1536]{2,1,0:T(8,128)} %collective-permute-done.4.refs_6_), channel_id=1, source_target_pairs={{0,8},{2,10},{4,12},{6,14},{8,0},{10,2},{12,4},{14,6},{16,24},{18,... | collective-permute-start | bytes 1769480 | tf_op jit(solution)/shard_map/ppermute | solution.py:58
  33.7 20.8 %collective-permute-start.8 = (f32[192,768]{1,0:T(8,128)S(1)}, f32[192,768]{1,0:T(8,128)S(1)}, u32[]{:S(2)}, u32[]{:S(2)}) collective-permute-start(f32[192,768]{1,0:T(8,128)S(1)} %dynamic-slice_convert_fusion), channel_id=1, source_target_pairs={{0,1},{1,0},{2,3},{3,2},{4,5},{5,4},{6,7},{7,6},{8,9},{9,8},{10,11... | collective-permute-start | bytes 1769480 | tf_op jit(solution)/shard_map/ppermute | solution.py:54
  42.8 13.9 %collective-permute-start.7 = (f32[1,96,1536]{2,1,0:T(8,128)}, f32[1,96,1536]{2,1,0:T(8,128)S(1)}, u32[]{:S(2)}, u32[]{:S(2)}) collective-permute-start(f32[1,96,1536]{2,1,0:T(8,128)} %collective-permute-done.4.refs_6_), channel_id=1, source_target_pairs={{0,4},{2,6},{4,0},{6,2},{8,12},{10,14},{12,8},{14,10},{16,20},{18,... | collective-permute-start | bytes 1769480 | tf_op jit(solution)/shard_map/ppermute | solution.py:58
  44.9 13.9 %collective-permute-start.15 = (f32[1,96,1536]{2,1,0:T(8,128)}, f32[1,96,1536]{2,1,0:T(8,128)S(1)}, u32[]{:S(2)}, u32[]{:S(2)}) collective-permute-start(f32[1,96,1536]{2,1,0:T(8,128)} %collective-permute-done.4.refs_6_), channel_id=1, source_target_pairs={{0,2},{2,0},{4,6},{6,4},{8,10},{10,8},{12,14},{14,12},{16,18},{18,... | collective-permute-start | bytes 1769480 | tf_op jit(solution)/shard_map/ppermute | solution.py:58
  44.9 13.9 %collective-permute-start.12 = (f32[1,96,1536]{2,1,0:T(8,128)S(1)}, f32[1,96,1536]{2,1,0:T(8,128)S(1)}, u32[]{:S(2)}, u32[]{:S(2)}) collective-permute-start(f32[1,96,1536]{2,1,0:T(8,128)S(1)} %collective-permute-done.refs_0_), channel_id=1, source_target_pairs={{0,2},{2,0},{4,6},{6,4},{8,10},{10,8},{12,14},{14,12},{16,18},{18,... | collective-permute-start | bytes 1769480 | tf_op jit(solution)/shard_map/ppermute | solution.py:58
  54.5 16.3 %copy-start.18 = (f32[192,768]{1,0:T(8,128)}, f32[192,768]{1,0:T(8,128)S(1)}, u32[]{:S(2)}) copy-start(f32[192,768]{1,0:T(8,128)S(1)} %collective-permute-done.8.refs_9_) | copy-start | bytes 1769476
  56.7 3.0 %collective-permute-start.16 = (f32[1,96,1536]{2,1,0:T(8,128)}, f32[1,96,1536]{2,1,0:T(8,128)S(1)}, u32[]{:S(2)}, u32[]{:S(2)}) collective-permute-start(f32[1,96,1536]{2,1,0:T(8,128)} %collective-permute-done.6.refs_7_), channel_id=1, source_target_pairs={{0,2},{2,0},{4,6},{6,4},{8,10},{10,8},{12,14},{14,12},{16,18},{18,... | collective-permute-start | bytes 1769480 | tf_op jit(solution)/shard_map/ppermute | solution.py:58
  56.7 4.5 %collective-permute-start.17 = (f32[1,96,1536]{2,1,0:T(8,128)S(1)}, f32[1,96,1536]{2,1,0:T(8,128)S(1)}, u32[]{:S(2)}, u32[]{:S(2)}) collective-permute-start(f32[1,96,1536]{2,1,0:T(8,128)S(1)} %collective-permute-done.7.refs_8_), channel_id=1, source_target_pairs={{0,2},{2,0},{4,6},{6,4},{8,10},{10,8},{12,14},{14,12},{16,18},{18,... | collective-permute-start | bytes 1769480 | tf_op jit(solution)/shard_map/ppermute | solution.py:58
  57.3 25.3 %collective-permute-start.10 = (f32[256,1024]{1,0:T(8,128)S(1)}, f32[256,1024]{1,0:T(8,128)S(1)}, u32[]{:S(2)}, u32[]{:S(2)}) collective-permute-start(f32[256,1024]{1,0:T(8,128)S(1)} %slice_convert_fusion), channel_id=1, source_target_pairs={{0,1},{1,0},{2,3},{3,2},{4,5},{5,4},{6,7},{7,6},{8,9},{9,8},{10,11... | collective-permute-start | bytes 3145736 | tf_op jit(solution)/shard_map/ppermute | solution.py:54
  58.8 3.0 %collective-permute-start.13 = (f32[1,96,1536]{2,1,0:T(8,128)}, f32[1,96,1536]{2,1,0:T(8,128)S(1)}, u32[]{:S(2)}, u32[]{:S(2)}) collective-permute-start(f32[1,96,1536]{2,1,0:T(8,128)} %collective-permute-done.1.refs_1_), channel_id=1, source_target_pairs={{0,2},{2,0},{4,6},{6,4},{8,10},{10,8},{12,14},{14,12},{16,18},{18,... | collective-permute-start | bytes 1769480 | tf_op jit(solution)/shard_map/ppermute | solution.py:58
  58.9 6.1 %collective-permute-start.14 = (f32[1,96,1536]{2,1,0:T(8,128)}, f32[1,96,1536]{2,1,0:T(8,128)}, u32[]{:S(2)}, u32[]{:S(2)}) collective-permute-start(f32[1,96,1536]{2,1,0:T(8,128)} %collective-permute-done.2.refs_2_), channel_id=1, source_target_pairs={{0,2},{2,0},{4,6},{6,4},{8,10},{10,8},{12,14},{14,12},{16,18},{18,... | collective-permute-start | bytes 1769480 | tf_op jit(solution)/shard_map/ppermute | solution.py:58
  59.7 22.9 %collective-permute-start.9 = (f32[1,96,1536]{2,1,0:T(8,128)}, f32[1,96,1536]{2,1,0:T(8,128)}, u32[]{:S(2)}, u32[]{:S(2)}) collective-permute-start(f32[1,96,1536]{2,1,0:T(8,128)} %collective-permute-done.6.refs_7_), channel_id=1, source_target_pairs={{0,4},{2,6},{4,0},{6,2},{8,12},{10,14},{12,8},{14,10},{16,20},{18,... | collective-permute-start | bytes 1769480 | tf_op jit(solution)/shard_map/ppermute | solution.py:58
  61.2 26.9 %collective-permute-start.5 = (f32[1,96,1536]{2,1,0:T(8,128)}, f32[1,96,1536]{2,1,0:T(8,128)}, u32[]{:S(2)}, u32[]{:S(2)}) collective-permute-start(f32[1,96,1536]{2,1,0:T(8,128)} %collective-permute-done.1.refs_1_), channel_id=1, source_target_pairs={{0,4},{2,6},{4,0},{6,2},{8,12},{10,14},{12,8},{14,10},{16,20},{18,... | collective-permute-start | bytes 1769480 | tf_op jit(solution)/shard_map/ppermute | solution.py:58
  62.9 19.8 %collective-permute-start.11 = (f32[1536]{0:T(1024)S(1)}, f32[1536]{0:T(1024)S(1)}, u32[]{:S(2)}, u32[]{:S(2)}) collective-permute-start(f32[1536]{0:T(1024)S(1)} %copy-done.31), channel_id=1, source_target_pairs={{0,1},{1,0},{2,3},{3,2},{4,5},{5,4},{6,7},{7,6},{8,9},{9,8},{10,11... | collective-permute-start | bytes 18440 | tf_op jit(solution)/shard_map/ppermute | solution.py:54
  65.0 24.2 %collective-permute-start.18 = (f32[192,768]{1,0:T(8,128)S(1)}, f32[192,768]{1,0:T(8,128)}, u32[]{:S(2)}, u32[]{:S(2)}) collective-permute-start(f32[192,768]{1,0:T(8,128)S(1)} %collective-permute-done.8.refs_9_), channel_id=1, source_target_pairs={{0,2},{2,0},{4,6},{6,4},{8,10},{10,8},{12,14},{14,12},{16,18},{18,... | collective-permute-start | bytes 1769480 | tf_op jit(solution)/shard_map/ppermute | solution.py:58
  88.1 2.2 collective-permute-start.19
  88.1 3.1 %collective-permute-start.20 = (f32[1,96,1536]{2,1,0:T(8,128)}, f32[1,96,1536]{2,1,0:T(8,128)S(1)}, u32[]{:S(2)}, u32[]{:S(2)}) collective-permute-start(f32[1,96,1536]{2,1,0:T(8,128)} %collective-permute-done.9.refs_17_), channel_id=1, source_target_pairs={{0,2},{2,0},{4,6},{6,4},{8,10},{10,8},{12,14},{14,12},{16,18},{18,... | collective-permute-start | bytes 1769480 | tf_op jit(solution)/shard_map/ppermute | solution.py:58
  92.0 61.2 %copy-start.13 = (s32[3,2,1024]{2,1,0:T(2,128)S(1)}, s32[3,2,1024]{2,1,0:T(2,128)}, u32[]{:S(2)}) copy-start(s32[3,2,1024]{2,1,0:T(2,128)} %reshape_squeeze.3.row_ref) | copy-start | bytes 73732
  136.2 7.0 %collective-permute-start.21 = (f32[8,48,1536]{2,1,0:T(8,128)}, f32[8,48,1536]{2,1,0:T(8,128)S(1)}, u32[]{:S(2)}, u32[]{:S(2)}) collective-permute-start(f32[8,48,1536]{2,1,0:T(8,128)} %get-tuple-element.93), channel_id=1, source_target_pairs={{0,2},{2,0},{4,6},{6,4},{8,10},{10,8},{12,14},{14,12},{16,18},{18,... | collective-permute-start | bytes 7077896 | tf_op jit(solution)/shard_map/ppermute | solution.py:58
  136.4 8.1 %collective-permute-start.22 = (f32[8,48,1536]{2,1,0:T(8,128)}, f32[8,48,1536]{2,1,0:T(8,128)}, u32[]{:S(2)}, u32[]{:S(2)}) collective-permute-start(f32[8,48,1536]{2,1,0:T(8,128)} %get-tuple-element.94), channel_id=1, source_target_pairs={{0,2},{2,0},{4,6},{6,4},{8,10},{10,8},{12,14},{14,12},{16,18},{18,... | collective-permute-start | bytes 7077896 | tf_op jit(solution)/shard_map/ppermute | solution.py:58
  147.6 32.8 %collective-permute-start.25 = (f32[4,48,1536]{2,1,0:T(8,128)}, f32[4,48,1536]{2,1,0:T(8,128)}, u32[]{:S(2)}, u32[]{:S(2)}) collective-permute-start(f32[4,48,1536]{2,1,0:T(8,128)} %bitcast.19), channel_id=1, source_target_pairs={{0,8},{2,10},{4,12},{6,14},{8,0},{10,2},{12,4},{14,6},{16,24},{18,... | collective-permute-start | bytes 3538952 | tf_op jit(solution)/shard_map/ppermute | solution.py:58
  151.7 28.7 %collective-permute-start.24 = (f32[4,48,1536]{2,1,0:T(8,128)}, f32[4,48,1536]{2,1,0:T(8,128)}, u32[]{:S(2)}, u32[]{:S(2)}) collective-permute-start(f32[4,48,1536]{2,1,0:T(8,128)} %bitcast.16), channel_id=1, source_target_pairs={{0,4},{2,6},{4,0},{6,2},{8,12},{10,14},{12,8},{14,10},{16,20},{18,... | collective-permute-start | bytes 3538952 | tf_op jit(solution)/shard_map/ppermute | solution.py:58
  156.1 22.7 %copy-start.33 = (f32[1,1536]{1,0:T(1,128)S(1)}, f32[1,1536]{1,0:T(1,128)}, u32[]{:S(2)}) copy-start(f32[1,1536]{1,0:T(1,128)} %get-tuple-element.111) | copy-start | bytes 18436
  178.2 7.0 %collective-permute-start.28 = (f32[8,2,48,384]{3,2,1,0:T(8,128)}, f32[8,2,48,384]{3,2,1,0:T(8,128)}, u32[]{:S(2)}, u32[]{:S(2)}) collective-permute-start(f32[8,2,48,384]{3,2,1,0:T(8,128)} %get-tuple-element.105), channel_id=1, source_target_pairs={{0,2},{2,0},{4,6},{6,4},{8,10},{10,8},{12,14},{14,12},{16,18},{18,... | collective-permute-start | bytes 3538952 | tf_op jit(solution)/shard_map/ppermute | solution.py:58
  178.2 7.0 %collective-permute-start.29 = (f32[8,2,48,384]{3,2,1,0:T(8,128)}, f32[8,2,48,384]{3,2,1,0:T(8,128)}, u32[]{:S(2)}, u32[]{:S(2)}) collective-permute-start(f32[8,2,48,384]{3,2,1,0:T(8,128)} %get-tuple-element.106), channel_id=1, source_target_pairs={{0,2},{2,0},{4,6},{6,4},{8,10},{10,8},{12,14},{14,12},{16,18},{18,... | collective-permute-start | bytes 3538952 | tf_op jit(solution)/shard_map/ppermute | solution.py:58
  178.8 80.0 %collective-permute-start.23 = (f32[1024,768]{1,0:T(8,128)S(1)}, f32[1024,768]{1,0:T(8,128)}, u32[]{:S(2)}, u32[]{:S(2)}) collective-permute-start(f32[1024,768]{1,0:T(8,128)S(1)} %get-tuple-element.101), channel_id=1, source_target_pairs={{0,1},{1,0},{2,3},{3,2},{4,5},{5,4},{6,7},{7,6},{8,9},{9,8},{10,11... | collective-permute-start | bytes 9437192 | tf_op jit(solution)/shard_map/ppermute | solution.py:54
  189.1 1.3 collective-permute-start.32
  190.4 4.5 %collective-permute-start.33 = (f32[11,768]{1,0:T(8,128)S(1)}, f32[11,768]{1,0:T(8,128)S(1)}, u32[]{:S(2)}, u32[]{:S(2)}) collective-permute-start(f32[11,768]{1,0:T(8,128)S(1)} %fusion.14), channel_id=1, source_target_pairs={{0,4},{2,6},{4,0},{6,2},{8,12},{10,14},{12,8},{14,10},{16,20},{18,... | collective-permute-start | bytes 101384 | tf_op jit(solution)/shard_map/ppermute | solution.py:58
  191.4 16.5 %collective-permute-start.31 = (f32[4,2,48,384]{3,2,1,0:T(8,128)}, f32[4,2,48,384]{3,2,1,0:T(8,128)}, u32[]{:S(2)}, u32[]{:S(2)}) collective-permute-start(f32[4,2,48,384]{3,2,1,0:T(8,128)} %bitcast.33), channel_id=1, source_target_pairs={{0,8},{2,10},{4,12},{6,14},{8,0},{10,2},{12,4},{14,6},{16,24},{18,... | collective-permute-start | bytes 1769480 | tf_op jit(solution)/shard_map/ppermute | solution.py:58
  191.9 16.6 %collective-permute-start.30 = (f32[4,2,48,384]{3,2,1,0:T(8,128)}, f32[4,2,48,384]{3,2,1,0:T(8,128)}, u32[]{:S(2)}, u32[]{:S(2)}) collective-permute-start(f32[4,2,48,384]{3,2,1,0:T(8,128)} %bitcast.30), channel_id=1, source_target_pairs={{0,4},{2,6},{4,0},{6,2},{8,12},{10,14},{12,8},{14,10},{16,20},{18,... | collective-permute-start | bytes 1769480 | tf_op jit(solution)/shard_map/ppermute | solution.py:58
  193.0 27.0 %collective-permute-start.27 = (f32[2,48,1536]{2,1,0:T(8,128)}, f32[2,48,1536]{2,1,0:T(8,128)}, u32[]{:S(2)}, u32[]{:S(2)}) collective-permute-start(f32[2,48,1536]{2,1,0:T(8,128)} %bitcast_add_fusion), channel_id=1, source_target_pairs={{0,4},{2,6},{4,0},{6,2},{8,12},{10,14},{12,8},{14,10},{16,20},{18,... | collective-permute-start | bytes 1769480 | tf_op jit(solution)/shard_map/ppermute | solution.py:58
  194.9 27.6 %copy-start.28 = (f32[11,768]{1,0:T(8,128)}, f32[11,768]{1,0:T(8,128)S(1)}, u32[]{:S(2)}) copy-start(f32[11,768]{1,0:T(8,128)S(1)} %collective-permute-done.33) | copy-start | bytes 101380
  194.9 25.1 %collective-permute-start.26 = (f32[2,48,1536]{2,1,0:T(8,128)}, f32[2,48,1536]{2,1,0:T(8,128)}, u32[]{:S(2)}, u32[]{:S(2)}) collective-permute-start(f32[2,48,1536]{2,1,0:T(8,128)} %bitcast_add_fusion.1), channel_id=1, source_target_pairs={{0,8},{2,10},{4,12},{6,14},{8,0},{10,2},{12,4},{14,6},{16,24},{18,... | collective-permute-start | bytes 1769480 | tf_op jit(solution)/shard_map/ppermute | solution.py:58
  222.6 28.1 %collective-permute-start.34 = (f32[2,48,1536]{2,1,0:T(8,128)}, f32[2,48,1536]{2,1,0:T(8,128)}, u32[]{:S(2)}, u32[]{:S(2)}) collective-permute-start(f32[2,48,1536]{2,1,0:T(8,128)} %pad_maximum_fusion.1), channel_id=1, source_target_pairs={{0,16},{2,18},{4,20},{6,22},{8,24},{10,26},{12,28},{14,30},{16,0},... | collective-permute-start | bytes 1769480 | tf_op jit(solution)/shard_map/ppermute | solution.py:58
  227.1 17.5 %collective-permute-start.36 = (f32[2,2,48,384]{3,2,1,0:T(8,128)}, f32[2,2,48,384]{3,2,1,0:T(8,128)S(1)}, u32[]{:S(2)}, u32[]{:S(2)}) collective-permute-start(f32[2,2,48,384]{3,2,1,0:T(8,128)} %bitcast_add_fusion.3), channel_id=1, source_target_pairs={{0,4},{2,6},{4,0},{6,2},{8,12},{10,14},{12,8},{14,10},{16,20},{18,... | collective-permute-start | bytes 884744 | tf_op jit(solution)/shard_map/ppermute | solution.py:58
  229.8 14.7 %collective-permute-start.35 = (f32[2,2,48,384]{3,2,1,0:T(8,128)}, f32[2,2,48,384]{3,2,1,0:T(8,128)}, u32[]{:S(2)}, u32[]{:S(2)}) collective-permute-start(f32[2,2,48,384]{3,2,1,0:T(8,128)} %bitcast_add_fusion.4), channel_id=1, source_target_pairs={{0,8},{2,10},{4,12},{6,14},{8,0},{10,2},{12,4},{14,6},{16,24},{18,... | collective-permute-start | bytes 884744 | tf_op jit(solution)/shard_map/ppermute | solution.py:58
  231.3 13.2 %collective-permute-start.37 = (f32[11,768]{1,0:T(8,128)S(1)}, f32[11,768]{1,0:T(8,128)S(1)}, u32[]{:S(2)}, u32[]{:S(2)}) collective-permute-start(f32[11,768]{1,0:T(8,128)S(1)} %add.486), channel_id=1, source_target_pairs={{0,8},{2,10},{4,12},{6,14},{8,0},{10,2},{12,4},{14,6},{16,24},{18,... | collective-permute-start | bytes 101384 | tf_op jit(solution)/shard_map/ppermute | solution.py:58
  250.7 11.8 %collective-permute-start.39 = (f32[11,768]{1,0:T(8,128)S(1)}, f32[11,768]{1,0:T(8,128)S(1)}, u32[]{:S(2)}, u32[]{:S(2)}) collective-permute-start(f32[11,768]{1,0:T(8,128)S(1)} %add.506), channel_id=1, source_target_pairs={{0,16},{2,18},{4,20},{6,22},{8,24},{10,26},{12,28},{14,30},{16,0},... | collective-permute-start | bytes 101384 | tf_op jit(solution)/shard_map/ppermute | solution.py:58
  253.1 15.9 %collective-permute-start.38 = (f32[2,2,48,384]{3,2,1,0:T(8,128)S(1)}, f32[2,2,48,384]{3,2,1,0:T(8,128)}, u32[]{:S(2)}, u32[]{:S(2)}) collective-permute-start(f32[2,2,48,384]{3,2,1,0:T(8,128)S(1)} %pad_maximum_fusion.2), channel_id=1, source_target_pairs={{0,16},{2,18},{4,20},{6,22},{8,24},{10,26},{12,28},{14,30},{16,0},... | collective-permute-start | bytes 884744 | tf_op jit(solution)/shard_map/ppermute | solution.py:58
  (27 other events, 96.4 us)

commit v4 on v3

--- a/solution.py
+++ b/solution.py
@@ -441,7 +441,7 @@
 
 
 def feed_kernel(
-    orders, tiles, late_count, core_ref, slots_ref, x_ref, cot_ref, ctx_ref, far0_ref, far1_ref, *refs
+    orders, tiles, late_count, core_ref, slots_ref, x_ref, cot_ref, ctx_ref, far_ctx_ref, *refs
 ):
     vector_refs, refs = refs[:8], refs[8:]
     out_hbm, near_half_hbm, far_half_hbm, up_hbm, down_hbm, far_up_hbm, far_down_hbm, *refs = refs
@@ -492,7 +492,7 @@
     def _():
         here = pl.ds(pl.multiple_of(step * tile, tile), tile)
         feed_rows(
-            x_ref, cot_ref, ctx_ref, (far0_ref, far1_ref), vector_refs, ready, out_s, far_out_s, up_s,
+            x_ref, cot_ref, ctx_ref, (far_ctx_ref,), vector_refs, ready, out_s, far_out_s, up_s,
             down_s, far_up_s, far_down_s, mixed_ref, d_pre_ref, d_attn_ref, sums_ref, up_sums_ref, nb_s, act_s,
             d_feed_s, d_hidden_s, here,
         )
@@ -610,9 +610,7 @@
         x = after(hidden_in, up_piece, down_piece)
         context, moved, probs = attend(x, qkv_weight, qv_bias.T, order_rows)
         pairs = order_rows.shape[0]
-        far_context = [
-            swapped(context[:128].astype(F32)), swapped(context[128:].astype(F32))
-        ]
+        far_context = [swapped(context.astype(F32))]
         out_piece = lax.dynamic_slice_in_dim(out_weight, core * half, half, 0).astype(F32)
 
         trade = lambda values, step: traded(values, step, n_items)
@@ -620,18 +618,16 @@
         a0 = after(far_a, context)
         a4, a2 = trade(a0, 4), trade(a0, 2)
         b0 = after(far_b, a0)
-        far_half = swapped(after(out_piece, b0))
         b4, b2 = trade(b0, 4), trade(b0, 2)
-        a4, a2, far_context[0], _ = at_once(a4, a2, far_context[0], b0)
+        a4, a2, _ = at_once(a4, a2, b0)
         a6 = trade(a4, 2)
-        b4, b2, far_half, _ = at_once(b4, b2, far_half, a4)
+        b4, b2, a6, far_context[0] = at_once(b4, b2, a6, far_context[0])
         b6 = trade(b4, 2)
+        far_half = swapped(after(out_piece, b4))
         all_slots = lambda ks: jnp.stack([place ^ k for k in ks]).astype(jnp.int32)
         come = [part for one in ((a0, a4, a2), (b0, b4, b2)) for part in (*one, *(trade(p, 1) for p in one))]
         far_up, far_down = placed(all_slots((0, 4, 2, 1, 5, 3)), come, group)
-        a6, b6, far_context[1], far_bias, far_up = at_once(
-            a6, b6, far_context[1], far_bias, far_up
-        )
+        b6, far_half, far_bias, far_up = at_once(b6, far_half, far_bias, far_up)
         other_half = trade(far_half, 1)
         late, slots = [a6, trade(a6, 1), b6, trade(b6, 1)], all_slots((6, 7))
         which = core.astype(jnp.int32).reshape(1)

time: 274 us -> 271 us (0.989)
    ppermute x7 -> x6, waiting for transfers between devices: 30.1 us -> 11.8 us  [swapped(): return lax.ppermute(values, 'heads', [(0, 1), (1, 0)])]
    ppermute x33, waiting for transfers between devices: 69.6 us -> 85.2 us  [traded(): lax.ppermute(values, 'items', [(i, i ^ step) for i in range(n_items)])]
    ppermute x7 -> x6, starting transfers between devices: 11.1 us -> 8.61 us  [swapped(): return lax.ppermute(values, 'heads', [(0, 1), (1, 0)])]
    unnamed x72 -> x62, local copies, waits for them, and re-layouts: 7.63 us -> 6.66 us
  transfers between devices with their start and end apart: 40 -> 39, of which waited for: 19 -> 20; matrix products, arithmetic and copies ran while one was open for 12% -> 13% of each run, Pallas kernels for 15% -> 15%
where the time goes in v4:
time: 271 us; the launch traced here: 270 us
  waiting for transfers between devices  97 us (36%)
  Pallas kernels  85.6 us (32%)
  other arithmetic  38.6 us (14%)
  starting transfers between devices  37.6 us (14%)
  local copies, waits for them, and re-layouts  10.4 us (4%)
    ppermute x33, waiting for transfers between devices, traded(): lax.ppermute(values, 'items', [(i, i ^ step) for i in range(n_items)])  85.2 us
    pallas_call x1, Pallas kernels, feed(): pl.pallas_call(functools.partial(feed_kernel, orders, tiles, len(late)),...  44.2 us
    ppermute x33, starting transfers between devices, traded(): lax.ppermute(values, 'items', [(i, i ^ step) for i in range(n_items)])  29 us
    add x11, other arithmetic, add(): self.send = sum((self.part(term, [1 - mine]) for term in self.terms))  22 us
    pallas_call x1, Pallas kernels, attend_back(): pl.pallas_call(functools.partial(attend_back_kernel, orders), grid=(pairs...  20.2 us
    pallas_call x1, Pallas kernels, attend(): pl.pallas_call(attend_kernel, grid=(pairs,), in_specs=[whole(rows, width)...  15.4 us
    ppermute x6, waiting for transfers between devices, swapped(): return lax.ppermute(values, 'heads', [(0, 1), (1, 0)])  11.8 us
    ppermute x6, starting transfers between devices, swapped(): return lax.ppermute(values, 'heads', [(0, 1), (1, 0)])  8.61 us
  transfers between devices with their start and end apart: 39, of which 20 were waited for; matrix products, arithmetic and copies ran while one was open for 13% of the time, Pallas kernels for 15%

profile of v4, /device:TPU:0, one launch (start us, length us, event | category | flops | bytes accessed | tf_op | source)
XLA Modules:
  0.0 270.1 jit_solution(7346296005557097915)
XLA Ops:
  1.7 3.0 %collective-permute-start.1 = (f32[1,96,1536]{2,1,0:T(8,128)S(1)}, f32[1,96,1536]{2,1,0:T(8,128)S(1)}, u32[]{:S(2)}, u32[]{:S(2)}) collective-permute-start(f32[1,96,1536]{2,1,0:T(8,128)S(1)} %bitcast_convert_fusion.1), channel_id=1, source_target_pairs={{0,1},{1,0},{2,3},{3,2},{4,5},{5,4},{6,7},{7,6},{8,9},{9,8},{10,11... | collective-permute-start | bytes 1769480 | tf_op jit(solution)/shard_map/ppermute | solution.py:54
  8.2 15.4 %attend.1 = (bf16[384,1024]{1,0:T(8,128)(2,1)}, bf16[6,192,1024]{2,1,0:T(8,128)(2,1)}, bf16[6,1024,128]{2,1,0:T(8,128)(2,1)}) custom-call(bf16[1024,768]{1,0:T(8,128)(2,1)} %x_ref.2, bf16[3,768,384]{2,1,0:T(8,128)(2,1)} %w_ref.3, f32[384,2]{1,0:T(8,128)} %bitcast.148, s32[3,2,1024]{2,1,0:T(2,128)} %reshape_squeeze.3.row_ref), custom_call_target="tpu_custom_call" | custom-call | flops 12000000 | bytes 12000 | tf_op jit(solution)/shard_map/attend/pallas_call | solution.py:177
  23.6 2.5 convert_element_type.11
  26.1 2.0 collective-permute-start.7
  28.0 1.6 collective-permute-start.4
  29.6 1.5 collective-permute-start.5
  31.6 2.1 collective-permute-start.2
  33.7 1.5 collective-permute-start.3
  35.3 9.2 %collective-permute-done.4.refs_1_ = f32[1,96,1536]{2,1,0:T(8,128)} collective-permute-done((f32[1,96,1536]{2,1,0:T(8,128)S(1)}, f32[1,96,1536]{2,1,0:T(8,128)}, u32[]{:S(2)}, u32[]{:S(2)}) %collective-permute-start.4) | collective-permute-done | bytes 589856 | tf_op jit(solution)/shard_map/ppermute | solution.py:58
  44.4 1.5 collective-permute-done.5.refs_2_
  45.9 1.5 collective-permute-start.6
  47.4 7.6 %collective-permute-done.2.refs_7_ = f32[1,96,1536]{2,1,0:T(8,128)} collective-permute-done((f32[1,96,1536]{2,1,0:T(8,128)}, f32[1,96,1536]{2,1,0:T(8,128)}, u32[]{:S(2)}, u32[]{:S(2)}) %collective-permute-start.2) | collective-permute-done | bytes 589856 | tf_op jit(solution)/shard_map/ppermute | solution.py:58
  55.0 3.6 %collective-permute-done.3.refs_8_ = f32[1,96,1536]{2,1,0:T(8,128)} collective-permute-done((f32[1,96,1536]{2,1,0:T(8,128)}, f32[1,96,1536]{2,1,0:T(8,128)}, u32[]{:S(2)}, u32[]{:S(2)}) %collective-permute-start.3) | collective-permute-done | bytes 589856 | tf_op jit(solution)/shard_map/ppermute | solution.py:58
  58.6 5.7 %collective-permute-done.7.far_ctx_ref = f32[384,1024]{1,0:T(8,128)S(1)} collective-permute-done((f32[384,1024]{1,0:T(8,128)}, f32[384,1024]{1,0:T(8,128)S(1)}, u32[]{:S(2)}, u32[]{:S(2)}) %collective-permute-start.7) | collective-permute-done | bytes 1572896 | tf_op jit(solution)/shard_map/ppermute | solution.py:54
  65.3 3.6 %collective-permute-done.6.refs_15_ = f32[1,96,1536]{2,1,0:T(8,128)S(1)} collective-permute-done((f32[1,96,1536]{2,1,0:T(8,128)}, f32[1,96,1536]{2,1,0:T(8,128)S(1)}, u32[]{:S(2)}, u32[]{:S(2)}) %collective-permute-start.6) | collective-permute-done | bytes 589856 | tf_op jit(solution)/shard_map/ppermute | solution.py:58
  69.9 1.5 collective-permute-start.8
  71.4 1.5 collective-permute-start.10
  73.6 5.9 %placed.1 = (bf16[768,1536]{1,0:T(8,128)(2,1)}, bf16[1536,768]{1,0:T(8,128)(2,1)}) custom-call(s32[6]{0:T(128)} %stack.42.slots_ref, f32[1,96,1536]{2,1,0:T(8,128)} %copy-done.16, f32[1,96,1536]{2,1,0:T(8,128)} %collective-permute-done.4.refs_1_, f32[1,96,1536]{2,1,0:T(8,128)} %copy-done.18, f32[1,96,1536]{2,1,0:T(8,128)} %collective-permute-done.11.refs_3_, ...), custom_call_target="tpu_custom_call" | custom-call | flops 1000 | bytes 1000 | tf_op jit(solution)/shard_map/placed/pallas_call | solution.py:371
  79.5 5.6 %collective-permute-done.10.refs_7_ = f32[1536]{0:T(1024)S(1)} collective-permute-done((f32[1536]{0:T(1024)S(1)}, f32[1536]{0:T(1024)S(1)}, u32[]{:S(2)}, u32[]{:S(2)}) %collective-permute-start.10) | collective-permute-done | bytes 6176 | tf_op jit(solution)/shard_map/ppermute | solution.py:54
  86.3 1.7 collective-permute-done.17.refs_10_
  89.1 44.2 %feed.1 = (bf16[1024,768]{1,0:T(8,128)(2,1)}, f32[1024,768]{1,0:T(8,128)}, bf16[1024,768]{1,0:T(8,128)(2,1)}, f32[8,768]{1,0:T(8,128)}, f32[1,1536]{1,0:T(1,128)...) custom-call(s32[1]{0:T(128)} %bitcast.core_ref, ...), custom_call_target="tpu_custom_call" | custom-call | flops 25000000 | bytes 30000 | tf_op jit(solution)/shard_map/feed/pallas_call | solution.py:535
  133.9 6.3 %collective-permute-done.20 = f32[8,48,1536]{2,1,0:T(8,128)S(1)} collective-permute-done((f32[8,48,1536]{2,1,0:T(8,128)}, f32[8,48,1536]{2,1,0:T(8,128)S(1)}, u32[]{:S(2)}, u32[]{:S(2)}) %collective-permute-start.20) | collective-permute-done | bytes 2359328 | tf_op jit(solution)/shard_map/ppermute | solution.py:58
  141.6 3.0 %dynamic-slice_add_fusion = f32[1,2,2,48,1536]{4,3,2,1,0:T(8,128)} fusion(f32[2,2,2,48,1536]{4,3,2,1,0:T(8,128)} %bitcast.18, s32[]{:T(128)S(6)} %select_n.30, f32[2,2,2,48,1536]{4,3,2,1,0:T(8,128)} %bitcast.140), kind=kLoop, calls=%fused_computation.1 | loop fusion | flops 294912 | bytes 3538948 | tf_op jit(solution)/shard_map/add | solution.py:115
  145.0 2.6 dynamic-slice_add_fusion.1
  147.6 1.6 collective-permute-start.23
  152.1 20.2 %attend_back.1 = (f32[1024,768]{1,0:T(8,128)S(1)}, f32[2,384]{1,0:T(2,128)S(1)}, f32[8,2,48,384]{3,2,1,0:T(8,128)S(1)}, f32[8,2,48,384]{3,2,1,0:T(8,128)}, f32[8...) custom-call(s32[1]{0:T(128)} %bitcast.core_ref, bf16[1024,768]{1,0:T(8,128)(2,1)S(1)} %copy-done, ...), custom_call_target="tpu_custom_call" | custom-call | flops 20000000 | bytes 20000 | tf_op jit(solution)/shard_map/attend_back/pallas_call | solution.py:282
  174.9 1.6 collective-permute-start.22
  176.4 2.3 bitcast_add_fusion
  178.7 2.5 bitcast_add_fusion.1
  181.2 1.9 dynamic-slice_add_fusion.2
  183.2 2.0 dynamic-slice_add_fusion.3
  187.4 1.6 collective-permute-start.30
  190.9 1.7 collective-permute-start.25
  192.6 11.2 %collective-permute-done.30 = f32[4,2,48,384]{3,2,1,0:T(8,128)} collective-permute-done((f32[4,2,48,384]{3,2,1,0:T(8,128)}, f32[4,2,48,384]{3,2,1,0:T(8,128)}, u32[]{:S(2)}, u32[]{:S(2)}) %collective-permute-start.30) | collective-permute-done | bytes 589856 | tf_op jit(solution)/shard_map/ppermute | solution.py:58
  203.9 1.6 collective-permute-done.29
  205.5 11.2 %collective-permute-done.26 = f32[2,48,1536]{2,1,0:T(8,128)} collective-permute-done((f32[2,48,1536]{2,1,0:T(8,128)}, f32[2,48,1536]{2,1,0:T(8,128)}, u32[]{:S(2)}, u32[]{:S(2)}) %collective-permute-start.26) | collective-permute-done | bytes 589856 | tf_op jit(solution)/shard_map/ppermute | solution.py:58
  216.7 1.7 fusion.3
  219.3 2.6 collective-permute-start.33
  221.9 1.9 bitcast_add_fusion.3
  225.0 1.9 bitcast_add_fusion.4
  227.4 1.6 collective-permute-start.36
  229.0 12.0 %collective-permute-done.36 = f32[11,768]{1,0:T(8,128)S(1)} collective-permute-done((f32[11,768]{1,0:T(8,128)S(1)}, f32[11,768]{1,0:T(8,128)S(1)}, u32[]{:S(2)}, u32[]{:S(2)}) %collective-permute-start.36) | collective-permute-done | bytes 33824 | tf_op jit(solution)/shard_map/ppermute | solution.py:58
  241.0 6.1 %collective-permute-done.33 = f32[2,48,1536]{2,1,0:T(8,128)} collective-permute-done((f32[2,48,1536]{2,1,0:T(8,128)}, f32[2,48,1536]{2,1,0:T(8,128)}, u32[]{:S(2)}, u32[]{:S(2)}) %collective-permute-start.33) | collective-permute-done | bytes 589856 | tf_op jit(solution)/shard_map/ppermute | solution.py:58
  249.5 3.0 %collective-permute-start.37 = (f32[2,2,48,384]{3,2,1,0:T(8,128)S(1)}, f32[2,2,48,384]{3,2,1,0:T(8,128)}, u32[]{:S(2)}, u32[]{:S(2)}) collective-permute-start(f32[2,2,48,384]{3,2,1,0:T(8,128)S(1)} %pad_maximum_fusion.2), channel_id=1, source_target_pairs={{0,16},{2,18},{4,20},{6,22},{8,24},{10,26},{12,28},{14,30},{16,0},... | collective-permute-start | bytes 884744 | tf_op jit(solution)/shard_map/ppermute | solution.py:58
  252.4 2.8 %fusion.7 = (f32[1536,48]{0,1:T(8,128)}, f32[48,1536]{1,0:T(8,128)}) fusion(f32[2,48,1536]{2,1,0:T(8,128)} %collective-permute-done.33, f32[2,48,1536]{2,1,0:T(8,128)} %collective-permute-done.25, s32[]{:T(128)S(6)} %select_n.33, f32[2,2,48,1536]{3,2,1,0:T(8,128)} %bitcast.21, s32[]{:T(128)S(6)} %select_n.32, f32[2,2,2,48,1536]{4,3,2,1,0:T(8,128)} %bitcast.147, ...), kind=kLoop, calls=%fused_computation.23 | loop fusion | flops 589824 | bytes 3538956 | tf_op jit(solution)/shard_map/transpose | solution.py:719
  255.2 3.7 %add_convert_fusion = bf16[1024,768]{1,0:T(8,128)(2,1)} fusion(f32[1024,768]{1,0:T(8,128)} %collective-permute-done.22, f32[1024,768]{1,0:T(8,128)S(1)} %copy-done.13, f32[1024,768]{1,0:T(8,128)S(1)} %get-tuple-element.99), kind=kLoop, calls=%fused_computation | loop fusion | flops 2359296 | bytes 11010048 | tf_op jit(solution)/shard_map/convert_element_type | solution.py:692
  258.9 6.5 %collective-permute-done.37 = f32[2,2,48,384]{3,2,1,0:T(8,128)} collective-permute-done((f32[2,2,48,384]{3,2,1,0:T(8,128)S(1)}, f32[2,2,48,384]{3,2,1,0:T(8,128)}, u32[]{:S(2)}, u32[]{:S(2)}) %collective-permute-start.37) | collective-permute-done | bytes 294944 | tf_op jit(solution)/shard_map/ppermute | solution.py:58
  267.3 1.4 fusion.11
  (136 shorter events, 30.1 us)
Async XLA Ops:
  1.7 26.3 %collective-permute-start.1 = (f32[1,96,1536]{2,1,0:T(8,128)S(1)}, f32[1,96,1536]{2,1,0:T(8,128)S(1)}, u32[]{:S(2)}, u32[]{:S(2)}) collective-permute-start(f32[1,96,1536]{2,1,0:T(8,128)S(1)} %bitcast_convert_fusion.1), channel_id=1, source_target_pairs={{0,1},{1,0},{2,3},{3,2},{4,5},{5,4},{6,7},{7,6},{8,9},{9,8},{10,11... | collective-permute-start | bytes 1769480 | tf_op jit(solution)/shard_map/ppermute | solution.py:54
  6.6 25.0 %collective-permute-start = (f32[1,96,1536]{2,1,0:T(8,128)}, f32[1,96,1536]{2,1,0:T(8,128)}, u32[]{:S(2)}, u32[]{:S(2)}) collective-permute-start(f32[1,96,1536]{2,1,0:T(8,128)} %pad_maximum_fusion), channel_id=1, source_target_pairs={{0,1},{1,0},{2,3},{3,2},{4,5},{5,4},{6,7},{7,6},{8,9},{9,8},{10,11... | collective-permute-start | bytes 1769480 | tf_op jit(solution)/shard_map/ppermute | solution.py:54
  23.5 40.8 %copy-start.3 = (bf16[384,768]{1,0:T(8,128)(2,1)S(1)}, bf16[384,768]{1,0:T(8,128)(2,1)}, u32[]{:S(2)}) copy-start(bf16[384,768]{1,0:T(8,128)(2,1)} %ow_ref.1) | copy-start | bytes 1769476
  23.5 47.9 %copy-start.26 = (f32[1536]{0:T(1024)S(1)}, f32[1536]{0:T(1024)}, u32[]{:S(2)}) copy-start(f32[1536]{0:T(1024)} %refs_6_.1) | copy-start | bytes 18436
  26.1 38.3 %collective-permute-start.7 = (f32[384,1024]{1,0:T(8,128)}, f32[384,1024]{1,0:T(8,128)S(1)}, u32[]{:S(2)}, u32[]{:S(2)}) collective-permute-start(f32[384,1024]{1,0:T(8,128)} %convert_element_type.11), channel_id=1, source_target_pairs={{0,1},{1,0},{2,3},{3,2},{4,5},{5,4},{6,7},{7,6},{8,9},{9,8},{10,11... | collective-permute-start | bytes 4718600 | tf_op jit(solution)/shard_map/ppermute | solution.py:54
  28.0 45.5 %copy-start.16 = (f32[1,96,1536]{2,1,0:T(8,128)}, f32[1,96,1536]{2,1,0:T(8,128)S(1)}, u32[]{:S(2)}) copy-start(f32[1,96,1536]{2,1,0:T(8,128)S(1)} %collective-permute-done.1.refs_0_) | copy-start | bytes 1769476
  28.0 16.4 %collective-permute-start.4 = (f32[1,96,1536]{2,1,0:T(8,128)S(1)}, f32[1,96,1536]{2,1,0:T(8,128)}, u32[]{:S(2)}, u32[]{:S(2)}) collective-permute-start(f32[1,96,1536]{2,1,0:T(8,128)S(1)} %collective-permute-done.1.refs_0_), channel_id=1, source_target_pairs={{0,8},{2,10},{4,12},{6,14},{8,0},{10,2},{12,4},{14,6},{16,24},{18,... | collective-permute-start | bytes 1769480 | tf_op jit(solution)/shard_map/ppermute | solution.py:58
  29.6 16.3 %collective-permute-start.5 = (f32[1,96,1536]{2,1,0:T(8,128)S(1)}, f32[1,96,1536]{2,1,0:T(8,128)S(1)}, u32[]{:S(2)}, u32[]{:S(2)}) collective-permute-start(f32[1,96,1536]{2,1,0:T(8,128)S(1)} %collective-permute-done.1.refs_0_), channel_id=1, source_target_pairs={{0,4},{2,6},{4,0},{6,2},{8,12},{10,14},{12,8},{14,10},{16,20},{18,... | collective-permute-start | bytes 1769480 | tf_op jit(solution)/shard_map/ppermute | solution.py:58
  31.6 23.4 %collective-permute-start.2 = (f32[1,96,1536]{2,1,0:T(8,128)}, f32[1,96,1536]{2,1,0:T(8,128)}, u32[]{:S(2)}, u32[]{:S(2)}) collective-permute-start(f32[1,96,1536]{2,1,0:T(8,128)} %collective-permute-done.refs_6_), channel_id=1, source_target_pairs={{0,8},{2,10},{4,12},{6,14},{8,0},{10,2},{12,4},{14,6},{16,24},{18,... | collective-permute-start | bytes 1769480 | tf_op jit(solution)/shard_map/ppermute | solution.py:58
  33.7 24.9 %collective-permute-start.3 = (f32[1,96,1536]{2,1,0:T(8,128)}, f32[1,96,1536]{2,1,0:T(8,128)}, u32[]{:S(2)}, u32[]{:S(2)}) collective-permute-start(f32[1,96,1536]{2,1,0:T(8,128)} %collective-permute-done.refs_6_), channel_id=1, source_target_pairs={{0,4},{2,6},{4,0},{6,2},{8,12},{10,14},{12,8},{14,10},{16,20},{18,... | collective-permute-start | bytes 1769480 | tf_op jit(solution)/shard_map/ppermute | solution.py:58
  45.9 23.0 %collective-permute-start.6 = (f32[1,96,1536]{2,1,0:T(8,128)}, f32[1,96,1536]{2,1,0:T(8,128)S(1)}, u32[]{:S(2)}, u32[]{:S(2)}) collective-permute-start(f32[1,96,1536]{2,1,0:T(8,128)} %collective-permute-done.4.refs_1_), channel_id=1, source_target_pairs={{0,4},{2,6},{4,0},{6,2},{8,12},{10,14},{12,8},{14,10},{16,20},{18,... | collective-permute-start | bytes 1769480 | tf_op jit(solution)/shard_map/ppermute | solution.py:58
  47.4 21.5 %collective-permute-start.14 = (f32[1,96,1536]{2,1,0:T(8,128)}, f32[1,96,1536]{2,1,0:T(8,128)}, u32[]{:S(2)}, u32[]{:S(2)}) collective-permute-start(f32[1,96,1536]{2,1,0:T(8,128)} %collective-permute-done.refs_6_), channel_id=1, source_target_pairs={{0,2},{2,0},{4,6},{6,4},{8,10},{10,8},{12,14},{14,12},{16,18},{18,... | collective-permute-start | bytes 1769480 | tf_op jit(solution)/shard_map/ppermute | solution.py:58
  55.0 14.3 %collective-permute-start.11 = (f32[1,96,1536]{2,1,0:T(8,128)S(1)}, f32[1,96,1536]{2,1,0:T(8,128)}, u32[]{:S(2)}, u32[]{:S(2)}) collective-permute-start(f32[1,96,1536]{2,1,0:T(8,128)S(1)} %collective-permute-done.1.refs_0_), channel_id=1, source_target_pairs={{0,2},{2,0},{4,6},{6,4},{8,10},{10,8},{12,14},{14,12},{16,18},{18,... | collective-permute-start | bytes 1769480 | tf_op jit(solution)/shard_map/ppermute | solution.py:58
  58.6 11.3 %collective-permute-start.12 = (f32[1,96,1536]{2,1,0:T(8,128)}, f32[1,96,1536]{2,1,0:T(8,128)}, u32[]{:S(2)}, u32[]{:S(2)}) collective-permute-start(f32[1,96,1536]{2,1,0:T(8,128)} %collective-permute-done.4.refs_1_), channel_id=1, source_target_pairs={{0,2},{2,0},{4,6},{6,4},{8,10},{10,8},{12,14},{14,12},{16,18},{18,... | collective-permute-start | bytes 1769480 | tf_op jit(solution)/shard_map/ppermute | solution.py:58
  64.4 15.1 %copy-start.15 = (f32[384,1024]{1,0:T(8,128)}, f32[384,1024]{1,0:T(8,128)S(1)}, u32[]{:S(2)}) copy-start(f32[384,1024]{1,0:T(8,128)S(1)} %collective-permute-done.7.far_ctx_ref) | copy-start | bytes 4718596
  64.4 7.1 %collective-permute-start.13 = (f32[1,96,1536]{2,1,0:T(8,128)}, f32[1,96,1536]{2,1,0:T(8,128)}, u32[]{:S(2)}, u32[]{:S(2)}) collective-permute-start(f32[1,96,1536]{2,1,0:T(8,128)} %copy-done.18), channel_id=1, source_target_pairs={{0,2},{2,0},{4,6},{6,4},{8,10},{10,8},{12,14},{14,12},{16,18},{18,... | collective-permute-start | bytes 1769480 | tf_op jit(solution)/shard_map/ppermute | solution.py:58
  68.9 10.6 %copy-start.17 = (f32[1,96,1536]{2,1,0:T(8,128)}, f32[1,96,1536]{2,1,0:T(8,128)S(1)}, u32[]{:S(2)}) copy-start(f32[1,96,1536]{2,1,0:T(8,128)S(1)} %collective-permute-done.6.refs_15_) | copy-start | bytes 1769476
  68.9 4.7 %collective-permute-start.15 = (f32[1,96,1536]{2,1,0:T(8,128)}, f32[1,96,1536]{2,1,0:T(8,128)}, u32[]{:S(2)}, u32[]{:S(2)}) collective-permute-start(f32[1,96,1536]{2,1,0:T(8,128)} %collective-permute-done.2.refs_7_), channel_id=1, source_target_pairs={{0,2},{2,0},{4,6},{6,4},{8,10},{10,8},{12,14},{14,12},{16,18},{18,... | collective-permute-start | bytes 1769480 | tf_op jit(solution)/shard_map/ppermute | solution.py:58
  68.9 4.7 %collective-permute-start.16 = (f32[1,96,1536]{2,1,0:T(8,128)}, f32[1,96,1536]{2,1,0:T(8,128)}, u32[]{:S(2)}, u32[]{:S(2)}) collective-permute-start(f32[1,96,1536]{2,1,0:T(8,128)} %collective-permute-done.3.refs_8_), channel_id=1, source_target_pairs={{0,2},{2,0},{4,6},{6,4},{8,10},{10,8},{12,14},{14,12},{16,18},{18,... | collective-permute-start | bytes 1769480 | tf_op jit(solution)/shard_map/ppermute | solution.py:58
  69.4 15.7 %collective-permute-start.9 = (f32[192,768]{1,0:T(8,128)}, f32[192,768]{1,0:T(8,128)S(1)}, u32[]{:S(2)}, u32[]{:S(2)}) collective-permute-start(f32[192,768]{1,0:T(8,128)} %dynamic-slice_convert_fusion), channel_id=1, source_target_pairs={{0,1},{1,0},{2,3},{3,2},{4,5},{5,4},{6,7},{7,6},{8,9},{9,8},{10,11... | collective-permute-start | bytes 1769480 | tf_op jit(solution)/shard_map/ppermute | solution.py:54
  69.9 15.3 %collective-permute-start.8 = (f32[1,96,1536]{2,1,0:T(8,128)}, f32[1,96,1536]{2,1,0:T(8,128)}, u32[]{:S(2)}, u32[]{:S(2)}) collective-permute-start(f32[1,96,1536]{2,1,0:T(8,128)} %collective-permute-done.2.refs_7_), channel_id=1, source_target_pairs={{0,4},{2,6},{4,0},{6,2},{8,12},{10,14},{12,8},{14,10},{16,20},{18,... | collective-permute-start | bytes 1769480 | tf_op jit(solution)/shard_map/ppermute | solution.py:58
  71.4 13.6 %collective-permute-start.10 = (f32[1536]{0:T(1024)S(1)}, f32[1536]{0:T(1024)S(1)}, u32[]{:S(2)}, u32[]{:S(2)}) collective-permute-start(f32[1536]{0:T(1024)S(1)} %copy-done.26), channel_id=1, source_target_pairs={{0,1},{1,0},{2,3},{3,2},{4,5},{5,4},{6,7},{7,6},{8,9},{9,8},{10,11... | collective-permute-start | bytes 18440 | tf_op jit(solution)/shard_map/ppermute | solution.py:54
  73.5 12.8 %collective-permute-start.18 = (f32[1,96,1536]{2,1,0:T(8,128)S(1)}, f32[1,96,1536]{2,1,0:T(8,128)}, u32[]{:S(2)}, u32[]{:S(2)}) collective-permute-start(f32[1,96,1536]{2,1,0:T(8,128)S(1)} %collective-permute-done.6.refs_15_), channel_id=1, source_target_pairs={{0,2},{2,0},{4,6},{6,4},{8,10},{10,8},{12,14},{14,12},{16,18},{18,... | collective-permute-start | bytes 1769480 | tf_op jit(solution)/shard_map/ppermute | solution.py:58
  85.2 2.8 %collective-permute-start.17 = (f32[192,768]{1,0:T(8,128)S(1)}, f32[192,768]{1,0:T(8,128)S(1)}, u32[]{:S(2)}, u32[]{:S(2)}) collective-permute-start(f32[192,768]{1,0:T(8,128)S(1)} %collective-permute-done.9.refs_9_), channel_id=1, source_target_pairs={{0,2},{2,0},{4,6},{6,4},{8,10},{10,8},{12,14},{14,12},{16,18},{18,... | collective-permute-start | bytes 1769480 | tf_op jit(solution)/shard_map/ppermute | solution.py:58
  85.2 3.1 %collective-permute-start.19 = (f32[1,96,1536]{2,1,0:T(8,128)}, f32[1,96,1536]{2,1,0:T(8,128)S(1)}, u32[]{:S(2)}, u32[]{:S(2)}) collective-permute-start(f32[1,96,1536]{2,1,0:T(8,128)} %collective-permute-done.8.refs_17_), channel_id=1, source_target_pairs={{0,2},{2,0},{4,6},{6,4},{8,10},{10,8},{12,14},{14,12},{16,18},{18,... | collective-permute-start | bytes 1769480 | tf_op jit(solution)/shard_map/ppermute | solution.py:58
  89.1 60.1 %copy-start.12 = (s32[3,2,1024]{2,1,0:T(2,128)S(1)}, s32[3,2,1024]{2,1,0:T(2,128)}, u32[]{:S(2)}) copy-start(s32[3,2,1024]{2,1,0:T(2,128)} %reshape_squeeze.3.row_ref) | copy-start | bytes 73732
  133.3 6.9 %collective-permute-start.20 = (f32[8,48,1536]{2,1,0:T(8,128)}, f32[8,48,1536]{2,1,0:T(8,128)S(1)}, u32[]{:S(2)}, u32[]{:S(2)}) collective-permute-start(f32[8,48,1536]{2,1,0:T(8,128)} %get-tuple-element.91), channel_id=1, source_target_pairs={{0,2},{2,0},{4,6},{6,4},{8,10},{10,8},{12,14},{14,12},{16,18},{18,... | collective-permute-start | bytes 7077896 | tf_op jit(solution)/shard_map/ppermute | solution.py:58
  133.5 8.1 %collective-permute-start.21 = (f32[8,48,1536]{2,1,0:T(8,128)}, f32[8,48,1536]{2,1,0:T(8,128)}, u32[]{:S(2)}, u32[]{:S(2)}) collective-permute-start(f32[8,48,1536]{2,1,0:T(8,128)} %get-tuple-element.92), channel_id=1, source_target_pairs={{0,2},{2,0},{4,6},{6,4},{8,10},{10,8},{12,14},{14,12},{16,18},{18,... | collective-permute-start | bytes 7077896 | tf_op jit(solution)/shard_map/ppermute | solution.py:58
  141.6 7.6 %copy-start.5 = (bf16[6,192,1024]{2,1,0:T(8,128)(2,1)S(1)}, bf16[6,192,1024]{2,1,0:T(8,128)(2,1)}, u32[]{:S(2)}) copy-start(bf16[6,192,1024]{2,1,0:T(8,128)(2,1)} %get-tuple-element.97.moved_ref) | copy-start | bytes 7077892
  144.6 31.8 %collective-permute-start.24 = (f32[4,48,1536]{2,1,0:T(8,128)}, f32[4,48,1536]{2,1,0:T(8,128)}, u32[]{:S(2)}, u32[]{:S(2)}) collective-permute-start(f32[4,48,1536]{2,1,0:T(8,128)} %bitcast.19), channel_id=1, source_target_pairs={{0,8},{2,10},{4,12},{6,14},{8,0},{10,2},{12,4},{14,6},{16,24},{18,... | collective-permute-start | bytes 3538952 | tf_op jit(solution)/shard_map/ppermute | solution.py:58
  147.6 28.9 %collective-permute-start.23 = (f32[4,48,1536]{2,1,0:T(8,128)}, f32[4,48,1536]{2,1,0:T(8,128)}, u32[]{:S(2)}, u32[]{:S(2)}) collective-permute-start(f32[4,48,1536]{2,1,0:T(8,128)} %bitcast.16), channel_id=1, source_target_pairs={{0,4},{2,6},{4,0},{6,2},{8,12},{10,14},{12,8},{14,10},{16,20},{18,... | collective-permute-start | bytes 3538952 | tf_op jit(solution)/shard_map/ppermute | solution.py:58
  152.0 22.8 %copy-start.28 = (f32[1,1536]{1,0:T(1,128)S(1)}, f32[1,1536]{1,0:T(1,128)}, u32[]{:S(2)}) copy-start(f32[1,1536]{1,0:T(1,128)} %get-tuple-element.109) | copy-start | bytes 18436
  174.3 6.9 %collective-permute-start.27 = (f32[8,2,48,384]{3,2,1,0:T(8,128)}, f32[8,2,48,384]{3,2,1,0:T(8,128)}, u32[]{:S(2)}, u32[]{:S(2)}) collective-permute-start(f32[8,2,48,384]{3,2,1,0:T(8,128)} %get-tuple-element.103), channel_id=1, source_target_pairs={{0,2},{2,0},{4,6},{6,4},{8,10},{10,8},{12,14},{14,12},{16,18},{18,... | collective-permute-start | bytes 3538952 | tf_op jit(solution)/shard_map/ppermute | solution.py:58
  174.3 6.9 %collective-permute-start.28 = (f32[8,2,48,384]{3,2,1,0:T(8,128)}, f32[8,2,48,384]{3,2,1,0:T(8,128)}, u32[]{:S(2)}, u32[]{:S(2)}) collective-permute-start(f32[8,2,48,384]{3,2,1,0:T(8,128)} %get-tuple-element.104), channel_id=1, source_target_pairs={{0,2},{2,0},{4,6},{6,4},{8,10},{10,8},{12,14},{14,12},{16,18},{18,... | collective-permute-start | bytes 3538952 | tf_op jit(solution)/shard_map/ppermute | solution.py:58
  174.9 80.3 %collective-permute-start.22 = (f32[1024,768]{1,0:T(8,128)S(1)}, f32[1024,768]{1,0:T(8,128)}, u32[]{:S(2)}, u32[]{:S(2)}) collective-permute-start(f32[1024,768]{1,0:T(8,128)S(1)} %get-tuple-element.99), channel_id=1, source_target_pairs={{0,1},{1,0},{2,3},{3,2},{4,5},{5,4},{6,7},{7,6},{8,9},{9,8},{10,11... | collective-permute-start | bytes 9437192 | tf_op jit(solution)/shard_map/ppermute | solution.py:54
  185.2 1.3 collective-permute-start.31
  186.5 4.5 %collective-permute-start.32 = (f32[11,768]{1,0:T(8,128)S(1)}, f32[11,768]{1,0:T(8,128)S(1)}, u32[]{:S(2)}, u32[]{:S(2)}) collective-permute-start(f32[11,768]{1,0:T(8,128)S(1)} %fusion.14), channel_id=1, source_target_pairs={{0,4},{2,6},{4,0},{6,2},{8,12},{10,14},{12,8},{14,10},{16,20},{18,... | collective-permute-start | bytes 101384 | tf_op jit(solution)/shard_map/ppermute | solution.py:58
  187.4 16.5 %collective-permute-start.30 = (f32[4,2,48,384]{3,2,1,0:T(8,128)}, f32[4,2,48,384]{3,2,1,0:T(8,128)}, u32[]{:S(2)}, u32[]{:S(2)}) collective-permute-start(f32[4,2,48,384]{3,2,1,0:T(8,128)} %bitcast.33), channel_id=1, source_target_pairs={{0,8},{2,10},{4,12},{6,14},{8,0},{10,2},{12,4},{14,6},{16,24},{18,... | collective-permute-start | bytes 1769480 | tf_op jit(solution)/shard_map/ppermute | solution.py:58
  188.9 16.6 %collective-permute-start.29 = (f32[4,2,48,384]{3,2,1,0:T(8,128)}, f32[4,2,48,384]{3,2,1,0:T(8,128)}, u32[]{:S(2)}, u32[]{:S(2)}) collective-permute-start(f32[4,2,48,384]{3,2,1,0:T(8,128)} %bitcast.30), channel_id=1, source_target_pairs={{0,4},{2,6},{4,0},{6,2},{8,12},{10,14},{12,8},{14,10},{16,20},{18,... | collective-permute-start | bytes 1769480 | tf_op jit(solution)/shard_map/ppermute | solution.py:58
  190.1 26.6 %collective-permute-start.26 = (f32[2,48,1536]{2,1,0:T(8,128)}, f32[2,48,1536]{2,1,0:T(8,128)}, u32[]{:S(2)}, u32[]{:S(2)}) collective-permute-start(f32[2,48,1536]{2,1,0:T(8,128)} %bitcast_add_fusion), channel_id=1, source_target_pairs={{0,4},{2,6},{4,0},{6,2},{8,12},{10,14},{12,8},{14,10},{16,20},{18,... | collective-permute-start | bytes 1769480 | tf_op jit(solution)/shard_map/ppermute | solution.py:58
  190.9 28.3 %copy-start.23 = (f32[11,768]{1,0:T(8,128)}, f32[11,768]{1,0:T(8,128)S(1)}, u32[]{:S(2)}) copy-start(f32[11,768]{1,0:T(8,128)S(1)} %collective-permute-done.32) | copy-start | bytes 101380
  190.9 25.8 %collective-permute-start.25 = (f32[2,48,1536]{2,1,0:T(8,128)}, f32[2,48,1536]{2,1,0:T(8,128)}, u32[]{:S(2)}, u32[]{:S(2)}) collective-permute-start(f32[2,48,1536]{2,1,0:T(8,128)} %bitcast_add_fusion.1), channel_id=1, source_target_pairs={{0,8},{2,10},{4,12},{6,14},{8,0},{10,2},{12,4},{14,6},{16,24},{18,... | collective-permute-start | bytes 1769480 | tf_op jit(solution)/shard_map/ppermute | solution.py:58
  219.3 27.8 %collective-permute-start.33 = (f32[2,48,1536]{2,1,0:T(8,128)}, f32[2,48,1536]{2,1,0:T(8,128)}, u32[]{:S(2)}, u32[]{:S(2)}) collective-permute-start(f32[2,48,1536]{2,1,0:T(8,128)} %pad_maximum_fusion.1), channel_id=1, source_target_pairs={{0,16},{2,18},{4,20},{6,22},{8,24},{10,26},{12,28},{14,30},{16,0},... | collective-permute-start | bytes 1769480 | tf_op jit(solution)/shard_map/ppermute | solution.py:58
  223.8 17.2 %collective-permute-start.35 = (f32[2,2,48,384]{3,2,1,0:T(8,128)}, f32[2,2,48,384]{3,2,1,0:T(8,128)S(1)}, u32[]{:S(2)}, u32[]{:S(2)}) collective-permute-start(f32[2,2,48,384]{3,2,1,0:T(8,128)} %bitcast_add_fusion.3), channel_id=1, source_target_pairs={{0,4},{2,6},{4,0},{6,2},{8,12},{10,14},{12,8},{14,10},{16,20},{18,... | collective-permute-start | bytes 884744 | tf_op jit(solution)/shard_map/ppermute | solution.py:58
  226.9 14.1 %collective-permute-start.34 = (f32[2,2,48,384]{3,2,1,0:T(8,128)}, f32[2,2,48,384]{3,2,1,0:T(8,128)}, u32[]{:S(2)}, u32[]{:S(2)}) collective-permute-start(f32[2,2,48,384]{3,2,1,0:T(8,128)} %bitcast_add_fusion.4), channel_id=1, source_target_pairs={{0,8},{2,10},{4,12},{6,14},{8,0},{10,2},{12,4},{14,6},{16,24},{18,... | collective-permute-start | bytes 884744 | tf_op jit(solution)/shard_map/ppermute | solution.py:58
  227.4 13.6 %collective-permute-start.36 = (f32[11,768]{1,0:T(8,128)S(1)}, f32[11,768]{1,0:T(8,128)S(1)}, u32[]{:S(2)}, u32[]{:S(2)}) collective-permute-start(f32[11,768]{1,0:T(8,128)S(1)} %add.486), channel_id=1, source_target_pairs={{0,8},{2,10},{4,12},{6,14},{8,0},{10,2},{12,4},{14,6},{16,24},{18,... | collective-permute-start | bytes 101384 | tf_op jit(solution)/shard_map/ppermute | solution.py:58
  247.1 11.8 %collective-permute-start.38 = (f32[11,768]{1,0:T(8,128)S(1)}, f32[11,768]{1,0:T(8,128)S(1)}, u32[]{:S(2)}, u32[]{:S(2)}) collective-permute-start(f32[11,768]{1,0:T(8,128)S(1)} %add.506), channel_id=1, source_target_pairs={{0,16},{2,18},{4,20},{6,22},{8,24},{10,26},{12,28},{14,30},{16,0},... | collective-permute-start | bytes 101384 | tf_op jit(solution)/shard_map/ppermute | solution.py:58
  249.5 16.0 %collective-permute-start.37 = (f32[2,2,48,384]{3,2,1,0:T(8,128)S(1)}, f32[2,2,48,384]{3,2,1,0:T(8,128)}, u32[]{:S(2)}, u32[]{:S(2)}) collective-permute-start(f32[2,2,48,384]{3,2,1,0:T(8,128)S(1)} %pad_maximum_fusion.2), channel_id=1, source_target_pairs={{0,16},{2,18},{4,20},{6,22},{8,24},{10,26},{12,28},{14,30},{16,0},... | collective-permute-start | bytes 884744 | tf_op jit(solution)/shard_map/ppermute | solution.py:58
  (21 other events, 66.4 us)

commit v5 on v4

--- a/solution.py
+++ b/solution.py
@@ -654,8 +654,9 @@
         if split:
             halving = lambda keep, send, order: Halving(keep, send, order, n_items).trade()
             down_sum, up_sum = halving(*grads[:2], bits), halving(*grads[2:], late_y)
-            sent = arrived([down_sum, up_sum])
+            sent = arrived([down_sum])
             down_sum.trade()
+            sent += arrived([up_sum], *sent)
             up_sum.trade()
             part, grad_qv, *halves = back(after(d_attn, *sent))
             far_part = swapped(part)

time: 271 us -> 270 us (level)
  transfers between devices with their start and end apart: 39 -> 39, of which waited for: 20 -> 19; matrix products, arithmetic and copies ran while one was open for 13% -> 13% of each run, Pallas kernels for 15% -> 15%
where the time goes in v5:
time: 270 us; the launch traced here: 269 us
  waiting for transfers between devices  95.6 us (35%)
  Pallas kernels  85.6 us (32%)
  other arithmetic  39.3 us (15%)
  starting transfers between devices  37.6 us (14%)
  local copies, waits for them, and re-layouts  10.4 us (4%)
    ppermute x33, waiting for transfers between devices, traded(): lax.ppermute(values, 'items', [(i, i ^ step) for i in range(n_items)])  83.8 us
    pallas_call x1, Pallas kernels, feed(): pl.pallas_call(functools.partial(feed_kernel, orders, tiles, len(late)),...  44.2 us
    ppermute x33, starting transfers between devices, traded(): lax.ppermute(values, 'items', [(i, i ^ step) for i in range(n_items)])  29 us
    add x11, other arithmetic, add(): self.send = sum((self.part(term, [1 - mine]) for term in self.terms))  22.8 us
    pallas_call x1, Pallas kernels, attend_back(): pl.pallas_call(functools.partial(attend_back_kernel, orders), grid=(pairs...  20.1 us
    pallas_call x1, Pallas kernels, attend(): pl.pallas_call(attend_kernel, grid=(pairs,), in_specs=[whole(rows, width)...  15.4 us
    ppermute x6, waiting for transfers between devices, swapped(): return lax.ppermute(values, 'heads', [(0, 1), (1, 0)])  11.8 us
    ppermute x6, starting transfers between devices, swapped(): return lax.ppermute(values, 'heads', [(0, 1), (1, 0)])  8.61 us
  transfers between devices with their start and end apart: 39, of which 19 were waited for; matrix products, arithmetic and copies ran while one was open for 13% of the time, Pallas kernels for 15%

profile of v5, /device:TPU:0, one launch (start us, length us, event | category | flops | bytes accessed | tf_op | source)
XLA Modules:
  0.0 269.4 jit_solution(1976376178076715728)
XLA Ops:
  1.7 3.0 %collective-permute-start.1 = (f32[1,96,1536]{2,1,0:T(8,128)S(1)}, f32[1,96,1536]{2,1,0:T(8,128)S(1)}, u32[]{:S(2)}, u32[]{:S(2)}) collective-permute-start(f32[1,96,1536]{2,1,0:T(8,128)S(1)} %bitcast_convert_fusion.1), channel_id=1, source_target_pairs={{0,1},{1,0},{2,3},{3,2},{4,5},{5,4},{6,7},{7,6},{8,9},{9,8},{10,11... | collective-permute-start | bytes 1769480 | tf_op jit(solution)/shard_map/ppermute | solution.py:54
  8.2 15.4 %attend.1 = (bf16[384,1024]{1,0:T(8,128)(2,1)}, bf16[6,192,1024]{2,1,0:T(8,128)(2,1)}, bf16[6,1024,128]{2,1,0:T(8,128)(2,1)}) custom-call(bf16[1024,768]{1,0:T(8,128)(2,1)} %x_ref.2, bf16[3,768,384]{2,1,0:T(8,128)(2,1)} %w_ref.3, f32[384,2]{1,0:T(8,128)} %bitcast.148, s32[3,2,1024]{2,1,0:T(2,128)} %reshape_squeeze.3.row_ref), custom_call_target="tpu_custom_call" | custom-call | flops 12000000 | bytes 12000 | tf_op jit(solution)/shard_map/attend/pallas_call | solution.py:177
  23.6 2.5 convert_element_type.11
  26.1 2.0 collective-permute-start.7
  28.0 1.6 collective-permute-start.4
  29.6 1.5 collective-permute-start.5
  31.6 2.1 collective-permute-start.2
  33.7 1.5 collective-permute-start.3
  35.3 9.2 %collective-permute-done.4.refs_1_ = f32[1,96,1536]{2,1,0:T(8,128)} collective-permute-done((f32[1,96,1536]{2,1,0:T(8,128)S(1)}, f32[1,96,1536]{2,1,0:T(8,128)}, u32[]{:S(2)}, u32[]{:S(2)}) %collective-permute-start.4) | collective-permute-done | bytes 589856 | tf_op jit(solution)/shard_map/ppermute | solution.py:58
  44.4 1.5 collective-permute-done.5.refs_2_
  45.9 1.5 collective-permute-start.6
  47.4 7.6 %collective-permute-done.2.refs_7_ = f32[1,96,1536]{2,1,0:T(8,128)} collective-permute-done((f32[1,96,1536]{2,1,0:T(8,128)}, f32[1,96,1536]{2,1,0:T(8,128)}, u32[]{:S(2)}, u32[]{:S(2)}) %collective-permute-start.2) | collective-permute-done | bytes 589856 | tf_op jit(solution)/shard_map/ppermute | solution.py:58
  55.0 3.6 %collective-permute-done.3.refs_8_ = f32[1,96,1536]{2,1,0:T(8,128)} collective-permute-done((f32[1,96,1536]{2,1,0:T(8,128)}, f32[1,96,1536]{2,1,0:T(8,128)}, u32[]{:S(2)}, u32[]{:S(2)}) %collective-permute-start.3) | collective-permute-done | bytes 589856 | tf_op jit(solution)/shard_map/ppermute | solution.py:58
  58.6 5.7 %collective-permute-done.7.far_ctx_ref = f32[384,1024]{1,0:T(8,128)S(1)} collective-permute-done((f32[384,1024]{1,0:T(8,128)}, f32[384,1024]{1,0:T(8,128)S(1)}, u32[]{:S(2)}, u32[]{:S(2)}) %collective-permute-start.7) | collective-permute-done | bytes 1572896 | tf_op jit(solution)/shard_map/ppermute | solution.py:54
  65.3 3.6 %collective-permute-done.6.refs_15_ = f32[1,96,1536]{2,1,0:T(8,128)S(1)} collective-permute-done((f32[1,96,1536]{2,1,0:T(8,128)}, f32[1,96,1536]{2,1,0:T(8,128)S(1)}, u32[]{:S(2)}, u32[]{:S(2)}) %collective-permute-start.6) | collective-permute-done | bytes 589856 | tf_op jit(solution)/shard_map/ppermute | solution.py:58
  69.9 1.5 collective-permute-start.8
  71.4 1.5 collective-permute-start.10
  73.6 5.9 %placed.1 = (bf16[768,1536]{1,0:T(8,128)(2,1)}, bf16[1536,768]{1,0:T(8,128)(2,1)}) custom-call(s32[6]{0:T(128)} %stack.42.slots_ref, f32[1,96,1536]{2,1,0:T(8,128)} %copy-done.16, f32[1,96,1536]{2,1,0:T(8,128)} %collective-permute-done.4.refs_1_, f32[1,96,1536]{2,1,0:T(8,128)} %copy-done.18, f32[1,96,1536]{2,1,0:T(8,128)} %collective-permute-done.11.refs_3_, ...), custom_call_target="tpu_custom_call" | custom-call | flops 1000 | bytes 1000 | tf_op jit(solution)/shard_map/placed/pallas_call | solution.py:371
  79.5 5.6 %collective-permute-done.10.refs_7_ = f32[1536]{0:T(1024)S(1)} collective-permute-done((f32[1536]{0:T(1024)S(1)}, f32[1536]{0:T(1024)S(1)}, u32[]{:S(2)}, u32[]{:S(2)}) %collective-permute-start.10) | collective-permute-done | bytes 6176 | tf_op jit(solution)/shard_map/ppermute | solution.py:54
  86.3 1.7 collective-permute-done.17.refs_10_
  89.1 44.2 %feed.1 = (bf16[1024,768]{1,0:T(8,128)(2,1)}, f32[1024,768]{1,0:T(8,128)}, bf16[1024,768]{1,0:T(8,128)(2,1)}, f32[8,768]{1,0:T(8,128)}, f32[1,1536]{1,0:T(1,128)...) custom-call(s32[1]{0:T(128)} %bitcast.core_ref, ...), custom_call_target="tpu_custom_call" | custom-call | flops 25000000 | bytes 30000 | tf_op jit(solution)/shard_map/feed/pallas_call | solution.py:535
  133.9 6.3 %collective-permute-done.20 = f32[8,48,1536]{2,1,0:T(8,128)S(1)} collective-permute-done((f32[8,48,1536]{2,1,0:T(8,128)}, f32[8,48,1536]{2,1,0:T(8,128)S(1)}, u32[]{:S(2)}, u32[]{:S(2)}) %collective-permute-start.20) | collective-permute-done | bytes 2359328 | tf_op jit(solution)/shard_map/ppermute | solution.py:58
  140.2 3.4 %dynamic-slice_add_fusion.1 = f32[1,2,2,48,1536]{4,3,2,1,0:T(8,128)} fusion(f32[2,2,2,48,1536]{4,3,2,1,0:T(8,128)S(1)} %bitcast.144, s32[]{:T(128)S(6)} %select_n.29, f32[2,2,2,48,1536]{4,3,2,1,0:T(8,128)} %bitcast.136), kind=kLoop, calls=%fused_computation.2 | loop fusion | flops 294912 | bytes 3538948 | tf_op jit(solution)/shard_map/add | solution.py:115
  143.6 2.9 %dynamic-slice_add_fusion = f32[1,2,2,48,1536]{4,3,2,1,0:T(8,128)} fusion(f32[2,2,2,48,1536]{4,3,2,1,0:T(8,128)} %bitcast.18, s32[]{:T(128)S(6)} %select_n.30, f32[2,2,2,48,1536]{4,3,2,1,0:T(8,128)} %bitcast.140), kind=kLoop, calls=%fused_computation.1 | loop fusion | flops 294912 | bytes 3538948 | tf_op jit(solution)/shard_map/add | solution.py:115
  146.7 1.9 collective-permute-start.23
  151.4 20.1 %attend_back.1 = (f32[1024,768]{1,0:T(8,128)S(1)}, f32[2,384]{1,0:T(2,128)S(1)}, f32[8,2,48,384]{3,2,1,0:T(8,128)S(1)}, f32[8,2,48,384]{3,2,1,0:T(8,128)}, f32[8...) custom-call(s32[1]{0:T(128)} %bitcast.core_ref, bf16[1024,768]{1,0:T(8,128)(2,1)S(1)} %copy-done, ...), custom_call_target="tpu_custom_call" | custom-call | flops 20000000 | bytes 20000 | tf_op jit(solution)/shard_map/attend_back/pallas_call | solution.py:282
  174.2 1.6 collective-permute-start.22
  175.7 2.3 bitcast_add_fusion
  178.0 2.5 bitcast_add_fusion.1
  180.5 1.9 dynamic-slice_add_fusion.2
  182.5 2.0 dynamic-slice_add_fusion.3
  186.7 1.6 collective-permute-start.30
  190.3 1.7 collective-permute-start.25
  191.9 11.3 %collective-permute-done.30 = f32[4,2,48,384]{3,2,1,0:T(8,128)} collective-permute-done((f32[4,2,48,384]{3,2,1,0:T(8,128)}, f32[4,2,48,384]{3,2,1,0:T(8,128)}, u32[]{:S(2)}, u32[]{:S(2)}) %collective-permute-start.30) | collective-permute-done | bytes 589856 | tf_op jit(solution)/shard_map/ppermute | solution.py:58
  203.2 1.6 collective-permute-done.29
  204.8 11.2 %collective-permute-done.26 = f32[2,48,1536]{2,1,0:T(8,128)} collective-permute-done((f32[2,48,1536]{2,1,0:T(8,128)}, f32[2,48,1536]{2,1,0:T(8,128)}, u32[]{:S(2)}, u32[]{:S(2)}) %collective-permute-start.26) | collective-permute-done | bytes 589856 | tf_op jit(solution)/shard_map/ppermute | solution.py:58
  216.0 1.7 fusion.3
  218.6 2.6 collective-permute-start.33
  221.2 1.9 bitcast_add_fusion.3
  224.3 1.9 bitcast_add_fusion.4
  226.7 1.6 collective-permute-start.36
  228.3 12.0 %collective-permute-done.36 = f32[11,768]{1,0:T(8,128)S(1)} collective-permute-done((f32[11,768]{1,0:T(8,128)S(1)}, f32[11,768]{1,0:T(8,128)S(1)}, u32[]{:S(2)}, u32[]{:S(2)}) %collective-permute-start.36) | collective-permute-done | bytes 33824 | tf_op jit(solution)/shard_map/ppermute | solution.py:58
  240.3 6.1 %collective-permute-done.33 = f32[2,48,1536]{2,1,0:T(8,128)} collective-permute-done((f32[2,48,1536]{2,1,0:T(8,128)}, f32[2,48,1536]{2,1,0:T(8,128)}, u32[]{:S(2)}, u32[]{:S(2)}) %collective-permute-start.33) | collective-permute-done | bytes 589856 | tf_op jit(solution)/shard_map/ppermute | solution.py:58
  248.8 3.0 %collective-permute-start.37 = (f32[2,2,48,384]{3,2,1,0:T(8,128)S(1)}, f32[2,2,48,384]{3,2,1,0:T(8,128)}, u32[]{:S(2)}, u32[]{:S(2)}) collective-permute-start(f32[2,2,48,384]{3,2,1,0:T(8,128)S(1)} %pad_maximum_fusion.2), channel_id=1, source_target_pairs={{0,16},{2,18},{4,20},{6,22},{8,24},{10,26},{12,28},{14,30},{16,0},... | collective-permute-start | bytes 884744 | tf_op jit(solution)/shard_map/ppermute | solution.py:58
  251.8 2.8 %fusion.7 = (f32[1536,48]{0,1:T(8,128)}, f32[48,1536]{1,0:T(8,128)}) fusion(f32[2,48,1536]{2,1,0:T(8,128)} %collective-permute-done.33, f32[2,48,1536]{2,1,0:T(8,128)} %collective-permute-done.25, s32[]{:T(128)S(6)} %select_n.33, f32[2,2,48,1536]{3,2,1,0:T(8,128)} %bitcast.21, s32[]{:T(128)S(6)} %select_n.32, f32[2,2,2,48,1536]{4,3,2,1,0:T(8,128)} %bitcast.147, ...), kind=kLoop, calls=%fused_computation.23 | loop fusion | flops 589824 | bytes 3538956 | tf_op jit(solution)/shard_map/transpose | solution.py:720
  254.5 3.7 %add_convert_fusion = bf16[1024,768]{1,0:T(8,128)(2,1)} fusion(f32[1024,768]{1,0:T(8,128)} %collective-permute-done.22, f32[1024,768]{1,0:T(8,128)S(1)} %copy-done.13, f32[1024,768]{1,0:T(8,128)S(1)} %get-tuple-element.97), kind=kLoop, calls=%fused_computation | loop fusion | flops 2359296 | bytes 11010048 | tf_op jit(solution)/shard_map/convert_element_type | solution.py:693
  258.3 6.5 %collective-permute-done.37 = f32[2,2,48,384]{3,2,1,0:T(8,128)} collective-permute-done((f32[2,2,48,384]{3,2,1,0:T(8,128)S(1)}, f32[2,2,48,384]{3,2,1,0:T(8,128)}, u32[]{:S(2)}, u32[]{:S(2)}) %collective-permute-start.37) | collective-permute-done | bytes 294944 | tf_op jit(solution)/shard_map/ppermute | solution.py:58
  266.6 1.4 fusion.11
  (136 shorter events, 28.5 us)
Async XLA Ops:
  1.7 26.3 %collective-permute-start.1 = (f32[1,96,1536]{2,1,0:T(8,128)S(1)}, f32[1,96,1536]{2,1,0:T(8,128)S(1)}, u32[]{:S(2)}, u32[]{:S(2)}) collective-permute-start(f32[1,96,1536]{2,1,0:T(8,128)S(1)} %bitcast_convert_fusion.1), channel_id=1, source_target_pairs={{0,1},{1,0},{2,3},{3,2},{4,5},{5,4},{6,7},{7,6},{8,9},{9,8},{10,11... | collective-permute-start | bytes 1769480 | tf_op jit(solution)/shard_map/ppermute | solution.py:54
  6.6 25.0 %collective-permute-start = (f32[1,96,1536]{2,1,0:T(8,128)}, f32[1,96,1536]{2,1,0:T(8,128)}, u32[]{:S(2)}, u32[]{:S(2)}) collective-permute-start(f32[1,96,1536]{2,1,0:T(8,128)} %pad_maximum_fusion), channel_id=1, source_target_pairs={{0,1},{1,0},{2,3},{3,2},{4,5},{5,4},{6,7},{7,6},{8,9},{9,8},{10,11... | collective-permute-start | bytes 1769480 | tf_op jit(solution)/shard_map/ppermute | solution.py:54
  23.5 40.8 %copy-start.3 = (bf16[384,768]{1,0:T(8,128)(2,1)S(1)}, bf16[384,768]{1,0:T(8,128)(2,1)}, u32[]{:S(2)}) copy-start(bf16[384,768]{1,0:T(8,128)(2,1)} %ow_ref.1) | copy-start | bytes 1769476
  23.5 47.9 %copy-start.26 = (f32[1536]{0:T(1024)S(1)}, f32[1536]{0:T(1024)}, u32[]{:S(2)}) copy-start(f32[1536]{0:T(1024)} %refs_6_.1) | copy-start | bytes 18436
  26.1 38.3 %collective-permute-start.7 = (f32[384,1024]{1,0:T(8,128)}, f32[384,1024]{1,0:T(8,128)S(1)}, u32[]{:S(2)}, u32[]{:S(2)}) collective-permute-start(f32[384,1024]{1,0:T(8,128)} %convert_element_type.11), channel_id=1, source_target_pairs={{0,1},{1,0},{2,3},{3,2},{4,5},{5,4},{6,7},{7,6},{8,9},{9,8},{10,11... | collective-permute-start | bytes 4718600 | tf_op jit(solution)/shard_map/ppermute | solution.py:54
  28.0 45.5 %copy-start.16 = (f32[1,96,1536]{2,1,0:T(8,128)}, f32[1,96,1536]{2,1,0:T(8,128)S(1)}, u32[]{:S(2)}) copy-start(f32[1,96,1536]{2,1,0:T(8,128)S(1)} %collective-permute-done.1.refs_0_) | copy-start | bytes 1769476
  28.0 16.4 %collective-permute-start.4 = (f32[1,96,1536]{2,1,0:T(8,128)S(1)}, f32[1,96,1536]{2,1,0:T(8,128)}, u32[]{:S(2)}, u32[]{:S(2)}) collective-permute-start(f32[1,96,1536]{2,1,0:T(8,128)S(1)} %collective-permute-done.1.refs_0_), channel_id=1, source_target_pairs={{0,8},{2,10},{4,12},{6,14},{8,0},{10,2},{12,4},{14,6},{16,24},{18,... | collective-permute-start | bytes 1769480 | tf_op jit(solution)/shard_map/ppermute | solution.py:58
  29.6 16.3 %collective-permute-start.5 = (f32[1,96,1536]{2,1,0:T(8,128)S(1)}, f32[1,96,1536]{2,1,0:T(8,128)S(1)}, u32[]{:S(2)}, u32[]{:S(2)}) collective-permute-start(f32[1,96,1536]{2,1,0:T(8,128)S(1)} %collective-permute-done.1.refs_0_), channel_id=1, source_target_pairs={{0,4},{2,6},{4,0},{6,2},{8,12},{10,14},{12,8},{14,10},{16,20},{18,... | collective-permute-start | bytes 1769480 | tf_op jit(solution)/shard_map/ppermute | solution.py:58
  31.6 23.4 %collective-permute-start.2 = (f32[1,96,1536]{2,1,0:T(8,128)}, f32[1,96,1536]{2,1,0:T(8,128)}, u32[]{:S(2)}, u32[]{:S(2)}) collective-permute-start(f32[1,96,1536]{2,1,0:T(8,128)} %collective-permute-done.refs_6_), channel_id=1, source_target_pairs={{0,8},{2,10},{4,12},{6,14},{8,0},{10,2},{12,4},{14,6},{16,24},{18,... | collective-permute-start | bytes 1769480 | tf_op jit(solution)/shard_map/ppermute | solution.py:58
  33.7 24.9 %collective-permute-start.3 = (f32[1,96,1536]{2,1,0:T(8,128)}, f32[1,96,1536]{2,1,0:T(8,128)}, u32[]{:S(2)}, u32[]{:S(2)}) collective-permute-start(f32[1,96,1536]{2,1,0:T(8,128)} %collective-permute-done.refs_6_), channel_id=1, source_target_pairs={{0,4},{2,6},{4,0},{6,2},{8,12},{10,14},{12,8},{14,10},{16,20},{18,... | collective-permute-start | bytes 1769480 | tf_op jit(solution)/shard_map/ppermute | solution.py:58
  45.9 23.0 %collective-permute-start.6 = (f32[1,96,1536]{2,1,0:T(8,128)}, f32[1,96,1536]{2,1,0:T(8,128)S(1)}, u32[]{:S(2)}, u32[]{:S(2)}) collective-permute-start(f32[1,96,1536]{2,1,0:T(8,128)} %collective-permute-done.4.refs_1_), channel_id=1, source_target_pairs={{0,4},{2,6},{4,0},{6,2},{8,12},{10,14},{12,8},{14,10},{16,20},{18,... | collective-permute-start | bytes 1769480 | tf_op jit(solution)/shard_map/ppermute | solution.py:58
  47.4 21.5 %collective-permute-start.14 = (f32[1,96,1536]{2,1,0:T(8,128)}, f32[1,96,1536]{2,1,0:T(8,128)}, u32[]{:S(2)}, u32[]{:S(2)}) collective-permute-start(f32[1,96,1536]{2,1,0:T(8,128)} %collective-permute-done.refs_6_), channel_id=1, source_target_pairs={{0,2},{2,0},{4,6},{6,4},{8,10},{10,8},{12,14},{14,12},{16,18},{18,... | collective-permute-start | bytes 1769480 | tf_op jit(solution)/shard_map/ppermute | solution.py:58
  55.0 14.3 %collective-permute-start.11 = (f32[1,96,1536]{2,1,0:T(8,128)S(1)}, f32[1,96,1536]{2,1,0:T(8,128)}, u32[]{:S(2)}, u32[]{:S(2)}) collective-permute-start(f32[1,96,1536]{2,1,0:T(8,128)S(1)} %collective-permute-done.1.refs_0_), channel_id=1, source_target_pairs={{0,2},{2,0},{4,6},{6,4},{8,10},{10,8},{12,14},{14,12},{16,18},{18,... | collective-permute-start | bytes 1769480 | tf_op jit(solution)/shard_map/ppermute | solution.py:58
  58.6 11.3 %collective-permute-start.12 = (f32[1,96,1536]{2,1,0:T(8,128)}, f32[1,96,1536]{2,1,0:T(8,128)}, u32[]{:S(2)}, u32[]{:S(2)}) collective-permute-start(f32[1,96,1536]{2,1,0:T(8,128)} %collective-permute-done.4.refs_1_), channel_id=1, source_target_pairs={{0,2},{2,0},{4,6},{6,4},{8,10},{10,8},{12,14},{14,12},{16,18},{18,... | collective-permute-start | bytes 1769480 | tf_op jit(solution)/shard_map/ppermute | solution.py:58
  64.4 15.1 %copy-start.15 = (f32[384,1024]{1,0:T(8,128)}, f32[384,1024]{1,0:T(8,128)S(1)}, u32[]{:S(2)}) copy-start(f32[384,1024]{1,0:T(8,128)S(1)} %collective-permute-done.7.far_ctx_ref) | copy-start | bytes 4718596
  64.4 7.1 %collective-permute-start.13 = (f32[1,96,1536]{2,1,0:T(8,128)}, f32[1,96,1536]{2,1,0:T(8,128)}, u32[]{:S(2)}, u32[]{:S(2)}) collective-permute-start(f32[1,96,1536]{2,1,0:T(8,128)} %copy-done.18), channel_id=1, source_target_pairs={{0,2},{2,0},{4,6},{6,4},{8,10},{10,8},{12,14},{14,12},{16,18},{18,... | collective-permute-start | bytes 1769480 | tf_op jit(solution)/shard_map/ppermute | solution.py:58
  68.9 10.6 %copy-start.17 = (f32[1,96,1536]{2,1,0:T(8,128)}, f32[1,96,1536]{2,1,0:T(8,128)S(1)}, u32[]{:S(2)}) copy-start(f32[1,96,1536]{2,1,0:T(8,128)S(1)} %collective-permute-done.6.refs_15_) | copy-start | bytes 1769476
  68.9 4.7 %collective-permute-start.15 = (f32[1,96,1536]{2,1,0:T(8,128)}, f32[1,96,1536]{2,1,0:T(8,128)}, u32[]{:S(2)}, u32[]{:S(2)}) collective-permute-start(f32[1,96,1536]{2,1,0:T(8,128)} %collective-permute-done.2.refs_7_), channel_id=1, source_target_pairs={{0,2},{2,0},{4,6},{6,4},{8,10},{10,8},{12,14},{14,12},{16,18},{18,... | collective-permute-start | bytes 1769480 | tf_op jit(solution)/shard_map/ppermute | solution.py:58
  68.9 4.7 %collective-permute-start.16 = (f32[1,96,1536]{2,1,0:T(8,128)}, f32[1,96,1536]{2,1,0:T(8,128)}, u32[]{:S(2)}, u32[]{:S(2)}) collective-permute-start(f32[1,96,1536]{2,1,0:T(8,128)} %collective-permute-done.3.refs_8_), channel_id=1, source_target_pairs={{0,2},{2,0},{4,6},{6,4},{8,10},{10,8},{12,14},{14,12},{16,18},{18,... | collective-permute-start | bytes 1769480 | tf_op jit(solution)/shard_map/ppermute | solution.py:58
  69.4 15.7 %collective-permute-start.9 = (f32[192,768]{1,0:T(8,128)}, f32[192,768]{1,0:T(8,128)S(1)}, u32[]{:S(2)}, u32[]{:S(2)}) collective-permute-start(f32[192,768]{1,0:T(8,128)} %dynamic-slice_convert_fusion), channel_id=1, source_target_pairs={{0,1},{1,0},{2,3},{3,2},{4,5},{5,4},{6,7},{7,6},{8,9},{9,8},{10,11... | collective-permute-start | bytes 1769480 | tf_op jit(solution)/shard_map/ppermute | solution.py:54
  69.9 15.3 %collective-permute-start.8 = (f32[1,96,1536]{2,1,0:T(8,128)}, f32[1,96,1536]{2,1,0:T(8,128)}, u32[]{:S(2)}, u32[]{:S(2)}) collective-permute-start(f32[1,96,1536]{2,1,0:T(8,128)} %collective-permute-done.2.refs_7_), channel_id=1, source_target_pairs={{0,4},{2,6},{4,0},{6,2},{8,12},{10,14},{12,8},{14,10},{16,20},{18,... | collective-permute-start | bytes 1769480 | tf_op jit(solution)/shard_map/ppermute | solution.py:58
  71.4 13.6 %collective-permute-start.10 = (f32[1536]{0:T(1024)S(1)}, f32[1536]{0:T(1024)S(1)}, u32[]{:S(2)}, u32[]{:S(2)}) collective-permute-start(f32[1536]{0:T(1024)S(1)} %copy-done.26), channel_id=1, source_target_pairs={{0,1},{1,0},{2,3},{3,2},{4,5},{5,4},{6,7},{7,6},{8,9},{9,8},{10,11... | collective-permute-start | bytes 18440 | tf_op jit(solution)/shard_map/ppermute | solution.py:54
  73.5 12.8 %collective-permute-start.18 = (f32[1,96,1536]{2,1,0:T(8,128)S(1)}, f32[1,96,1536]{2,1,0:T(8,128)}, u32[]{:S(2)}, u32[]{:S(2)}) collective-permute-start(f32[1,96,1536]{2,1,0:T(8,128)S(1)} %collective-permute-done.6.refs_15_), channel_id=1, source_target_pairs={{0,2},{2,0},{4,6},{6,4},{8,10},{10,8},{12,14},{14,12},{16,18},{18,... | collective-permute-start | bytes 1769480 | tf_op jit(solution)/shard_map/ppermute | solution.py:58
  85.2 2.8 %collective-permute-start.17 = (f32[192,768]{1,0:T(8,128)S(1)}, f32[192,768]{1,0:T(8,128)S(1)}, u32[]{:S(2)}, u32[]{:S(2)}) collective-permute-start(f32[192,768]{1,0:T(8,128)S(1)} %collective-permute-done.9.refs_9_), channel_id=1, source_target_pairs={{0,2},{2,0},{4,6},{6,4},{8,10},{10,8},{12,14},{14,12},{16,18},{18,... | collective-permute-start | bytes 1769480 | tf_op jit(solution)/shard_map/ppermute | solution.py:58
  85.2 3.1 %collective-permute-start.19 = (f32[1,96,1536]{2,1,0:T(8,128)}, f32[1,96,1536]{2,1,0:T(8,128)S(1)}, u32[]{:S(2)}, u32[]{:S(2)}) collective-permute-start(f32[1,96,1536]{2,1,0:T(8,128)} %collective-permute-done.8.refs_17_), channel_id=1, source_target_pairs={{0,2},{2,0},{4,6},{6,4},{8,10},{10,8},{12,14},{14,12},{16,18},{18,... | collective-permute-start | bytes 1769480 | tf_op jit(solution)/shard_map/ppermute | solution.py:58
  89.1 59.4 %copy-start.12 = (s32[3,2,1024]{2,1,0:T(2,128)S(1)}, s32[3,2,1024]{2,1,0:T(2,128)}, u32[]{:S(2)}) copy-start(s32[3,2,1024]{2,1,0:T(2,128)} %reshape_squeeze.3.row_ref) | copy-start | bytes 73732
  133.3 6.9 %collective-permute-start.20 = (f32[8,48,1536]{2,1,0:T(8,128)}, f32[8,48,1536]{2,1,0:T(8,128)S(1)}, u32[]{:S(2)}, u32[]{:S(2)}) collective-permute-start(f32[8,48,1536]{2,1,0:T(8,128)} %get-tuple-element.90), channel_id=1, source_target_pairs={{0,2},{2,0},{4,6},{6,4},{8,10},{10,8},{12,14},{14,12},{16,18},{18,... | collective-permute-start | bytes 7077896 | tf_op jit(solution)/shard_map/ppermute | solution.py:58
  133.5 10.1 %collective-permute-start.21 = (f32[8,48,1536]{2,1,0:T(8,128)}, f32[8,48,1536]{2,1,0:T(8,128)}, u32[]{:S(2)}, u32[]{:S(2)}) collective-permute-start(f32[8,48,1536]{2,1,0:T(8,128)} %get-tuple-element.92), channel_id=1, source_target_pairs={{0,2},{2,0},{4,6},{6,4},{8,10},{10,8},{12,14},{14,12},{16,18},{18,... | collective-permute-start | bytes 7077896 | tf_op jit(solution)/shard_map/ppermute | solution.py:58
  140.2 8.3 %copy-start.5 = (bf16[6,192,1024]{2,1,0:T(8,128)(2,1)S(1)}, bf16[6,192,1024]{2,1,0:T(8,128)(2,1)}, u32[]{:S(2)}) copy-start(bf16[6,192,1024]{2,1,0:T(8,128)(2,1)} %get-tuple-element.95.moved_ref) | copy-start | bytes 7077892
  146.5 29.2 %collective-permute-start.24 = (f32[4,48,1536]{2,1,0:T(8,128)}, f32[4,48,1536]{2,1,0:T(8,128)}, u32[]{:S(2)}, u32[]{:S(2)}) collective-permute-start(f32[4,48,1536]{2,1,0:T(8,128)} %bitcast.19), channel_id=1, source_target_pairs={{0,8},{2,10},{4,12},{6,14},{8,0},{10,2},{12,4},{14,6},{16,24},{18,... | collective-permute-start | bytes 3538952 | tf_op jit(solution)/shard_map/ppermute | solution.py:58
  146.7 29.1 %collective-permute-start.23 = (f32[4,48,1536]{2,1,0:T(8,128)}, f32[4,48,1536]{2,1,0:T(8,128)}, u32[]{:S(2)}, u32[]{:S(2)}) collective-permute-start(f32[4,48,1536]{2,1,0:T(8,128)} %bitcast.16), channel_id=1, source_target_pairs={{0,4},{2,6},{4,0},{6,2},{8,12},{10,14},{12,8},{14,10},{16,20},{18,... | collective-permute-start | bytes 3538952 | tf_op jit(solution)/shard_map/ppermute | solution.py:58
  151.4 22.8 %copy-start.28 = (f32[1,1536]{1,0:T(1,128)S(1)}, f32[1,1536]{1,0:T(1,128)}, u32[]{:S(2)}) copy-start(f32[1,1536]{1,0:T(1,128)} %get-tuple-element.107) | copy-start | bytes 18436
  173.6 6.9 %collective-permute-start.27 = (f32[8,2,48,384]{3,2,1,0:T(8,128)}, f32[8,2,48,384]{3,2,1,0:T(8,128)}, u32[]{:S(2)}, u32[]{:S(2)}) collective-permute-start(f32[8,2,48,384]{3,2,1,0:T(8,128)} %get-tuple-element.101), channel_id=1, source_target_pairs={{0,2},{2,0},{4,6},{6,4},{8,10},{10,8},{12,14},{14,12},{16,18},{18,... | collective-permute-start | bytes 3538952 | tf_op jit(solution)/shard_map/ppermute | solution.py:58
  173.6 6.9 %collective-permute-start.28 = (f32[8,2,48,384]{3,2,1,0:T(8,128)}, f32[8,2,48,384]{3,2,1,0:T(8,128)}, u32[]{:S(2)}, u32[]{:S(2)}) collective-permute-start(f32[8,2,48,384]{3,2,1,0:T(8,128)} %get-tuple-element.102), channel_id=1, source_target_pairs={{0,2},{2,0},{4,6},{6,4},{8,10},{10,8},{12,14},{14,12},{16,18},{18,... | collective-permute-start | bytes 3538952 | tf_op jit(solution)/shard_map/ppermute | solution.py:58
  174.2 80.4 %collective-permute-start.22 = (f32[1024,768]{1,0:T(8,128)S(1)}, f32[1024,768]{1,0:T(8,128)}, u32[]{:S(2)}, u32[]{:S(2)}) collective-permute-start(f32[1024,768]{1,0:T(8,128)S(1)} %get-tuple-element.97), channel_id=1, source_target_pairs={{0,1},{1,0},{2,3},{3,2},{4,5},{5,4},{6,7},{7,6},{8,9},{9,8},{10,11... | collective-permute-start | bytes 9437192 | tf_op jit(solution)/shard_map/ppermute | solution.py:54
  184.5 1.3 collective-permute-start.31
  185.8 4.5 %collective-permute-start.32 = (f32[11,768]{1,0:T(8,128)S(1)}, f32[11,768]{1,0:T(8,128)S(1)}, u32[]{:S(2)}, u32[]{:S(2)}) collective-permute-start(f32[11,768]{1,0:T(8,128)S(1)} %fusion.14), channel_id=1, source_target_pairs={{0,4},{2,6},{4,0},{6,2},{8,12},{10,14},{12,8},{14,10},{16,20},{18,... | collective-permute-start | bytes 101384 | tf_op jit(solution)/shard_map/ppermute | solution.py:58
  186.7 16.5 %collective-permute-start.30 = (f32[4,2,48,384]{3,2,1,0:T(8,128)}, f32[4,2,48,384]{3,2,1,0:T(8,128)}, u32[]{:S(2)}, u32[]{:S(2)}) collective-permute-start(f32[4,2,48,384]{3,2,1,0:T(8,128)} %bitcast.33), channel_id=1, source_target_pairs={{0,8},{2,10},{4,12},{6,14},{8,0},{10,2},{12,4},{14,6},{16,24},{18,... | collective-permute-start | bytes 1769480 | tf_op jit(solution)/shard_map/ppermute | solution.py:58
  188.2 16.6 %collective-permute-start.29 = (f32[4,2,48,384]{3,2,1,0:T(8,128)}, f32[4,2,48,384]{3,2,1,0:T(8,128)}, u32[]{:S(2)}, u32[]{:S(2)}) collective-permute-start(f32[4,2,48,384]{3,2,1,0:T(8,128)} %bitcast.30), channel_id=1, source_target_pairs={{0,4},{2,6},{4,0},{6,2},{8,12},{10,14},{12,8},{14,10},{16,20},{18,... | collective-permute-start | bytes 1769480 | tf_op jit(solution)/shard_map/ppermute | solution.py:58
  189.5 26.6 %collective-permute-start.26 = (f32[2,48,1536]{2,1,0:T(8,128)}, f32[2,48,1536]{2,1,0:T(8,128)}, u32[]{:S(2)}, u32[]{:S(2)}) collective-permute-start(f32[2,48,1536]{2,1,0:T(8,128)} %bitcast_add_fusion), channel_id=1, source_target_pairs={{0,4},{2,6},{4,0},{6,2},{8,12},{10,14},{12,8},{14,10},{16,20},{18,... | collective-permute-start | bytes 1769480 | tf_op jit(solution)/shard_map/ppermute | solution.py:58
  190.3 28.3 %copy-start.23 = (f32[11,768]{1,0:T(8,128)}, f32[11,768]{1,0:T(8,128)S(1)}, u32[]{:S(2)}) copy-start(f32[11,768]{1,0:T(8,128)S(1)} %collective-permute-done.32) | copy-start | bytes 101380
  190.3 25.8 %collective-permute-start.25 = (f32[2,48,1536]{2,1,0:T(8,128)}, f32[2,48,1536]{2,1,0:T(8,128)}, u32[]{:S(2)}, u32[]{:S(2)}) collective-permute-start(f32[2,48,1536]{2,1,0:T(8,128)} %bitcast_add_fusion.1), channel_id=1, source_target_pairs={{0,8},{2,10},{4,12},{6,14},{8,0},{10,2},{12,4},{14,6},{16,24},{18,... | collective-permute-start | bytes 1769480 | tf_op jit(solution)/shard_map/ppermute | solution.py:58
  218.6 27.8 %collective-permute-start.33 = (f32[2,48,1536]{2,1,0:T(8,128)}, f32[2,48,1536]{2,1,0:T(8,128)}, u32[]{:S(2)}, u32[]{:S(2)}) collective-permute-start(f32[2,48,1536]{2,1,0:T(8,128)} %pad_maximum_fusion.1), channel_id=1, source_target_pairs={{0,16},{2,18},{4,20},{6,22},{8,24},{10,26},{12,28},{14,30},{16,0},... | collective-permute-start | bytes 1769480 | tf_op jit(solution)/shard_map/ppermute | solution.py:58
  223.1 17.2 %collective-permute-start.35 = (f32[2,2,48,384]{3,2,1,0:T(8,128)}, f32[2,2,48,384]{3,2,1,0:T(8,128)S(1)}, u32[]{:S(2)}, u32[]{:S(2)}) collective-permute-start(f32[2,2,48,384]{3,2,1,0:T(8,128)} %bitcast_add_fusion.3), channel_id=1, source_target_pairs={{0,4},{2,6},{4,0},{6,2},{8,12},{10,14},{12,8},{14,10},{16,20},{18,... | collective-permute-start | bytes 884744 | tf_op jit(solution)/shard_map/ppermute | solution.py:58
  226.2 14.1 %collective-permute-start.34 = (f32[2,2,48,384]{3,2,1,0:T(8,128)}, f32[2,2,48,384]{3,2,1,0:T(8,128)}, u32[]{:S(2)}, u32[]{:S(2)}) collective-permute-start(f32[2,2,48,384]{3,2,1,0:T(8,128)} %bitcast_add_fusion.4), channel_id=1, source_target_pairs={{0,8},{2,10},{4,12},{6,14},{8,0},{10,2},{12,4},{14,6},{16,24},{18,... | collective-permute-start | bytes 884744 | tf_op jit(solution)/shard_map/ppermute | solution.py:58
  226.7 13.6 %collective-permute-start.36 = (f32[11,768]{1,0:T(8,128)S(1)}, f32[11,768]{1,0:T(8,128)S(1)}, u32[]{:S(2)}, u32[]{:S(2)}) collective-permute-start(f32[11,768]{1,0:T(8,128)S(1)} %add.486), channel_id=1, source_target_pairs={{0,8},{2,10},{4,12},{6,14},{8,0},{10,2},{12,4},{14,6},{16,24},{18,... | collective-permute-start | bytes 101384 | tf_op jit(solution)/shard_map/ppermute | solution.py:58
  246.4 11.8 %collective-permute-start.38 = (f32[11,768]{1,0:T(8,128)S(1)}, f32[11,768]{1,0:T(8,128)S(1)}, u32[]{:S(2)}, u32[]{:S(2)}) collective-permute-start(f32[11,768]{1,0:T(8,128)S(1)} %add.506), channel_id=1, source_target_pairs={{0,16},{2,18},{4,20},{6,22},{8,24},{10,26},{12,28},{14,30},{16,0},... | collective-permute-start | bytes 101384 | tf_op jit(solution)/shard_map/ppermute | solution.py:58
  248.8 15.9 %collective-permute-start.37 = (f32[2,2,48,384]{3,2,1,0:T(8,128)S(1)}, f32[2,2,48,384]{3,2,1,0:T(8,128)}, u32[]{:S(2)}, u32[]{:S(2)}) collective-permute-start(f32[2,2,48,384]{3,2,1,0:T(8,128)S(1)} %pad_maximum_fusion.2), channel_id=1, source_target_pairs={{0,16},{2,18},{4,20},{6,22},{8,24},{10,26},{12,28},{14,30},{16,0},... | collective-permute-start | bytes 884744 | tf_op jit(solution)/shard_map/ppermute | solution.py:58
  (21 other events, 67.9 us)
